TPU v7x, 512 devices: a whole 4x4x16 slice. The times are simulated.
512 devices in a mesh: band: 8 (over y, x_lo), dom: 64 (over x_hi, z, core).
Axes of the slice: x: 4 (x_hi: 2, x_lo: 2; x = x_hi * 2 + x_lo), y: 4, z: 16, core: 2. Of those that a mesh axis runs over, the one named last changes fastest.
Arguments:
- orbitals: bfloat16 [512, 128, 32, 128], P('band', 'dom'), may hold values from -270 to 270
- potential: float32 [128, 32, 128], P('dom'), may hold values from 0 to 4
Outputs:
- rotated: bfloat16 [512, 128, 32, 128], P('band', 'dom')
All inputs are finite; a program needn't handle non-finite values.
Results may differ from a plain program's by a relative error of at most 0.025.
Values may be sent and summed in bfloat16 or wider, within the bound.
No kernel may reach another device: no remote copies, remote signals or barrier semaphores. Data moves between devices by JAX's collectives and lax.ppermute only.
A program may use at most 64 MiB of HBM per device.

v0:
```python
from functools import partial

import jax
import jax.numpy as jnp
from jax import lax
from jax.experimental import pallas as pl
from jax.experimental.pallas import tpu as pltpu
from jax.sharding import PartitionSpec as P

HIGHEST = lax.Precision.HIGHEST

spectrum_center = 7.5
spectrum_half = 4.5


def padded_2(cells, sides, width):
    for axis, dim in sides:
        count = lax.axis_size(axis)
        ends = count - 1
        head = lax.slice_in_dim(cells, 0, width, axis=dim)
        tail = lax.slice_in_dim(cells, cells.shape[dim] - width, cells.shape[dim], axis=dim)
        cells = jnp.concatenate(
            [
                lax.ppermute(tail, axis, [(i, (i + 1) % count) for i in range(ends)]),
                cells,
                lax.ppermute(head, axis, [((i + 1) % count, i) for i in range(ends)]),
            ],
            axis=dim,
        )
    return cells


def neighbours(padded, axis_dim, offset):
    index_list = [slice(None), slice(2, -2), slice(2, -2), slice(2, -2)]
    index_list[axis_dim] = slice(2 + offset, padded.shape[axis_dim] - 2 + offset)
    return padded[tuple(index_list)]


def hamiltonian(padded, potential):
    center = neighbours(padded, 1, 0)
    laplace = -7.5 * center
    for axis_dim in (1, 2, 3):
        near_sum = neighbours(padded, axis_dim, 1) + neighbours(padded, axis_dim, -1)
        far_sum = neighbours(padded, axis_dim, 2) + neighbours(padded, axis_dim, -2)
        laplace = laplace + 4.0 / 3.0 * near_sum - 1.0 / 12.0 * far_sum
    return (-0.5 * laplace + potential * center, center)


def chebyshev(field, operate):
    image, anchor = operate(field)
    degree_one = ((image - spectrum_center * anchor) / spectrum_half).astype(jnp.bfloat16)
    image, current = operate(degree_one)
    second = (2.0 * (image - spectrum_center * current) / spectrum_half - anchor).astype(
        jnp.bfloat16
    )
    image, latest = operate(second)
    return (2.0 * (image - spectrum_center * latest) / spectrum_half - current).astype(jnp.bfloat16)


def operator_on(field, potential):
    widened = padded_2(field, (("dom", 1),), 2)
    padded = jnp.pad(widened.astype(jnp.float32), ((0, 0), (0, 0), (2, 2), (2, 2)))
    return hamiltonian(padded, potential)


def dot_nn(a, b):
    return lax.dot_general(a, b, (((1,), (0,)), ((), ())), precision=HIGHEST, preferred_element_type=jnp.float32)


def dot_nt(a, b):
    return lax.dot_general(a, b, (((1,), (1,)), ((), ())), precision=HIGHEST, preferred_element_type=jnp.float32)


def reciprocal(value):
    guess = pl.reciprocal(value, approx=True)
    return guess * (2.0 - value * guess)


def inverse_factor_of_block(rows):
    lane = lax.broadcasted_iota(jnp.int32, (8, 128), 1)
    sub = lax.broadcasted_iota(jnp.int32, (8, 128), 0)
    rows = list(rows)
    out = []
    for p in range(16):
        k0 = 8 * p
        inside = (lane >= k0) & (lane < k0 + 8)
        x = rows[p]
        columns = [jnp.broadcast_to(x[:, k0 + j : k0 + j + 1], (8, 128)) for j in range(8)]
        a = [[jnp.broadcast_to(columns[j][i : i + 1, :], (8, 128)) for j in range(i + 1)] for i in range(8)]
        x = jnp.where(inside, (lane - k0 == sub).astype(jnp.float32), x)
        z = [jnp.broadcast_to(x[i : i + 1, :], (8, 128)) for i in range(8)]
        inv, m = [], [[None] * 8 for _ in range(8)]
        for j in range(8):
            inv.append(reciprocal(a[j][j]))
            for l in range(j + 1, 8):
                m[l][j] = a[l][j] * inv[j]
            for l in range(j + 1, 8):
                for q in range(j + 1, l + 1):
                    a[l][q] = a[l][q] - m[l][j] * a[q][j]
                z[l] = z[l] - m[l][j] * z[j]
        w = z[0] * lax.rsqrt(a[0][0])
        for i in range(1, 8):
            w = jnp.where(sub == i, z[i] * lax.rsqrt(a[i][i]), w)
        out.append(jnp.where(lane < k0 + 8, w, 0.0))
        if p == 15:
            break
        y = [z[j] * inv[j] for j in range(8)]
        for l in range(7, 0, -1):
            for j in range(l):
                y[j] = y[j] - m[l][j] * y[l]
        for i in range(p + 1, 16):
            c = [jnp.broadcast_to(rows[i][:, k0 + j : k0 + j + 1], (8, 128)) for j in range(8)]
            t = [c[j] * y[j] for j in range(8)]
            t = ((t[0] + t[1]) + (t[2] + t[3])) + ((t[4] + t[5]) + (t[6] + t[7]))
            rows[i] = jnp.where(inside, 0.0, rows[i]) - t
    return out


def rotation_kernel(gram_ref, out_ref, s_ref, a_ref, w_ref):
    n, b = gram_ref.shape[0], 128
    blocks = n // b
    s_ref[...] = gram_ref[...]
    a_ref[...] = jnp.zeros_like(a_ref)
    for k in range(blocks):
        lo, hi = k * b, (k + 1) * b
        out = inverse_factor_of_block([s_ref[lo + 8 * i : lo + 8 * i + 8, lo:hi] for i in range(16)])
        for i in range(16):
            w_ref[8 * i : 8 * i + 8, :] = out[i]
        w = w_ref[...]
        out_ref[lo:hi, lo:hi] = w.astype(jnp.bfloat16)
        if hi < n:
            out_ref[lo:hi, hi:] = jnp.zeros((b, n - hi), jnp.bfloat16)
            upper = dot_nn(w, s_ref[lo:hi, hi:])
            lower = dot_nt(s_ref[hi:, lo:hi], w)
            s_ref[hi:, hi:] -= dot_nn(lower, upper)
        if k > 0:
            v = dot_nn(w, a_ref[lo:hi, :lo])
            out_ref[lo:hi, :lo] = v.astype(jnp.bfloat16)
            if hi < n:
                a_ref[hi:, :lo] -= dot_nn(lower, v)
        if hi < n:
            a_ref[hi:, lo:hi] = -dot_nn(lower, w)


def rotation_from(gram):
    n = gram.shape[0]
    return pl.pallas_call(
        rotation_kernel,
        out_shape=jax.ShapeDtypeStruct((n, n), jnp.bfloat16),
        in_specs=[pl.BlockSpec(memory_space=pltpu.VMEM)],
        out_specs=pl.BlockSpec(memory_space=pltpu.VMEM),
        scratch_shapes=[
            pltpu.VMEM((n, n), jnp.float32),
            pltpu.VMEM((n, n), jnp.float32),
            pltpu.VMEM((128, 128), jnp.float32),
        ],
        compiler_params=pltpu.CompilerParams(vmem_limit_bytes=32 * 1024 * 1024),
    )(gram)


def exchange(pieces, axis):
    return lax.all_to_all(pieces, axis, 0, 0, tiled=True)


def summed_everywhere(terms):
    bands, doms = lax.axis_size("band"), lax.axis_size("dom")
    count = terms.shape[0]
    rows = jnp.sum(exchange(terms.reshape(bands, count // bands, count), "band"), axis=0)
    one = rows.reshape(doms, count // (bands * doms), count)
    one = jnp.sum(exchange(one, "dom"), axis=0, keepdims=True)
    rows = exchange(jnp.broadcast_to(one, (doms,) + one.shape[1:]), "dom")
    rows = rows.reshape(1, count // bands, count)
    return exchange(jnp.broadcast_to(rows, (bands,) + rows.shape[1:]), "band").reshape(count, count)


def local(orbitals, potential):
    orb_count = orbitals.shape[0]
    bands = lax.axis_size("band")
    cells_dev = orbitals.shape[1] * orbitals.shape[2] * orbitals.shape[3]
    total_cells = cells_dev * lax.axis_size("dom")
    filtered = chebyshev(orbitals, partial(operator_on, potential=potential))
    flat = filtered.reshape(orb_count, cells_dev)
    everyone = lax.all_to_all(flat, "band", 1, 0, tiled=True)
    contract = (((1,), (1,)), ((), ()))
    terms = lax.dot_general(everyone, everyone, contract, preferred_element_type=jnp.float32)
    gram = summed_everywhere(terms) / total_cells
    rotation = rotation_from(gram)
    turned = jnp.dot(rotation, everyone, preferred_element_type=jnp.float32).astype(jnp.bfloat16)
    result = lax.all_to_all(turned, "band", 0, 1, tiled=True)
    return result.reshape(orbitals.shape)


def solution(mesh):
    placed = (P("band", "dom", None, None), P("dom", None, None))
    return jax.shard_map(
        local, mesh=mesh, in_specs=placed, out_specs=P("band", "dom", None, None), check_vma=False
    )
```

profile of v0, /device:TPU:1, one launch (start us, length us, event | category | flops | bytes accessed | tf_op | source)
XLA Modules:
  0.0 234.0 jit_solution(16941664385326633070)
XLA Ops:
  0.0 0.0 copy-start
  0.0 5.1 %collective-permute-start = (bf16[64,2,32,128]{3,2,1,0:T(8,128)(2,1)}, bf16[64,2,32,128]{3,2,1,0:T(8,128)(2,1)S(1)}, u32[]{:S(2)}, u32[]{:S(2)}) collective-permute-start(bf16[64,2,32,128]{3,2,1,0:T(8,128)(2,1)} %param.2), channel_id=1, source_target_pairs={{0,1},{1,2},{2,3},{3,4},{4,5},{5,6},{6,7},{7,8},{8,9},{9,10},{10,1... | collective-permute-start | bytes 3145736 | tf_op jit(solution)/shard_map/ppermute | solution.py:24
  5.1 5.2 %collective-permute-start.1 = (bf16[64,2,32,128]{3,2,1,0:T(8,128)(2,1)}, bf16[64,2,32,128]{3,2,1,0:T(8,128)(2,1)S(1)}, u32[]{:S(2)}, u32[]{:S(2)}) collective-permute-start(bf16[64,2,32,128]{3,2,1,0:T(8,128)(2,1)} %param.2), channel_id=1, source_target_pairs={{1,0},{2,1},{3,2},{4,3},{5,4},{6,5},{7,6},{8,7},{9,8},{10,9},{11,1... | collective-permute-start | bytes 3145736 | tf_op jit(solution)/shard_map/ppermute | solution.py:26
  10.3 6.8 %collective-permute-done = bf16[64,2,32,128]{3,2,1,0:T(8,128)(2,1)S(1)} collective-permute-done((bf16[64,2,32,128]{3,2,1,0:T(8,128)(2,1)}, bf16[64,2,32,128]{3,2,1,0:T(8,128)(2,1)S(1)}, u32[]{:S(2)}, u32[]{:S(2)}) %collective-permute-start) | collective-permute-done | bytes 1048608 | tf_op jit(solution)/shard_map/ppermute | solution.py:24
  17.1 4.3 %collective-permute-done.1 = bf16[64,2,32,128]{3,2,1,0:T(8,128)(2,1)S(1)} collective-permute-done((bf16[64,2,32,128]{3,2,1,0:T(8,128)(2,1)}, bf16[64,2,32,128]{3,2,1,0:T(8,128)(2,1)S(1)}, u32[]{:S(2)}, u32[]{:S(2)}) %collective-permute-start.1) | collective-permute-done | bytes 1048608 | tf_op jit(solution)/shard_map/ppermute | solution.py:26
  21.4 1.7 maximum_convert_fusion
  23.1 0.0 copy-done
  23.1 3.0 %multiply_convert_fusion = bf16[64,2,32,128]{3,2,1,0:T(8,128)(2,1)S(1)} fusion(f32[64,6,32,128]{3,2,1,0:T(8,128)S(1)} %maximum_convert_fusion, f32[2,32,128]{2,1,0:T(8,128)S(1)} %copy-done), kind=kLoop, calls=%fused_computation.92 | loop fusion | flops 13631488 | bytes 17858560 | tf_op jit(solution)/shard_map/convert_element_type | solution.py:51
  26.1 1.9 collective-permute-start.3
  28.0 3.6 %collective-permute-start.2 = (bf16[64,2,32,128]{3,2,1,0:T(8,128)(2,1)S(1)}, bf16[64,2,32,128]{3,2,1,0:T(8,128)(2,1)S(1)}, u32[]{:S(2)}, u32[]{:S(2)}) collective-permute-start(bf16[64,2,32,128]{3,2,1,0:T(8,128)(2,1)S(1)} %multiply_convert_fusion), channel_id=1, source_target_pairs={{0,1},{1,2},{2,3},{3,4},{4,5},{5,6},{6,7},{7,8},{8,9},{9,10},{10,1... | collective-permute-start | bytes 3145736 | tf_op jit(solution)/shard_map/ppermute | solution.py:24
  31.7 10.5 %collective-permute-done.3 = bf16[64,2,32,128]{3,2,1,0:T(8,128)(2,1)S(1)} collective-permute-done((bf16[64,2,32,128]{3,2,1,0:T(8,128)(2,1)S(1)}, bf16[64,2,32,128]{3,2,1,0:T(8,128)(2,1)S(1)}, u32[]{:S(2)}, u32[]{:S(2)}) %collective-permute-start.3) | collective-permute-done | bytes 1048608 | tf_op jit(solution)/shard_map/ppermute | solution.py:26
  42.2 1.2 collective-permute-done.2
  43.4 0.5 maximum_convert_fusion.1
  43.9 3.3 %subtract_convert_fusion.1 = bf16[64,2,32,128]{3,2,1,0:T(8,128)(2,1)S(1)} fusion(f32[64,6,32,128]{3,2,1,0:T(8,128)S(1)} %maximum_convert_fusion.1, f32[64,6,32,128]{3,2,1,0:T(8,128)S(1)} %maximum_convert_fusion, f32[2,32,128]{2,1,0:T(8,128)S(1)} %copy-done), kind=kLoop, calls=%fused_computation.91 | loop fusion | flops 14155776 | bytes 19955712 | tf_op jit(solution)/shard_map/convert_element_type | solution.py:53
  47.2 1.9 collective-permute-start.5
  49.1 4.4 %collective-permute-start.4 = (bf16[64,2,32,128]{3,2,1,0:T(8,128)(2,1)S(1)}, bf16[64,2,32,128]{3,2,1,0:T(8,128)(2,1)S(1)}, u32[]{:S(2)}, u32[]{:S(2)}) collective-permute-start(bf16[64,2,32,128]{3,2,1,0:T(8,128)(2,1)S(1)} %subtract_convert_fusion.1), channel_id=1, source_target_pairs={{0,1},{1,2},{2,3},{3,4},{4,5},{5,6},{6,7},{7,8},{8,9},{9,10},{10,1... | collective-permute-start | bytes 3145736 | tf_op jit(solution)/shard_map/ppermute | solution.py:24
  53.5 10.5 %collective-permute-done.5 = bf16[64,2,32,128]{3,2,1,0:T(8,128)(2,1)S(1)} collective-permute-done((bf16[64,2,32,128]{3,2,1,0:T(8,128)(2,1)S(1)}, bf16[64,2,32,128]{3,2,1,0:T(8,128)(2,1)S(1)}, u32[]{:S(2)}, u32[]{:S(2)}) %collective-permute-start.5) | collective-permute-done | bytes 1048608 | tf_op jit(solution)/shard_map/ppermute | solution.py:26
  64.0 1.2 collective-permute-done.4
  65.2 0.4 maximum_convert_fusion.2
  65.6 3.3 %subtract_convert_fusion = bf16[64,2,32,128]{3,2,1,0:T(8,128)(2,1)S(1)} fusion(f32[64,6,32,128]{3,2,1,0:T(8,128)S(1)} %maximum_convert_fusion.2, f32[64,6,32,128]{3,2,1,0:T(8,128)S(1)} %maximum_convert_fusion.1, f32[2,32,128]{2,1,0:T(8,128)S(1)} %copy-done), kind=kLoop, calls=%fused_computation.90 | loop fusion | flops 14155776 | bytes 19955712 | tf_op jit(solution)/shard_map/convert_element_type | solution.py:57
  68.9 0.5 all_to_all.38
  69.4 0.6 copy.6
  70.0 28.3 %all_to_all.55 = bf16[64,8,1024]{2,0,1:T(8,128)(2,1)S(1)} all-to-all(bf16[64,8,1024]{2,0,1:T(8,128)(2,1)S(1)} %copy.6), channel_id=1, replica_groups=mesh['band'=8,'dom'=64] {'band'}, dimensions={1} | all-to-all | bytes 2097152 | tf_op jit(solution)/shard_map/all_to_all | solution.py:183
  98.3 0.7 fusion.57
  99.1 12.8 %all_to_all.56 = f32[8,64,512]{2,1,0:T(8,128)S(1)} all-to-all(f32[8,64,512]{2,1,0:T(8,128)S(1)} %fusion.57), channel_id=1, replica_groups=mesh['band'=8,'dom'=64] {'band'}, dimensions={0} | all-to-all | bytes 2097152 | tf_op jit(solution)/shard_map/all_to_all | solution.py:162
  111.8 0.1 reduce_sum.18
  111.9 0.1 reshape.29
  112.0 35.5 %all_to_all.57 = f32[64,1,512]{2,1,0:T(1,128)S(1)} all-to-all(f32[64,1,512]{2,1,0:T(1,128)S(1)} %reshape.29), channel_id=1, replica_groups=mesh['band'=8,'dom'=64] {'dom'}, dimensions={0} | all-to-all | bytes 262144 | tf_op jit(solution)/shard_map/all_to_all | solution.py:162
  147.5 0.1 reduce_sum.19
  147.6 0.1 broadcast_in_dim.6
  147.7 22.4 %all_to_all.58 = f32[64,1,512]{2,1,0:T(1,128)S(1)} all-to-all(f32[64,1,512]{2,1,0:T(1,128)S(1)} %broadcast_in_dim.6), channel_id=1, replica_groups=mesh['band'=8,'dom'=64] {'dom'}, dimensions={0} | all-to-all | bytes 262144 | tf_op jit(solution)/shard_map/all_to_all | solution.py:162
  170.1 0.1 broadcast_in_dim.8
  170.2 17.9 %all_to_all.59 = f32[8,64,512]{2,1,0:T(8,128)S(1)} all-to-all(f32[8,64,512]{2,1,0:T(8,128)S(1)} %broadcast_in_dim.8), channel_id=1, replica_groups=mesh['band'=8,'dom'=64] {'band'}, dimensions={0} | all-to-all | bytes 2097152 | tf_op jit(solution)/shard_map/all_to_all | solution.py:162
  188.1 0.1 broadcast_multiply_fusion
  188.2 26.4 %shard_map.28 = bf16[512,512]{1,0:T(8,128)(2,1)S(1)} custom-call(f32[512,512]{1,0:T(8,128)S(1)} %bitcast.18), custom_call_target="tpu_custom_call" | custom-call | tf_op jit(solution)/shard_map/pallas_call | solution.py:147
  214.6 0.7 convolution_convert_fusion
  215.3 16.8 %all_to_all.60 = bf16[8,64,1024]{2,1,0:T(8,128)(2,1)S(1)} all-to-all(bf16[8,64,1024]{2,1,0:T(8,128)(2,1)S(1)} %bitcast.22), channel_id=1, replica_groups=mesh['band'=8,'dom'=64] {'band'}, dimensions={0} | all-to-all | bytes 2097152 | tf_op jit(solution)/shard_map/all_to_all | solution.py:189
  232.1 0.6 copy.7
  232.7 1.3 reshape.30
  (1 shorter events, 0.0 us)
Async XLA Ops:
  0.0 23.1 %copy-start = (f32[2,32,128]{2,1,0:T(8,128)S(1)}, f32[2,32,128]{2,1,0:T(8,128)}, u32[]{:S(2)}) copy-start(f32[2,32,128]{2,1,0:T(8,128)} %param.3) | copy-start | bytes 98308
  0.0 17.1 %collective-permute-start = (bf16[64,2,32,128]{3,2,1,0:T(8,128)(2,1)}, bf16[64,2,32,128]{3,2,1,0:T(8,128)(2,1)S(1)}, u32[]{:S(2)}, u32[]{:S(2)}) collective-permute-start(bf16[64,2,32,128]{3,2,1,0:T(8,128)(2,1)} %param.2), channel_id=1, source_target_pairs={{0,1},{1,2},{2,3},{3,4},{4,5},{5,6},{6,7},{7,8},{8,9},{9,10},{10,1... | collective-permute-start | bytes 3145736 | tf_op jit(solution)/shard_map/ppermute | solution.py:24
  5.1 16.3 %collective-permute-start.1 = (bf16[64,2,32,128]{3,2,1,0:T(8,128)(2,1)}, bf16[64,2,32,128]{3,2,1,0:T(8,128)(2,1)S(1)}, u32[]{:S(2)}, u32[]{:S(2)}) collective-permute-start(bf16[64,2,32,128]{3,2,1,0:T(8,128)(2,1)} %param.2), channel_id=1, source_target_pairs={{1,0},{2,1},{3,2},{4,3},{5,4},{6,5},{7,6},{8,7},{9,8},{10,9},{11,1... | collective-permute-start | bytes 3145736 | tf_op jit(solution)/shard_map/ppermute | solution.py:26
  26.1 16.1 %collective-permute-start.3 = (bf16[64,2,32,128]{3,2,1,0:T(8,128)(2,1)S(1)}, bf16[64,2,32,128]{3,2,1,0:T(8,128)(2,1)S(1)}, u32[]{:S(2)}, u32[]{:S(2)}) collective-permute-start(bf16[64,2,32,128]{3,2,1,0:T(8,128)(2,1)S(1)} %multiply_convert_fusion), channel_id=1, source_target_pairs={{1,0},{2,1},{3,2},{4,3},{5,4},{6,5},{7,6},{8,7},{9,8},{10,9},{11,1... | collective-permute-start | bytes 3145736 | tf_op jit(solution)/shard_map/ppermute | solution.py:26
  28.0 15.4 %collective-permute-start.2 = (bf16[64,2,32,128]{3,2,1,0:T(8,128)(2,1)S(1)}, bf16[64,2,32,128]{3,2,1,0:T(8,128)(2,1)S(1)}, u32[]{:S(2)}, u32[]{:S(2)}) collective-permute-start(bf16[64,2,32,128]{3,2,1,0:T(8,128)(2,1)S(1)} %multiply_convert_fusion), channel_id=1, source_target_pairs={{0,1},{1,2},{2,3},{3,4},{4,5},{5,6},{6,7},{7,8},{8,9},{9,10},{10,1... | collective-permute-start | bytes 3145736 | tf_op jit(solution)/shard_map/ppermute | solution.py:24
  47.2 16.9 %collective-permute-start.5 = (bf16[64,2,32,128]{3,2,1,0:T(8,128)(2,1)S(1)}, bf16[64,2,32,128]{3,2,1,0:T(8,128)(2,1)S(1)}, u32[]{:S(2)}, u32[]{:S(2)}) collective-permute-start(bf16[64,2,32,128]{3,2,1,0:T(8,128)(2,1)S(1)} %subtract_convert_fusion.1), channel_id=1, source_target_pairs={{1,0},{2,1},{3,2},{4,3},{5,4},{6,5},{7,6},{8,7},{9,8},{10,9},{11,1... | collective-permute-start | bytes 3145736 | tf_op jit(solution)/shard_map/ppermute | solution.py:26
  49.1 16.1 %collective-permute-start.4 = (bf16[64,2,32,128]{3,2,1,0:T(8,128)(2,1)S(1)}, bf16[64,2,32,128]{3,2,1,0:T(8,128)(2,1)S(1)}, u32[]{:S(2)}, u32[]{:S(2)}) collective-permute-start(bf16[64,2,32,128]{3,2,1,0:T(8,128)(2,1)S(1)} %subtract_convert_fusion.1), channel_id=1, source_target_pairs={{0,1},{1,2},{2,3},{3,4},{4,5},{5,6},{6,7},{7,8},{8,9},{9,10},{10,1... | collective-permute-start | bytes 3145736 | tf_op jit(solution)/shard_map/ppermute | solution.py:24
where the time goes:
time: 235 us; the launch traced here: 234 us
  blocking collectives  134 us (57%)
  waiting for transfers between devices  34.6 us (15%)
  Pallas kernels  26.4 us (11%)
  starting transfers between devices  22.1 us (9%)
  other arithmetic  12.5 us (5%)
  local copies, waits for them, and re-layouts  3.22 us (1%)
    all_to_all x4, blocking collectives, exchange(): return lax.all_to_all(pieces, axis, 0, 0, tiled=True)  88.5 us
    all_to_all x1, blocking collectives, local(): everyone = lax.all_to_all(flat, 'band', 1, 0, tiled=True)  28.3 us
    pallas_call x1, Pallas kernels, rotation_from(): pl.pallas_call(rotation_kernel, out_shape=jax.ShapeDtypeStruct((n, n), jn...  26.4 us
    ppermute x3, waiting for transfers between devices, padded_2(): lax.ppermute(head, axis, [((i + 1) % count, i) for i in range(ends)])  25.4 us
    all_to_all x1, blocking collectives, local(): result = lax.all_to_all(turned, 'band', 0, 1, tiled=True)  16.8 us
    ppermute x3, starting transfers between devices, padded_2(): lax.ppermute(tail, axis, [(i, (i + 1) % count) for i in range(ends)])  13.1 us
    ppermute x3, waiting for transfers between devices, padded_2(): lax.ppermute(tail, axis, [(i, (i + 1) % count) for i in range(ends)])  9.19 us
    ppermute x3, starting transfers between devices, padded_2(): lax.ppermute(head, axis, [((i + 1) % count, i) for i in range(ends)])  9.05 us
  transfers between devices with their start and end apart: 6, of which 6 were waited for; matrix products, arithmetic and copies ran while one was open for 0% of the time, Pallas kernels for 0%

commit v1 on v0

--- a/solution.py
+++ b/solution.py
@@ -5,7 +5,11 @@
 from jax import lax
 from jax.experimental import pallas as pl
 from jax.experimental.pallas import tpu as pltpu
+from jax.sharding import Mesh
 from jax.sharding import PartitionSpec as P
+
+BAND, DOM = ("y", "x_lo"), ("x_hi", "z", "core")
+NEAR, FAR = ("y", "x_lo", "core"), ("x_hi", "z")
 
 HIGHEST = lax.Precision.HIGHEST
 
@@ -58,7 +62,7 @@
 
 
 def operator_on(field, potential):
-    widened = padded_2(field, (("dom", 1),), 2)
+    widened = padded_2(field, ((DOM, 1),), 2)
     padded = jnp.pad(widened.astype(jnp.float32), ((0, 0), (0, 0), (2, 2), (2, 2)))
     return hamiltonian(padded, potential)
 
@@ -116,82 +120,109 @@
     return out
 
 
-def rotation_kernel(gram_ref, out_ref, s_ref, a_ref, w_ref):
-    n, b = gram_ref.shape[0], 128
-    blocks = n // b
-    s_ref[...] = gram_ref[...]
-    a_ref[...] = jnp.zeros_like(a_ref)
-    for k in range(blocks):
+def gram_kernel(field_ref, tiles_ref):
+    tile = 0
+    for i in range(field_ref.shape[0] // 128):
+        rows = slice(128 * i, 128 * i + 128)
+        terms = lax.dot_general(
+            field_ref[rows, :],
+            field_ref[: 128 * i + 128, :],
+            (((1,), (1,)), ((), ())),
+            preferred_element_type=jnp.float32,
+        )
+        for j in range(i + 1):
+            tiles_ref[128 * tile : 128 * tile + 128, :] = terms[:, 128 * j : 128 * j + 128]
+            tile += 1
+
+
+def gram_tiles(field):
+    count = field.shape[0] // 128
+    return pl.pallas_call(
+        gram_kernel,
+        out_shape=jax.ShapeDtypeStruct((64 * count * (count + 1), 128), jnp.float32),
+        in_specs=[pl.BlockSpec(memory_space=pltpu.VMEM)],
+        out_specs=pl.BlockSpec(memory_space=pltpu.VMEM),
+        compiler_params=pltpu.CompilerParams(vmem_limit_bytes=32 * 1024 * 1024),
+    )(field)
+
+
+def rotation_kernel(tiles_ref, field_ref, out_ref, s_ref, a_ref, w_ref, r_ref):
+    n, b = field_ref.shape[0], 128
+    tile = 0
+    for i in range(n // b):
+        for j in range(i + 1):
+            s_ref[b * i : b * i + b, b * j : b * j + b] = tiles_ref[b * tile : b * tile + b, :]
+            tile += 1
+    for k in range(n // b):
         lo, hi = k * b, (k + 1) * b
         out = inverse_factor_of_block([s_ref[lo + 8 * i : lo + 8 * i + 8, lo:hi] for i in range(16)])
         for i in range(16):
             w_ref[8 * i : 8 * i + 8, :] = out[i]
         w = w_ref[...]
-        out_ref[lo:hi, lo:hi] = w.astype(jnp.bfloat16)
+        r_ref[lo:hi, lo:hi] = w.astype(jnp.bfloat16)
         if hi < n:
-            out_ref[lo:hi, hi:] = jnp.zeros((b, n - hi), jnp.bfloat16)
-            upper = dot_nn(w, s_ref[lo:hi, hi:])
             lower = dot_nt(s_ref[hi:, lo:hi], w)
-            s_ref[hi:, hi:] -= dot_nn(lower, upper)
+            s_ref[hi:, hi:] -= dot_nt(lower, lower)
         if k > 0:
             v = dot_nn(w, a_ref[lo:hi, :lo])
-            out_ref[lo:hi, :lo] = v.astype(jnp.bfloat16)
+            r_ref[lo:hi, :lo] = v.astype(jnp.bfloat16)
             if hi < n:
                 a_ref[hi:, :lo] -= dot_nn(lower, v)
         if hi < n:
             a_ref[hi:, lo:hi] = -dot_nn(lower, w)
-
-
-def rotation_from(gram):
-    n = gram.shape[0]
+        turned = jnp.dot(r_ref[lo:hi, :hi], field_ref[:hi, :], preferred_element_type=jnp.float32)
+        out_ref[lo:hi, :] = turned.astype(jnp.bfloat16)
+
+
+def rotated_by(tiles, field):
+    n = field.shape[0]
     return pl.pallas_call(
         rotation_kernel,
-        out_shape=jax.ShapeDtypeStruct((n, n), jnp.bfloat16),
-        in_specs=[pl.BlockSpec(memory_space=pltpu.VMEM)],
+        out_shape=jax.ShapeDtypeStruct(field.shape, jnp.bfloat16),
+        in_specs=[pl.BlockSpec(memory_space=pltpu.VMEM)] * 2,
         out_specs=pl.BlockSpec(memory_space=pltpu.VMEM),
         scratch_shapes=[
             pltpu.VMEM((n, n), jnp.float32),
             pltpu.VMEM((n, n), jnp.float32),
             pltpu.VMEM((128, 128), jnp.float32),
+            pltpu.VMEM((n, n), jnp.bfloat16),
         ],
         compiler_params=pltpu.CompilerParams(vmem_limit_bytes=32 * 1024 * 1024),
-    )(gram)
+    )(tiles, field)
 
 
 def exchange(pieces, axis):
     return lax.all_to_all(pieces, axis, 0, 0, tiled=True)
 
 
-def summed_everywhere(terms):
-    bands, doms = lax.axis_size("band"), lax.axis_size("dom")
-    count = terms.shape[0]
-    rows = jnp.sum(exchange(terms.reshape(bands, count // bands, count), "band"), axis=0)
-    one = rows.reshape(doms, count // (bands * doms), count)
-    one = jnp.sum(exchange(one, "dom"), axis=0, keepdims=True)
-    rows = exchange(jnp.broadcast_to(one, (doms,) + one.shape[1:]), "dom")
-    rows = rows.reshape(1, count // bands, count)
-    return exchange(jnp.broadcast_to(rows, (bands,) + rows.shape[1:]), "band").reshape(count, count)
+def summed_everywhere(terms, scale):
+    first, second = lax.axis_size(NEAR), lax.axis_size(FAR)
+    rows = terms.shape[0] // first
+    share = -(-rows // second)
+    part = jnp.sum(exchange(terms.reshape(first, rows, 128), NEAR), axis=0)
+    part = jnp.pad(part, ((0, share * second - rows), (0, 0))).reshape(second, share, 128)
+    own = jnp.sum(exchange(part, FAR), axis=0, keepdims=True) * scale
+    part = exchange(jnp.broadcast_to(own, (second, share, 128)), FAR)
+    part = part.reshape(share * second, 128)[:rows]
+    return exchange(jnp.broadcast_to(part[None], (first, rows, 128)), NEAR).reshape(terms.shape)
 
 
 def local(orbitals, potential):
     orb_count = orbitals.shape[0]
-    bands = lax.axis_size("band")
     cells_dev = orbitals.shape[1] * orbitals.shape[2] * orbitals.shape[3]
-    total_cells = cells_dev * lax.axis_size("dom")
+    total_cells = cells_dev * lax.axis_size(DOM)
     filtered = chebyshev(orbitals, partial(operator_on, potential=potential))
     flat = filtered.reshape(orb_count, cells_dev)
-    everyone = lax.all_to_all(flat, "band", 1, 0, tiled=True)
-    contract = (((1,), (1,)), ((), ()))
-    terms = lax.dot_general(everyone, everyone, contract, preferred_element_type=jnp.float32)
-    gram = summed_everywhere(terms) / total_cells
-    rotation = rotation_from(gram)
-    turned = jnp.dot(rotation, everyone, preferred_element_type=jnp.float32).astype(jnp.bfloat16)
-    result = lax.all_to_all(turned, "band", 0, 1, tiled=True)
+    everyone = lax.all_to_all(flat, BAND, 1, 0, tiled=True)
+    tiles = summed_everywhere(gram_tiles(everyone), 1.0 / total_cells)
+    turned = rotated_by(tiles, everyone)
+    result = lax.all_to_all(turned, BAND, 0, 1, tiled=True)
     return result.reshape(orbitals.shape)
 
 
 def solution(mesh):
-    placed = (P("band", "dom", None, None), P("dom", None, None))
+    named = Mesh(mesh.devices.reshape(4, 2, 2, 16, 2), ("y", "x_lo", "x_hi", "z", "core"))
+    placed = (P(BAND, DOM, None, None), P(DOM, None, None))
     return jax.shard_map(
-        local, mesh=mesh, in_specs=placed, out_specs=P("band", "dom", None, None), check_vma=False
+        local, mesh=named, in_specs=placed, out_specs=P(BAND, DOM, None, None), check_vma=False
     )

time: 235 us -> 222 us (0.945)
  blocking collectives: 134 us -> 122 us
    all_to_all x4, blocking collectives: 88.5 us -> 82.3 us  [exchange(): return lax.all_to_all(pieces, axis, 0, 0, tiled=True)]
    all_to_all x2, blocking collectives: 45.1 us -> 39.8 us  [the longest x1 22.5 us: local(): everyone = lax.all_to_all(flat, BAND, 1, 0, tiled=True)]
    pallas_call x1 -> x2, Pallas kernels: 26.4 us -> 27.4 us  [the longest x1 26.5 us: rotated_by(): pl.pallas_call(rotation_kernel, out_shape=jax.ShapeDtypeStruct(field.shap...]
where the time goes in v1:
time: 222 us
  blocking collectives  122 us (55%)
  waiting for transfers between devices  34.6 us (16%)
  Pallas kernels  27.4 us (12%)
  starting transfers between devices  22.1 us (10%)
  other arithmetic  12.2 us (5%)
  local copies, waits for them, and re-layouts  3.05 us (1%)
    all_to_all x4, blocking collectives, exchange(): return lax.all_to_all(pieces, axis, 0, 0, tiled=True)  82.3 us
    pallas_call x1, Pallas kernels, rotated_by(): pl.pallas_call(rotation_kernel, out_shape=jax.ShapeDtypeStruct(field.shap...  26.5 us
    ppermute x3, waiting for transfers between devices, padded_2(): lax.ppermute(head, axis, [((i + 1) % count, i) for i in range(ends)])  25.4 us
    all_to_all x1, blocking collectives, local(): everyone = lax.all_to_all(flat, BAND, 1, 0, tiled=True)  22.5 us
    all_to_all x1, blocking collectives, local(): result = lax.all_to_all(turned, BAND, 0, 1, tiled=True)  17.3 us
    ppermute x3, starting transfers between devices, padded_2(): lax.ppermute(tail, axis, [(i, (i + 1) % count) for i in range(ends)])  13.1 us
    ppermute x3, waiting for transfers between devices, padded_2(): lax.ppermute(tail, axis, [(i, (i + 1) % count) for i in range(ends)])  9.19 us
    ppermute x3, starting transfers between devices, padded_2(): lax.ppermute(head, axis, [((i + 1) % count, i) for i in range(ends)])  9.05 us
  transfers between devices with their start and end apart: 6, of which 6 were waited for; matrix products, arithmetic and copies ran while one was open for 0% of the time, Pallas kernels for 0%

profile of v1, /device:TPU:1, one launch (start us, length us, event | category | flops | bytes accessed | tf_op | source)
XLA Modules:
  0.0 221.7 jit_solution(10956446000262093375)
XLA Ops:
  0.0 0.0 copy-start
  0.0 5.1 %collective-permute-start = (bf16[64,2,32,128]{3,2,1,0:T(8,128)(2,1)}, bf16[64,2,32,128]{3,2,1,0:T(8,128)(2,1)S(1)}, u32[]{:S(2)}, u32[]{:S(2)}) collective-permute-start(bf16[64,2,32,128]{3,2,1,0:T(8,128)(2,1)} %param.2), channel_id=1, source_target_pairs={{0,1},{1,2},{2,3},{3,4},{4,5},{5,6},{6,7},{7,8},{8,9},{9,10},{10,1... | collective-permute-start | bytes 3145736 | tf_op jit(solution)/shard_map/ppermute | solution.py:28
  5.1 5.2 %collective-permute-start.1 = (bf16[64,2,32,128]{3,2,1,0:T(8,128)(2,1)}, bf16[64,2,32,128]{3,2,1,0:T(8,128)(2,1)S(1)}, u32[]{:S(2)}, u32[]{:S(2)}) collective-permute-start(bf16[64,2,32,128]{3,2,1,0:T(8,128)(2,1)} %param.2), channel_id=1, source_target_pairs={{1,0},{2,1},{3,2},{4,3},{5,4},{6,5},{7,6},{8,7},{9,8},{10,9},{11,1... | collective-permute-start | bytes 3145736 | tf_op jit(solution)/shard_map/ppermute | solution.py:30
  10.3 6.8 %collective-permute-done = bf16[64,2,32,128]{3,2,1,0:T(8,128)(2,1)S(1)} collective-permute-done((bf16[64,2,32,128]{3,2,1,0:T(8,128)(2,1)}, bf16[64,2,32,128]{3,2,1,0:T(8,128)(2,1)S(1)}, u32[]{:S(2)}, u32[]{:S(2)}) %collective-permute-start) | collective-permute-done | bytes 1048608 | tf_op jit(solution)/shard_map/ppermute | solution.py:28
  17.1 4.3 %collective-permute-done.1 = bf16[64,2,32,128]{3,2,1,0:T(8,128)(2,1)S(1)} collective-permute-done((bf16[64,2,32,128]{3,2,1,0:T(8,128)(2,1)}, bf16[64,2,32,128]{3,2,1,0:T(8,128)(2,1)S(1)}, u32[]{:S(2)}, u32[]{:S(2)}) %collective-permute-start.1) | collective-permute-done | bytes 1048608 | tf_op jit(solution)/shard_map/ppermute | solution.py:30
  21.4 1.7 maximum_convert_fusion
  23.1 0.0 copy-done
  23.1 3.0 %multiply_convert_fusion = bf16[64,2,32,128]{3,2,1,0:T(8,128)(2,1)S(1)} fusion(f32[64,6,32,128]{3,2,1,0:T(8,128)S(1)} %maximum_convert_fusion, f32[2,32,128]{2,1,0:T(8,128)S(1)} %copy-done), kind=kLoop, calls=%fused_computation.92 | loop fusion | flops 13631488 | bytes 17858560 | tf_op jit(solution)/shard_map/convert_element_type | solution.py:55
  26.1 1.9 collective-permute-start.3
  28.0 3.6 %collective-permute-start.2 = (bf16[64,2,32,128]{3,2,1,0:T(8,128)(2,1)S(1)}, bf16[64,2,32,128]{3,2,1,0:T(8,128)(2,1)S(1)}, u32[]{:S(2)}, u32[]{:S(2)}) collective-permute-start(bf16[64,2,32,128]{3,2,1,0:T(8,128)(2,1)S(1)} %multiply_convert_fusion), channel_id=1, source_target_pairs={{0,1},{1,2},{2,3},{3,4},{4,5},{5,6},{6,7},{7,8},{8,9},{9,10},{10,1... | collective-permute-start | bytes 3145736 | tf_op jit(solution)/shard_map/ppermute | solution.py:28
  31.7 10.5 %collective-permute-done.3 = bf16[64,2,32,128]{3,2,1,0:T(8,128)(2,1)S(1)} collective-permute-done((bf16[64,2,32,128]{3,2,1,0:T(8,128)(2,1)S(1)}, bf16[64,2,32,128]{3,2,1,0:T(8,128)(2,1)S(1)}, u32[]{:S(2)}, u32[]{:S(2)}) %collective-permute-start.3) | collective-permute-done | bytes 1048608 | tf_op jit(solution)/shard_map/ppermute | solution.py:30
  42.2 1.2 collective-permute-done.2
  43.4 0.5 maximum_convert_fusion.1
  43.9 3.3 %subtract_convert_fusion.1 = bf16[64,2,32,128]{3,2,1,0:T(8,128)(2,1)S(1)} fusion(f32[64,6,32,128]{3,2,1,0:T(8,128)S(1)} %maximum_convert_fusion.1, f32[64,6,32,128]{3,2,1,0:T(8,128)S(1)} %maximum_convert_fusion, f32[2,32,128]{2,1,0:T(8,128)S(1)} %copy-done), kind=kLoop, calls=%fused_computation.91 | loop fusion | flops 14155776 | bytes 19955712 | tf_op jit(solution)/shard_map/convert_element_type | solution.py:57
  47.2 1.9 collective-permute-start.5
  49.1 4.4 %collective-permute-start.4 = (bf16[64,2,32,128]{3,2,1,0:T(8,128)(2,1)S(1)}, bf16[64,2,32,128]{3,2,1,0:T(8,128)(2,1)S(1)}, u32[]{:S(2)}, u32[]{:S(2)}) collective-permute-start(bf16[64,2,32,128]{3,2,1,0:T(8,128)(2,1)S(1)} %subtract_convert_fusion.1), channel_id=1, source_target_pairs={{0,1},{1,2},{2,3},{3,4},{4,5},{5,6},{6,7},{7,8},{8,9},{9,10},{10,1... | collective-permute-start | bytes 3145736 | tf_op jit(solution)/shard_map/ppermute | solution.py:28
  53.5 10.5 %collective-permute-done.5 = bf16[64,2,32,128]{3,2,1,0:T(8,128)(2,1)S(1)} collective-permute-done((bf16[64,2,32,128]{3,2,1,0:T(8,128)(2,1)S(1)}, bf16[64,2,32,128]{3,2,1,0:T(8,128)(2,1)S(1)}, u32[]{:S(2)}, u32[]{:S(2)}) %collective-permute-start.5) | collective-permute-done | bytes 1048608 | tf_op jit(solution)/shard_map/ppermute | solution.py:30
  64.0 1.2 collective-permute-done.4
  65.2 0.4 maximum_convert_fusion.2
  65.6 3.3 %subtract_convert_fusion = bf16[64,2,32,128]{3,2,1,0:T(8,128)(2,1)S(1)} fusion(f32[64,6,32,128]{3,2,1,0:T(8,128)S(1)} %maximum_convert_fusion.2, f32[64,6,32,128]{3,2,1,0:T(8,128)S(1)} %maximum_convert_fusion.1, f32[2,32,128]{2,1,0:T(8,128)S(1)} %copy-done), kind=kLoop, calls=%fused_computation.90 | loop fusion | flops 14155776 | bytes 19955712 | tf_op jit(solution)/shard_map/convert_element_type | solution.py:61
  68.9 0.5 all_to_all.38
  69.4 0.6 copy.5
  70.0 22.5 %all_to_all.55 = bf16[64,8,1024]{2,0,1:T(8,128)(2,1)S(1)} all-to-all(bf16[64,8,1024]{2,0,1:T(8,128)(2,1)S(1)} %copy.5), channel_id=1, replica_groups=mesh['y'=4,'x_lo'=2,'x_hi'=2,'z'=16,'core'=2] {'y','x_lo'}, dimensions={1} | all-to-all | bytes 2097152 | tf_op jit(solution)/shard_map/all_to_all | solution.py:216
  92.5 0.9 shard_map.28
  93.4 14.1 %all_to_all.56 = f32[16,80,128]{2,1,0:T(8,128)S(1)} all-to-all(f32[16,80,128]{2,1,0:T(8,128)S(1)} %bitcast.12), channel_id=1, replica_groups=mesh['y'=4,'x_lo'=2,'x_hi'=2,'z'=16,'core'=2] {'y','x_lo','core'}, dimensions={0} | all-to-all | bytes 1310720 | tf_op jit(solution)/shard_map/all_to_all | solution.py:195
  107.6 33.3 %all_to_all.57 = f32[32,3,128]{2,1,0:T(4,128)S(1)} all-to-all(f32[32,3,128]{2,1,0:T(4,128)S(1)} %reshape.31), channel_id=1, replica_groups=mesh['y'=4,'x_lo'=2,'x_hi'=2,'z'=16,'core'=2] {'x_hi','z'}, dimensions={0} | all-to-all | bytes 98304 | tf_op jit(solution)/shard_map/all_to_all | solution.py:195
  141.0 17.7 %all_to_all.58 = f32[32,3,128]{2,1,0:T(4,128)S(1)} all-to-all(f32[32,3,128]{2,1,0:T(4,128)S(1)} %broadcast_in_dim.4), channel_id=1, replica_groups=mesh['y'=4,'x_lo'=2,'x_hi'=2,'z'=16,'core'=2] {'x_hi','z'}, dimensions={0} | all-to-all | bytes 98304 | tf_op jit(solution)/shard_map/all_to_all | solution.py:195
  158.7 17.3 %all_to_all.59 = f32[16,80,128]{2,1,0:T(8,128)S(1)} all-to-all(f32[16,80,128]{2,1,0:T(8,128)S(1)} %broadcast_in_dim.5), channel_id=1, replica_groups=mesh['y'=4,'x_lo'=2,'x_hi'=2,'z'=16,'core'=2] {'y','x_lo','core'}, dimensions={0} | all-to-all | bytes 1310720 | tf_op jit(solution)/shard_map/all_to_all | solution.py:195
  176.0 26.5 %shard_map.29 = bf16[512,1024]{1,0:T(8,128)(2,1)S(1)} custom-call(f32[1280,128]{1,0:T(8,128)S(1)} %bitcast.13, bf16[512,1024]{1,0:T(8,128)(2,1)S(1)} %bitcast.10), custom_call_target="tpu_custom_call" | custom-call | tf_op jit(solution)/shard_map/pallas_call | solution.py:179
  202.5 17.3 %all_to_all.60 = bf16[8,64,1024]{2,1,0:T(8,128)(2,1)S(1)} all-to-all(bf16[8,64,1024]{2,1,0:T(8,128)(2,1)S(1)} %bitcast.11), channel_id=1, replica_groups=mesh['y'=4,'x_lo'=2,'x_hi'=2,'z'=16,'core'=2] {'y','x_lo'}, dimensions={0} | all-to-all | bytes 2097152 | tf_op jit(solution)/shard_map/all_to_all | solution.py:219
  219.8 0.6 copy.6
  220.4 1.3 reshape.34
  (9 shorter events, 0.2 us)
Async XLA Ops:
  0.0 23.1 %copy-start = (f32[2,32,128]{2,1,0:T(8,128)S(1)}, f32[2,32,128]{2,1,0:T(8,128)}, u32[]{:S(2)}) copy-start(f32[2,32,128]{2,1,0:T(8,128)} %param.3) | copy-start | bytes 98308
  0.0 17.1 %collective-permute-start = (bf16[64,2,32,128]{3,2,1,0:T(8,128)(2,1)}, bf16[64,2,32,128]{3,2,1,0:T(8,128)(2,1)S(1)}, u32[]{:S(2)}, u32[]{:S(2)}) collective-permute-start(bf16[64,2,32,128]{3,2,1,0:T(8,128)(2,1)} %param.2), channel_id=1, source_target_pairs={{0,1},{1,2},{2,3},{3,4},{4,5},{5,6},{6,7},{7,8},{8,9},{9,10},{10,1... | collective-permute-start | bytes 3145736 | tf_op jit(solution)/shard_map/ppermute | solution.py:28
  5.1 16.3 %collective-permute-start.1 = (bf16[64,2,32,128]{3,2,1,0:T(8,128)(2,1)}, bf16[64,2,32,128]{3,2,1,0:T(8,128)(2,1)S(1)}, u32[]{:S(2)}, u32[]{:S(2)}) collective-permute-start(bf16[64,2,32,128]{3,2,1,0:T(8,128)(2,1)} %param.2), channel_id=1, source_target_pairs={{1,0},{2,1},{3,2},{4,3},{5,4},{6,5},{7,6},{8,7},{9,8},{10,9},{11,1... | collective-permute-start | bytes 3145736 | tf_op jit(solution)/shard_map/ppermute | solution.py:30
  26.1 16.1 %collective-permute-start.3 = (bf16[64,2,32,128]{3,2,1,0:T(8,128)(2,1)S(1)}, bf16[64,2,32,128]{3,2,1,0:T(8,128)(2,1)S(1)}, u32[]{:S(2)}, u32[]{:S(2)}) collective-permute-start(bf16[64,2,32,128]{3,2,1,0:T(8,128)(2,1)S(1)} %multiply_convert_fusion), channel_id=1, source_target_pairs={{1,0},{2,1},{3,2},{4,3},{5,4},{6,5},{7,6},{8,7},{9,8},{10,9},{11,1... | collective-permute-start | bytes 3145736 | tf_op jit(solution)/shard_map/ppermute | solution.py:30
  28.0 15.4 %collective-permute-start.2 = (bf16[64,2,32,128]{3,2,1,0:T(8,128)(2,1)S(1)}, bf16[64,2,32,128]{3,2,1,0:T(8,128)(2,1)S(1)}, u32[]{:S(2)}, u32[]{:S(2)}) collective-permute-start(bf16[64,2,32,128]{3,2,1,0:T(8,128)(2,1)S(1)} %multiply_convert_fusion), channel_id=1, source_target_pairs={{0,1},{1,2},{2,3},{3,4},{4,5},{5,6},{6,7},{7,8},{8,9},{9,10},{10,1... | collective-permute-start | bytes 3145736 | tf_op jit(solution)/shard_map/ppermute | solution.py:28
  47.2 16.9 %collective-permute-start.5 = (bf16[64,2,32,128]{3,2,1,0:T(8,128)(2,1)S(1)}, bf16[64,2,32,128]{3,2,1,0:T(8,128)(2,1)S(1)}, u32[]{:S(2)}, u32[]{:S(2)}) collective-permute-start(bf16[64,2,32,128]{3,2,1,0:T(8,128)(2,1)S(1)} %subtract_convert_fusion.1), channel_id=1, source_target_pairs={{1,0},{2,1},{3,2},{4,3},{5,4},{6,5},{7,6},{8,7},{9,8},{10,9},{11,1... | collective-permute-start | bytes 3145736 | tf_op jit(solution)/shard_map/ppermute | solution.py:30
  49.1 16.1 %collective-permute-start.4 = (bf16[64,2,32,128]{3,2,1,0:T(8,128)(2,1)S(1)}, bf16[64,2,32,128]{3,2,1,0:T(8,128)(2,1)S(1)}, u32[]{:S(2)}, u32[]{:S(2)}) collective-permute-start(bf16[64,2,32,128]{3,2,1,0:T(8,128)(2,1)S(1)} %subtract_convert_fusion.1), channel_id=1, source_target_pairs={{0,1},{1,2},{2,3},{3,4},{4,5},{5,6},{6,7},{7,8},{8,9},{9,10},{10,1... | collective-permute-start | bytes 3145736 | tf_op jit(solution)/shard_map/ppermute | solution.py:28

commit v2 on v1

--- a/solution.py
+++ b/solution.py
@@ -2,6 +2,7 @@
 
 import jax
 import jax.numpy as jnp
+import numpy as np
 from jax import lax
 from jax.experimental import pallas as pl
 from jax.experimental.pallas import tpu as pltpu
@@ -11,60 +12,77 @@
 BAND, DOM = ("y", "x_lo"), ("x_hi", "z", "core")
 NEAR, FAR = ("y", "x_lo", "core"), ("x_hi", "z")
 
+PARTS = 2
+
 HIGHEST = lax.Precision.HIGHEST
 
 spectrum_center = 7.5
 spectrum_half = 4.5
 
 
-def padded_2(cells, sides, width):
-    for axis, dim in sides:
-        count = lax.axis_size(axis)
-        ends = count - 1
-        head = lax.slice_in_dim(cells, 0, width, axis=dim)
-        tail = lax.slice_in_dim(cells, cells.shape[dim] - width, cells.shape[dim], axis=dim)
-        cells = jnp.concatenate(
-            [
-                lax.ppermute(tail, axis, [(i, (i + 1) % count) for i in range(ends)]),
-                cells,
-                lax.ppermute(head, axis, [((i + 1) % count, i) for i in range(ends)]),
-            ],
-            axis=dim,
-        )
-    return cells
-
-
-def neighbours(padded, axis_dim, offset):
-    index_list = [slice(None), slice(2, -2), slice(2, -2), slice(2, -2)]
-    index_list[axis_dim] = slice(2 + offset, padded.shape[axis_dim] - 2 + offset)
-    return padded[tuple(index_list)]
-
-
-def hamiltonian(padded, potential):
-    center = neighbours(padded, 1, 0)
-    laplace = -7.5 * center
-    for axis_dim in (1, 2, 3):
-        near_sum = neighbours(padded, axis_dim, 1) + neighbours(padded, axis_dim, -1)
-        far_sum = neighbours(padded, axis_dim, 2) + neighbours(padded, axis_dim, -2)
-        laplace = laplace + 4.0 / 3.0 * near_sum - 1.0 / 12.0 * far_sum
-    return (-0.5 * laplace + potential * center, center)
-
-
-def chebyshev(field, operate):
-    image, anchor = operate(field)
-    degree_one = ((image - spectrum_center * anchor) / spectrum_half).astype(jnp.bfloat16)
-    image, current = operate(degree_one)
-    second = (2.0 * (image - spectrum_center * current) / spectrum_half - anchor).astype(
-        jnp.bfloat16
-    )
-    image, latest = operate(second)
-    return (2.0 * (image - spectrum_center * latest) / spectrum_half - current).astype(jnp.bfloat16)
-
-
-def operator_on(field, potential):
-    widened = padded_2(field, ((DOM, 1),), 2)
-    padded = jnp.pad(widened.astype(jnp.float32), ((0, 0), (0, 0), (2, 2), (2, 2)))
-    return hamiltonian(padded, potential)
+def stencil_matrices():
+    def band(count):
+        away = np.abs(np.arange(count)[:, None] - np.arange(count)[None, :])
+        return 16.0 * (away == 1) - 1.0 * (away == 2)
+
+    eye, none = np.eye(32), np.zeros((32, 32))
+    own = np.block([[band(32), 16.0 * eye], [16.0 * eye, band(32)]])
+    left = np.block([[-eye, 16.0 * eye], [none, -eye]])
+    right = np.block([[-eye, none], [16.0 * eye, -eye]])
+    across = [np.kron(np.eye(2), part) for part in (left, own, right)]
+    return np.concatenate(across, axis=1), band(128) - 90.0 * np.eye(128)
+
+
+def stencil_kernel(degree, left_ref, cells_ref, right_ref, potential_ref, across_ref, along_ref, *rest):
+    out_ref = rest[-1]
+    double = 1.0 if degree == 0 else 2.0
+    weight = (potential_ref[...] - spectrum_center) * (double / spectrum_half)
+    weight = jnp.concatenate([weight, weight], axis=0)
+    for step in range(cells_ref.shape[0] // 128):
+        rows = slice(128 * step, 128 * step + 128)
+        cells = cells_ref[rows, :]
+        stack = jnp.concatenate([left_ref[rows, :], cells, right_ref[rows, :]], axis=0)
+        laplace = jnp.dot(across_ref[...], stack, preferred_element_type=jnp.float32)
+        laplace += jnp.dot(cells, along_ref[...], preferred_element_type=jnp.float32)
+        image = weight * cells.astype(jnp.float32) - laplace * (double / (24.0 * spectrum_half))
+        if degree > 0:
+            image = image - rest[0][rows, :].astype(jnp.float32)
+        out_ref[rows, :] = image.astype(jnp.bfloat16)
+
+
+def filtered_by_one(degree, sides, cells, before, potential, matrices):
+    operands = [sides[0], cells, sides[1], potential, *matrices] + ([before] if degree > 0 else [])
+    return pl.pallas_call(
+        partial(stencil_kernel, degree),
+        out_shape=jax.ShapeDtypeStruct(cells.shape, jnp.bfloat16),
+        in_specs=[pl.BlockSpec(memory_space=pltpu.VMEM)] * len(operands),
+        out_specs=pl.BlockSpec(memory_space=pltpu.VMEM),
+        compiler_params=pltpu.CompilerParams(vmem_limit_bytes=32 * 1024 * 1024),
+        cost_estimate=pl.CostEstimate(
+            flops=1024 * cells.size, bytes_accessed=10 * cells.size, transcendentals=0
+        ),
+    )(*operands)
+
+
+def halo(cells):
+    count = lax.axis_size(DOM)
+    left = lax.ppermute(cells, DOM, [(i, i + 1) for i in range(count - 1)])
+    right = lax.ppermute(cells, DOM, [(i + 1, i) for i in range(count - 1)])
+    return left, right
+
+
+def chebyshev(groups, potential):
+    matrices = [jnp.asarray(part, jnp.bfloat16) for part in stencil_matrices()]
+    latest, previous = list(groups), [None] * len(groups)
+    sides = [halo(cells) for cells in latest]
+    for degree in range(3):
+        for g in range(len(groups)):
+            cells = latest[g]
+            latest[g] = filtered_by_one(degree, sides[g], cells, previous[g], potential, matrices)
+            previous[g] = cells
+            if degree < 2:
+                sides[g] = halo(latest[g])
+    return latest
 
 
 def dot_nn(a, b):
@@ -208,11 +226,11 @@
 
 
 def local(orbitals, potential):
-    orb_count = orbitals.shape[0]
     cells_dev = orbitals.shape[1] * orbitals.shape[2] * orbitals.shape[3]
     total_cells = cells_dev * lax.axis_size(DOM)
-    filtered = chebyshev(orbitals, partial(operator_on, potential=potential))
-    flat = filtered.reshape(orb_count, cells_dev)
+    slabs = orbitals.reshape(PARTS, -1, orbitals.shape[3])
+    filtered = chebyshev([slabs[g] for g in range(PARTS)], potential.reshape(-1, potential.shape[2]))
+    flat = jnp.concatenate([part.reshape(-1, cells_dev) for part in filtered], axis=0)
     everyone = lax.all_to_all(flat, BAND, 1, 0, tiled=True)
     tiles = summed_everywhere(gram_tiles(everyone), 1.0 / total_cells)
     turned = rotated_by(tiles, everyone)

time: 222 us -> 212 us (0.955)
  waiting for transfers between devices: 34.6 us -> 4.59 us
  starting transfers between devices: 22.1 us -> 39.8 us
  other arithmetic: 12.2 us -> 0.19 us
  blocking collectives: 122 us -> 129 us
  Pallas kernels: 27.4 us -> 31.6 us
  local copies, waits for them, and re-layouts: 3.05 us -> 5.61 us
    ppermute x6 -> x12, waiting for transfers between devices: 34.6 us -> 4.59 us  [the longest x6 2.89 us: halo(): right = lax.ppermute(cells, DOM, [(i + 1, i) for i in range(count - 1)])]
    ppermute x6 -> x12, starting transfers between devices: 22.1 us -> 39.8 us  [the longest x6 20.9 us: halo(): left = lax.ppermute(cells, DOM, [(i, i + 1) for i in range(count - 1)])]
    convert_element_type x6 -> x0, other arithmetic: 12.1 us -> none  [the longest x1 3.29 us: chebyshev(): (2.0 * (image - spectrum_center * latest) / spectrum_half - current).asty...]
    all_to_all x1, blocking collectives: 22.5 us -> 29.5 us  [local(): everyone = lax.all_to_all(flat, BAND, 1, 0, tiled=True)]
    pallas_call x0 -> x6, Pallas kernels: none -> 4.22 us  [filtered_by_one(): pl.pallas_call(partial(stencil_kernel, degree), out_shape=jax.ShapeDtypeS...]
  transfers between devices with their start and end apart: 6 -> 12, of which waited for: 6 -> 3; matrix products, arithmetic and copies ran while one was open for 0% -> 1% of each run, Pallas kernels for 0% -> 2%
where the time goes in v2:
time: 212 us; the launch traced here: 211 us
  blocking collectives  129 us (61%)
  starting transfers between devices  39.8 us (19%)
  Pallas kernels  31.6 us (15%)
  local copies, waits for them, and re-layouts  5.61 us (3%)
  waiting for transfers between devices  4.59 us (2%)
    all_to_all x4, blocking collectives, exchange(): return lax.all_to_all(pieces, axis, 0, 0, tiled=True)  81.9 us
    all_to_all x1, blocking collectives, local(): everyone = lax.all_to_all(flat, BAND, 1, 0, tiled=True)  29.5 us
    pallas_call x1, Pallas kernels, rotated_by(): pl.pallas_call(rotation_kernel, out_shape=jax.ShapeDtypeStruct(field.shap...  26.5 us
    ppermute x6, starting transfers between devices, halo(): left = lax.ppermute(cells, DOM, [(i, i + 1) for i in range(count - 1)])  20.9 us
    ppermute x6, starting transfers between devices, halo(): right = lax.ppermute(cells, DOM, [(i + 1, i) for i in range(count - 1)])  18.9 us
    all_to_all x1, blocking collectives, local(): result = lax.all_to_all(turned, BAND, 0, 1, tiled=True)  17.3 us
  transfers between devices with their start and end apart: 12, of which 3 were waited for; matrix products, arithmetic and copies ran while one was open for 1% of the time, Pallas kernels for 2%

profile of v2, /device:TPU:1, one launch (start us, length us, event | category | flops | bytes accessed | tf_op | source)
XLA Modules:
  0.0 210.9 jit_solution(15362611557947806598)
XLA Ops:
  0.0 1.3 fusion
  1.3 8.8 %collective-permute-start.7 = (bf16[2048,128]{1,0:T(8,128)(2,1)S(1)}, bf16[2048,128]{1,0:T(8,128)(2,1)S(1)}, u32[]{:S(2)}, u32[]{:S(2)}) collective-permute-start(bf16[2048,128]{1,0:T(8,128)(2,1)S(1)} %bitcast.16), channel_id=1, source_target_pairs={{1,0},{2,1},{3,2},{4,3},{5,4},{6,5},{7,6},{8,7},{9,8},{10,9},{11,1... | collective-permute-start | bytes 1572872 | tf_op jit(solution)/shard_map/ppermute | solution.py:70
  10.1 1.9 collective-permute-start.6
  12.0 2.4 %collective-permute-start.1 = (bf16[2048,128]{1,0:T(8,128)(2,1)S(1)}, bf16[2048,128]{1,0:T(8,128)(2,1)S(1)}, u32[]{:S(2)}, u32[]{:S(2)}) collective-permute-start(bf16[2048,128]{1,0:T(8,128)(2,1)S(1)} %bitcast.12), channel_id=1, source_target_pairs={{1,0},{2,1},{3,2},{4,3},{5,4},{6,5},{7,6},{8,7},{9,8},{10,9},{11,1... | collective-permute-start | bytes 1572872 | tf_op jit(solution)/shard_map/ppermute | solution.py:70
  14.5 3.1 %collective-permute-start = (bf16[2048,128]{1,0:T(8,128)(2,1)S(1)}, bf16[2048,128]{1,0:T(8,128)(2,1)S(1)}, u32[]{:S(2)}, u32[]{:S(2)}) collective-permute-start(bf16[2048,128]{1,0:T(8,128)(2,1)S(1)} %bitcast.13), channel_id=1, source_target_pairs={{0,1},{1,2},{2,3},{3,4},{4,5},{5,6},{6,7},{7,8},{8,9},{9,10},{10,1... | collective-permute-start | bytes 1572872 | tf_op jit(solution)/shard_map/ppermute | solution.py:69
  17.6 0.0 collective-permute-done.7.right_ref
  17.6 0.5 collective-permute-done.6.left_ref
  18.1 0.7 shard_map.49.cells_ref.rest_0_
  18.9 1.9 collective-permute-start.9
  20.8 4.4 %collective-permute-start.8 = (bf16[2048,128]{1,0:T(8,128)(2,1)S(1)}, bf16[2048,128]{1,0:T(8,128)(2,1)S(1)}, u32[]{:S(2)}, u32[]{:S(2)}) collective-permute-start(bf16[2048,128]{1,0:T(8,128)(2,1)S(1)} %shard_map.49.cells_ref.rest_0_), channel_id=1, source_target_pairs={{0,1},{1,2},{2,3},{3,4},{4,5},{5,6},{6,7},{7,8},{8,9},{9,10},{10,1... | collective-permute-start | bytes 1572872 | tf_op jit(solution)/shard_map/ppermute | solution.py:69
  25.2 0.0 collective-permute-done.1.right_ref
  25.2 0.0 collective-permute-done.left_ref
  25.2 0.7 shard_map.46.cells_ref.rest_0_
  25.9 1.9 collective-permute-start.3
  27.8 3.6 %collective-permute-start.2 = (bf16[2048,128]{1,0:T(8,128)(2,1)S(1)}, bf16[2048,128]{1,0:T(8,128)(2,1)S(1)}, u32[]{:S(2)}, u32[]{:S(2)}) collective-permute-start(bf16[2048,128]{1,0:T(8,128)(2,1)S(1)} %shard_map.46.cells_ref.rest_0_), channel_id=1, source_target_pairs={{0,1},{1,2},{2,3},{3,4},{4,5},{5,6},{6,7},{7,8},{8,9},{9,10},{10,1... | collective-permute-start | bytes 1572872 | tf_op jit(solution)/shard_map/ppermute | solution.py:69
  31.5 0.0 collective-permute-done.9.right_ref
  31.5 0.0 collective-permute-done.8.left_ref
  31.5 0.7 shard_map.50.cells_ref
  32.2 1.9 collective-permute-start.11
  34.1 4.2 %collective-permute-start.10 = (bf16[2048,128]{1,0:T(8,128)(2,1)S(1)}, bf16[2048,128]{1,0:T(8,128)(2,1)S(1)}, u32[]{:S(2)}, u32[]{:S(2)}) collective-permute-start(bf16[2048,128]{1,0:T(8,128)(2,1)S(1)} %shard_map.50.cells_ref), channel_id=1, source_target_pairs={{0,1},{1,2},{2,3},{3,4},{4,5},{5,6},{6,7},{7,8},{8,9},{9,10},{10,1... | collective-permute-start | bytes 1572872 | tf_op jit(solution)/shard_map/ppermute | solution.py:69
  38.3 0.0 collective-permute-done.3.right_ref
  38.3 0.0 collective-permute-done.2.left_ref
  38.3 0.7 shard_map.47.cells_ref
  39.0 1.9 collective-permute-start.5
  41.0 3.6 %collective-permute-start.4 = (bf16[2048,128]{1,0:T(8,128)(2,1)S(1)}, bf16[2048,128]{1,0:T(8,128)(2,1)S(1)}, u32[]{:S(2)}, u32[]{:S(2)}) collective-permute-start(bf16[2048,128]{1,0:T(8,128)(2,1)S(1)} %shard_map.47.cells_ref), channel_id=1, source_target_pairs={{0,1},{1,2},{2,3},{3,4},{4,5},{5,6},{6,7},{7,8},{8,9},{9,10},{10,1... | collective-permute-start | bytes 1572872 | tf_op jit(solution)/shard_map/ppermute | solution.py:69
  44.6 0.0 collective-permute-done.11.right_ref
  44.6 0.0 collective-permute-done.10.left_ref
  44.6 0.7 shard_map.51
  45.4 0.2 concatenate.9
  45.6 1.1 copy.9
  46.7 2.9 %collective-permute-done.5.right_ref = bf16[2048,128]{1,0:T(8,128)(2,1)S(1)} collective-permute-done((bf16[2048,128]{1,0:T(8,128)(2,1)S(1)}, bf16[2048,128]{1,0:T(8,128)(2,1)S(1)}, u32[]{:S(2)}, u32[]{:S(2)}) %collective-permute-start.5) | collective-permute-done | bytes 524320 | tf_op jit(solution)/shard_map/ppermute | solution.py:70
  49.6 1.2 collective-permute-done.4.left_ref
  50.7 0.7 shard_map.48
  51.4 0.0 copy-start.3
  51.5 0.2 concatenate.8
  51.7 0.3 copy.8
  52.0 0.5 copy-done.3
  52.5 0.1 pad_maximum_fusion
  52.6 29.5 %all_to_all.52 = bf16[64,8,1024]{2,0,1:T(8,128)(2,1)S(1)} all-to-all(bf16[64,8,1024]{2,0,1:T(8,128)(2,1)S(1)} %pad_maximum_fusion), channel_id=1, replica_groups=mesh['y'=4,'x_lo'=2,'x_hi'=2,'z'=16,'core'=2] {'y','x_lo'}, dimensions={1} | all-to-all | bytes 2097152 | tf_op jit(solution)/shard_map/all_to_all | solution.py:234
  82.1 0.9 shard_map.52
  83.1 14.6 %all_to_all.53 = f32[16,80,128]{2,1,0:T(8,128)S(1)} all-to-all(f32[16,80,128]{2,1,0:T(8,128)S(1)} %bitcast.21), channel_id=1, replica_groups=mesh['y'=4,'x_lo'=2,'x_hi'=2,'z'=16,'core'=2] {'y','x_lo','core'}, dimensions={0} | all-to-all | bytes 1310720 | tf_op jit(solution)/shard_map/all_to_all | solution.py:213
  97.8 32.3 %all_to_all.54 = f32[32,3,128]{2,1,0:T(4,128)S(1)} all-to-all(f32[32,3,128]{2,1,0:T(4,128)S(1)} %reshape.43), channel_id=1, replica_groups=mesh['y'=4,'x_lo'=2,'x_hi'=2,'z'=16,'core'=2] {'x_hi','z'}, dimensions={0} | all-to-all | bytes 98304 | tf_op jit(solution)/shard_map/all_to_all | solution.py:213
  130.2 17.7 %all_to_all.55 = f32[32,3,128]{2,1,0:T(4,128)S(1)} all-to-all(f32[32,3,128]{2,1,0:T(4,128)S(1)} %broadcast_in_dim.4), channel_id=1, replica_groups=mesh['y'=4,'x_lo'=2,'x_hi'=2,'z'=16,'core'=2] {'x_hi','z'}, dimensions={0} | all-to-all | bytes 98304 | tf_op jit(solution)/shard_map/all_to_all | solution.py:213
  148.0 17.3 %all_to_all.56 = f32[16,80,128]{2,1,0:T(8,128)S(1)} all-to-all(f32[16,80,128]{2,1,0:T(8,128)S(1)} %broadcast_in_dim.5), channel_id=1, replica_groups=mesh['y'=4,'x_lo'=2,'x_hi'=2,'z'=16,'core'=2] {'y','x_lo','core'}, dimensions={0} | all-to-all | bytes 1310720 | tf_op jit(solution)/shard_map/all_to_all | solution.py:213
  165.2 26.5 %shard_map.53 = bf16[512,1024]{1,0:T(8,128)(2,1)S(1)} custom-call(f32[1280,128]{1,0:T(8,128)S(1)} %bitcast.22, bf16[512,1024]{1,0:T(8,128)(2,1)S(1)} %bitcast.11), custom_call_target="tpu_custom_call" | custom-call | tf_op jit(solution)/shard_map/pallas_call | solution.py:197
  191.7 17.3 %all_to_all.57 = bf16[8,64,1024]{2,1,0:T(8,128)(2,1)S(1)} all-to-all(bf16[8,64,1024]{2,1,0:T(8,128)(2,1)S(1)} %bitcast.20), channel_id=1, replica_groups=mesh['y'=4,'x_lo'=2,'x_hi'=2,'z'=16,'core'=2] {'y','x_lo'}, dimensions={0} | all-to-all | bytes 2097152 | tf_op jit(solution)/shard_map/all_to_all | solution.py:237
  209.0 0.6 copy.10
  209.6 1.3 reshape.46
  (15 shorter events, 0.2 us)
Async XLA Ops:
  0.0 18.1 %copy-start = (bf16[128,384]{1,0:T(8,128)(2,1)S(1)}, bf16[128,384]{1,0:T(8,128)(2,1)}, u32[]{:S(2)}) copy-start(bf16[128,384]{1,0:T(8,128)(2,1)} %constant.10.clone.across_ref) | copy-start | bytes 294916
  0.0 18.1 %copy-start.2 = (bf16[128,128]{1,0:T(8,128)(2,1)S(1)}, bf16[128,128]{1,0:T(8,128)(2,1)}, u32[]{:S(2)}) copy-start(bf16[128,128]{1,0:T(8,128)(2,1)} %constant.11.clone.along_ref) | copy-start | bytes 98308
  0.0 18.1 %copy-start.1 = (f32[2,32,128]{2,1,0:T(8,128)S(1)}, f32[2,32,128]{2,1,0:T(8,128)}, u32[]{:S(2)}) copy-start(f32[2,32,128]{2,1,0:T(8,128)} %param.5) | copy-start | bytes 98308
  1.3 16.3 %collective-permute-start.7 = (bf16[2048,128]{1,0:T(8,128)(2,1)S(1)}, bf16[2048,128]{1,0:T(8,128)(2,1)S(1)}, u32[]{:S(2)}, u32[]{:S(2)}) collective-permute-start(bf16[2048,128]{1,0:T(8,128)(2,1)S(1)} %bitcast.16), channel_id=1, source_target_pairs={{1,0},{2,1},{3,2},{4,3},{5,4},{6,5},{7,6},{8,7},{9,8},{10,9},{11,1... | collective-permute-start | bytes 1572872 | tf_op jit(solution)/shard_map/ppermute | solution.py:70
  10.1 8.0 %collective-permute-start.6 = (bf16[2048,128]{1,0:T(8,128)(2,1)S(1)}, bf16[2048,128]{1,0:T(8,128)(2,1)S(1)}, u32[]{:S(2)}, u32[]{:S(2)}) collective-permute-start(bf16[2048,128]{1,0:T(8,128)(2,1)S(1)} %bitcast.17), channel_id=1, source_target_pairs={{0,1},{1,2},{2,3},{3,4},{4,5},{5,6},{6,7},{7,8},{8,9},{9,10},{10,1... | collective-permute-start | bytes 1572872 | tf_op jit(solution)/shard_map/ppermute | solution.py:69
  12.0 13.2 %collective-permute-start.1 = (bf16[2048,128]{1,0:T(8,128)(2,1)S(1)}, bf16[2048,128]{1,0:T(8,128)(2,1)S(1)}, u32[]{:S(2)}, u32[]{:S(2)}) collective-permute-start(bf16[2048,128]{1,0:T(8,128)(2,1)S(1)} %bitcast.12), channel_id=1, source_target_pairs={{1,0},{2,1},{3,2},{4,3},{5,4},{6,5},{7,6},{8,7},{9,8},{10,9},{11,1... | collective-permute-start | bytes 1572872 | tf_op jit(solution)/shard_map/ppermute | solution.py:70
  14.5 10.7 %collective-permute-start = (bf16[2048,128]{1,0:T(8,128)(2,1)S(1)}, bf16[2048,128]{1,0:T(8,128)(2,1)S(1)}, u32[]{:S(2)}, u32[]{:S(2)}) collective-permute-start(bf16[2048,128]{1,0:T(8,128)(2,1)S(1)} %bitcast.13), channel_id=1, source_target_pairs={{0,1},{1,2},{2,3},{3,4},{4,5},{5,6},{6,7},{7,8},{8,9},{9,10},{10,1... | collective-permute-start | bytes 1572872 | tf_op jit(solution)/shard_map/ppermute | solution.py:69
  18.9 12.6 %collective-permute-start.9 = (bf16[2048,128]{1,0:T(8,128)(2,1)S(1)}, bf16[2048,128]{1,0:T(8,128)(2,1)S(1)}, u32[]{:S(2)}, u32[]{:S(2)}) collective-permute-start(bf16[2048,128]{1,0:T(8,128)(2,1)S(1)} %shard_map.49.cells_ref.rest_0_), channel_id=1, source_target_pairs={{1,0},{2,1},{3,2},{4,3},{5,4},{6,5},{7,6},{8,7},{9,8},{10,9},{11,1... | collective-permute-start | bytes 1572872 | tf_op jit(solution)/shard_map/ppermute | solution.py:70
  20.8 10.7 %collective-permute-start.8 = (bf16[2048,128]{1,0:T(8,128)(2,1)S(1)}, bf16[2048,128]{1,0:T(8,128)(2,1)S(1)}, u32[]{:S(2)}, u32[]{:S(2)}) collective-permute-start(bf16[2048,128]{1,0:T(8,128)(2,1)S(1)} %shard_map.49.cells_ref.rest_0_), channel_id=1, source_target_pairs={{0,1},{1,2},{2,3},{3,4},{4,5},{5,6},{6,7},{7,8},{8,9},{9,10},{10,1... | collective-permute-start | bytes 1572872 | tf_op jit(solution)/shard_map/ppermute | solution.py:69
  25.9 12.4 %collective-permute-start.3 = (bf16[2048,128]{1,0:T(8,128)(2,1)S(1)}, bf16[2048,128]{1,0:T(8,128)(2,1)S(1)}, u32[]{:S(2)}, u32[]{:S(2)}) collective-permute-start(bf16[2048,128]{1,0:T(8,128)(2,1)S(1)} %shard_map.46.cells_ref.rest_0_), channel_id=1, source_target_pairs={{1,0},{2,1},{3,2},{4,3},{5,4},{6,5},{7,6},{8,7},{9,8},{10,9},{11,1... | collective-permute-start | bytes 1572872 | tf_op jit(solution)/shard_map/ppermute | solution.py:70
  27.8 10.5 %collective-permute-start.2 = (bf16[2048,128]{1,0:T(8,128)(2,1)S(1)}, bf16[2048,128]{1,0:T(8,128)(2,1)S(1)}, u32[]{:S(2)}, u32[]{:S(2)}) collective-permute-start(bf16[2048,128]{1,0:T(8,128)(2,1)S(1)} %shard_map.46.cells_ref.rest_0_), channel_id=1, source_target_pairs={{0,1},{1,2},{2,3},{3,4},{4,5},{5,6},{6,7},{7,8},{8,9},{9,10},{10,1... | collective-permute-start | bytes 1572872 | tf_op jit(solution)/shard_map/ppermute | solution.py:69
  32.2 12.4 %collective-permute-start.11 = (bf16[2048,128]{1,0:T(8,128)(2,1)S(1)}, bf16[2048,128]{1,0:T(8,128)(2,1)S(1)}, u32[]{:S(2)}, u32[]{:S(2)}) collective-permute-start(bf16[2048,128]{1,0:T(8,128)(2,1)S(1)} %shard_map.50.cells_ref), channel_id=1, source_target_pairs={{1,0},{2,1},{3,2},{4,3},{5,4},{6,5},{7,6},{8,7},{9,8},{10,9},{11,1... | collective-permute-start | bytes 1572872 | tf_op jit(solution)/shard_map/ppermute | solution.py:70
  34.1 10.5 %collective-permute-start.10 = (bf16[2048,128]{1,0:T(8,128)(2,1)S(1)}, bf16[2048,128]{1,0:T(8,128)(2,1)S(1)}, u32[]{:S(2)}, u32[]{:S(2)}) collective-permute-start(bf16[2048,128]{1,0:T(8,128)(2,1)S(1)} %shard_map.50.cells_ref), channel_id=1, source_target_pairs={{0,1},{1,2},{2,3},{3,4},{4,5},{5,6},{6,7},{7,8},{8,9},{9,10},{10,1... | collective-permute-start | bytes 1572872 | tf_op jit(solution)/shard_map/ppermute | solution.py:69
  39.0 10.5 %collective-permute-start.5 = (bf16[2048,128]{1,0:T(8,128)(2,1)S(1)}, bf16[2048,128]{1,0:T(8,128)(2,1)S(1)}, u32[]{:S(2)}, u32[]{:S(2)}) collective-permute-start(bf16[2048,128]{1,0:T(8,128)(2,1)S(1)} %shard_map.47.cells_ref), channel_id=1, source_target_pairs={{1,0},{2,1},{3,2},{4,3},{5,4},{6,5},{7,6},{8,7},{9,8},{10,9},{11,1... | collective-permute-start | bytes 1572872 | tf_op jit(solution)/shard_map/ppermute | solution.py:70
  41.0 9.8 %collective-permute-start.4 = (bf16[2048,128]{1,0:T(8,128)(2,1)S(1)}, bf16[2048,128]{1,0:T(8,128)(2,1)S(1)}, u32[]{:S(2)}, u32[]{:S(2)}) collective-permute-start(bf16[2048,128]{1,0:T(8,128)(2,1)S(1)} %shard_map.47.cells_ref), channel_id=1, source_target_pairs={{0,1},{1,2},{2,3},{3,4},{4,5},{5,6},{6,7},{7,8},{8,9},{9,10},{10,1... | collective-permute-start | bytes 1572872 | tf_op jit(solution)/shard_map/ppermute | solution.py:69
  51.4 1.0 copy-start.3

commit v3 on v2

--- a/solution.py
+++ b/solution.py
@@ -9,8 +9,8 @@
 from jax.sharding import Mesh
 from jax.sharding import PartitionSpec as P
 
-BAND, DOM = ("y", "x_lo"), ("x_hi", "z", "core")
-NEAR, FAR = ("y", "x_lo", "core"), ("x_hi", "z")
+BAND, DOM = ("y", "x_lo"), ("x_hi", "z_hi", "z_lo", "core")
+STAGES = ("y", "x_lo", "core"), ("z_lo",), ("x_hi", "z_hi")
 
 PARTS = 2
 
@@ -214,15 +214,18 @@
 
 
 def summed_everywhere(terms, scale):
-    first, second = lax.axis_size(NEAR), lax.axis_size(FAR)
-    rows = terms.shape[0] // first
-    share = -(-rows // second)
-    part = jnp.sum(exchange(terms.reshape(first, rows, 128), NEAR), axis=0)
-    part = jnp.pad(part, ((0, share * second - rows), (0, 0))).reshape(second, share, 128)
-    own = jnp.sum(exchange(part, FAR), axis=0, keepdims=True) * scale
-    part = exchange(jnp.broadcast_to(own, (second, share, 128)), FAR)
-    part = part.reshape(share * second, 128)[:rows]
-    return exchange(jnp.broadcast_to(part[None], (first, rows, 128)), NEAR).reshape(terms.shape)
+    part, kept = terms, []
+    for axis in STAGES:
+        count, rows = lax.axis_size(axis), part.shape[0]
+        share = -(-rows // count)
+        kept.append((axis, count, share, rows))
+        part = jnp.pad(part, ((0, share * count - rows), (0, 0))).reshape(count, share, 128)
+        part = jnp.sum(exchange(part, axis), axis=0)
+    part = part * scale
+    for axis, count, share, rows in reversed(kept):
+        part = exchange(jnp.broadcast_to(part[None], (count, share, 128)), axis)
+        part = part.reshape(count * share, 128)[:rows]
+    return part
 
 
 def local(orbitals, potential):
@@ -239,7 +242,7 @@
 
 
 def solution(mesh):
-    named = Mesh(mesh.devices.reshape(4, 2, 2, 16, 2), ("y", "x_lo", "x_hi", "z", "core"))
+    named = Mesh(mesh.devices.reshape(4, 2, 2, 4, 4, 2), BAND + DOM)
     placed = (P(BAND, DOM, None, None), P(DOM, None, None))
     return jax.shard_map(
         local, mesh=named, in_specs=placed, out_specs=P(BAND, DOM, None, None), check_vma=False

time: 212 us -> 225 us (1.061)
  blocking collectives: 129 us -> 142 us
    all_to_all x4 -> x6, blocking collectives: 81.9 us -> 95.4 us  [exchange(): return lax.all_to_all(pieces, axis, 0, 0, tiled=True)]
where the time goes in v3:
time: 225 us; the launch traced here: 224 us
  blocking collectives  142 us (63%)
  starting transfers between devices  39.8 us (18%)
  Pallas kernels  31.6 us (14%)
  local copies, waits for them, and re-layouts  5.6 us (2%)
  waiting for transfers between devices  4.59 us (2%)
    all_to_all x6, blocking collectives, exchange(): return lax.all_to_all(pieces, axis, 0, 0, tiled=True)  95.4 us
    all_to_all x1, blocking collectives, local(): everyone = lax.all_to_all(flat, BAND, 1, 0, tiled=True)  29.5 us
    pallas_call x1, Pallas kernels, rotated_by(): pl.pallas_call(rotation_kernel, out_shape=jax.ShapeDtypeStruct(field.shap...  26.5 us
    ppermute x6, starting transfers between devices, halo(): left = lax.ppermute(cells, DOM, [(i, i + 1) for i in range(count - 1)])  20.9 us
    ppermute x6, starting transfers between devices, halo(): right = lax.ppermute(cells, DOM, [(i + 1, i) for i in range(count - 1)])  18.9 us
    all_to_all x1, blocking collectives, local(): result = lax.all_to_all(turned, BAND, 0, 1, tiled=True)  17.3 us
  transfers between devices with their start and end apart: 12, of which 3 were waited for; matrix products, arithmetic and copies ran while one was open for 1% of the time, Pallas kernels for 2%

profile of v3, /device:TPU:1, one launch (start us, length us, event | category | flops | bytes accessed | tf_op | source)
XLA Modules:
  0.0 224.3 jit_solution(5493306946985282656)
XLA Ops:
  0.0 1.3 fusion
  1.3 8.8 %collective-permute-start.7 = (bf16[2048,128]{1,0:T(8,128)(2,1)S(1)}, bf16[2048,128]{1,0:T(8,128)(2,1)S(1)}, u32[]{:S(2)}, u32[]{:S(2)}) collective-permute-start(bf16[2048,128]{1,0:T(8,128)(2,1)S(1)} %bitcast.17), channel_id=1, source_target_pairs={{1,0},{2,1},{3,2},{4,3},{5,4},{6,5},{7,6},{8,7},{9,8},{10,9},{11,1... | collective-permute-start | bytes 1572872 | tf_op jit(solution)/shard_map/ppermute | solution.py:70
  10.1 1.9 collective-permute-start.6
  12.0 2.4 %collective-permute-start.1 = (bf16[2048,128]{1,0:T(8,128)(2,1)S(1)}, bf16[2048,128]{1,0:T(8,128)(2,1)S(1)}, u32[]{:S(2)}, u32[]{:S(2)}) collective-permute-start(bf16[2048,128]{1,0:T(8,128)(2,1)S(1)} %bitcast.13), channel_id=1, source_target_pairs={{1,0},{2,1},{3,2},{4,3},{5,4},{6,5},{7,6},{8,7},{9,8},{10,9},{11,1... | collective-permute-start | bytes 1572872 | tf_op jit(solution)/shard_map/ppermute | solution.py:70
  14.5 3.1 %collective-permute-start = (bf16[2048,128]{1,0:T(8,128)(2,1)S(1)}, bf16[2048,128]{1,0:T(8,128)(2,1)S(1)}, u32[]{:S(2)}, u32[]{:S(2)}) collective-permute-start(bf16[2048,128]{1,0:T(8,128)(2,1)S(1)} %bitcast.14), channel_id=1, source_target_pairs={{0,1},{1,2},{2,3},{3,4},{4,5},{5,6},{6,7},{7,8},{8,9},{9,10},{10,1... | collective-permute-start | bytes 1572872 | tf_op jit(solution)/shard_map/ppermute | solution.py:69
  17.6 0.0 collective-permute-done.7.right_ref
  17.6 0.5 collective-permute-done.6.left_ref
  18.1 0.7 shard_map.49.cells_ref.rest_0_
  18.9 1.9 collective-permute-start.9
  20.8 4.4 %collective-permute-start.8 = (bf16[2048,128]{1,0:T(8,128)(2,1)S(1)}, bf16[2048,128]{1,0:T(8,128)(2,1)S(1)}, u32[]{:S(2)}, u32[]{:S(2)}) collective-permute-start(bf16[2048,128]{1,0:T(8,128)(2,1)S(1)} %shard_map.49.cells_ref.rest_0_), channel_id=1, source_target_pairs={{0,1},{1,2},{2,3},{3,4},{4,5},{5,6},{6,7},{7,8},{8,9},{9,10},{10,1... | collective-permute-start | bytes 1572872 | tf_op jit(solution)/shard_map/ppermute | solution.py:69
  25.2 0.0 collective-permute-done.1.right_ref
  25.2 0.0 collective-permute-done.left_ref
  25.2 0.7 shard_map.46.cells_ref.rest_0_
  25.9 1.9 collective-permute-start.3
  27.8 3.6 %collective-permute-start.2 = (bf16[2048,128]{1,0:T(8,128)(2,1)S(1)}, bf16[2048,128]{1,0:T(8,128)(2,1)S(1)}, u32[]{:S(2)}, u32[]{:S(2)}) collective-permute-start(bf16[2048,128]{1,0:T(8,128)(2,1)S(1)} %shard_map.46.cells_ref.rest_0_), channel_id=1, source_target_pairs={{0,1},{1,2},{2,3},{3,4},{4,5},{5,6},{6,7},{7,8},{8,9},{9,10},{10,1... | collective-permute-start | bytes 1572872 | tf_op jit(solution)/shard_map/ppermute | solution.py:69
  31.5 0.0 collective-permute-done.9.right_ref
  31.5 0.0 collective-permute-done.8.left_ref
  31.5 0.7 shard_map.50.cells_ref
  32.2 1.9 collective-permute-start.11
  34.1 4.2 %collective-permute-start.10 = (bf16[2048,128]{1,0:T(8,128)(2,1)S(1)}, bf16[2048,128]{1,0:T(8,128)(2,1)S(1)}, u32[]{:S(2)}, u32[]{:S(2)}) collective-permute-start(bf16[2048,128]{1,0:T(8,128)(2,1)S(1)} %shard_map.50.cells_ref), channel_id=1, source_target_pairs={{0,1},{1,2},{2,3},{3,4},{4,5},{5,6},{6,7},{7,8},{8,9},{9,10},{10,1... | collective-permute-start | bytes 1572872 | tf_op jit(solution)/shard_map/ppermute | solution.py:69
  38.3 0.0 collective-permute-done.3.right_ref
  38.3 0.7 shard_map.47.cells_ref
  39.0 1.9 collective-permute-start.5
  41.0 3.6 %collective-permute-start.4 = (bf16[2048,128]{1,0:T(8,128)(2,1)S(1)}, bf16[2048,128]{1,0:T(8,128)(2,1)S(1)}, u32[]{:S(2)}, u32[]{:S(2)}) collective-permute-start(bf16[2048,128]{1,0:T(8,128)(2,1)S(1)} %shard_map.47.cells_ref), channel_id=1, source_target_pairs={{0,1},{1,2},{2,3},{3,4},{4,5},{5,6},{6,7},{7,8},{8,9},{9,10},{10,1... | collective-permute-start | bytes 1572872 | tf_op jit(solution)/shard_map/ppermute | solution.py:69
  44.6 0.0 collective-permute-done.10.left_ref
  44.6 0.7 shard_map.51
  45.4 0.2 concatenate.9
  45.6 1.1 copy.9
  46.7 2.9 %collective-permute-done.5.right_ref = bf16[2048,128]{1,0:T(8,128)(2,1)S(1)} collective-permute-done((bf16[2048,128]{1,0:T(8,128)(2,1)S(1)}, bf16[2048,128]{1,0:T(8,128)(2,1)S(1)}, u32[]{:S(2)}, u32[]{:S(2)}) %collective-permute-start.5) | collective-permute-done | bytes 524320 | tf_op jit(solution)/shard_map/ppermute | solution.py:70
  49.6 1.2 collective-permute-done.4.left_ref
  50.7 0.7 shard_map.48
  51.4 0.0 copy-start.3
  51.5 0.2 concatenate.8
  51.7 0.3 copy.8
  52.0 0.5 copy-done.3
  52.5 0.1 pad_maximum_fusion
  52.6 29.5 %all_to_all.62 = bf16[64,8,1024]{2,0,1:T(8,128)(2,1)S(1)} all-to-all(bf16[64,8,1024]{2,0,1:T(8,128)(2,1)S(1)} %pad_maximum_fusion), channel_id=1, replica_groups=mesh['y'=4,'x_lo'=2,'x_hi'=2,'z_hi'=4,'z_lo'=4,'core'=2] {'y','x_lo'}, dimensions={1} | all-to-all | bytes 2097152 | tf_op jit(solution)/shard_map/all_to_all | solution.py:237
  82.1 0.9 shard_map.52
  83.1 14.6 %all_to_all.63 = f32[16,80,128]{2,1,0:T(8,128)S(1)} all-to-all(f32[16,80,128]{2,1,0:T(8,128)S(1)} %bitcast.22), channel_id=1, replica_groups=mesh['y'=4,'x_lo'=2,'x_hi'=2,'z_hi'=4,'z_lo'=4,'core'=2] {'y','x_lo','co..., dimensions={0} | all-to-all | bytes 1310720 | tf_op jit(solution)/shard_map/all_to_all | solution.py:213
  97.8 6.9 %all_to_all.64 = f32[4,20,128]{2,1,0:T(8,128)S(1)} all-to-all(f32[4,20,128]{2,1,0:T(8,128)S(1)} %reshape.46), channel_id=1, replica_groups=mesh['y'=4,'x_lo'=2,'x_hi'=2,'z_hi'=4,'z_lo'=4,'core'=2] {'z_lo'}, dimensions={0} | all-to-all | bytes 81920 | tf_op jit(solution)/shard_map/all_to_all | solution.py:213
  104.7 31.0 %all_to_all.65 = f32[8,3,128]{2,1,0:T(4,128)S(1)} all-to-all(f32[8,3,128]{2,1,0:T(4,128)S(1)} %reshape.47), channel_id=1, replica_groups=mesh['y'=4,'x_lo'=2,'x_hi'=2,'z_hi'=4,'z_lo'=4,'core'=2] {'x_hi','z_hi'}, dimensions={0} | all-to-all | bytes 24576 | tf_op jit(solution)/shard_map/all_to_all | solution.py:213
  135.8 16.2 %all_to_all.66 = f32[8,3,128]{2,1,0:T(4,128)S(1)} all-to-all(f32[8,3,128]{2,1,0:T(4,128)S(1)} %broadcast_in_dim.8), channel_id=1, replica_groups=mesh['y'=4,'x_lo'=2,'x_hi'=2,'z_hi'=4,'z_lo'=4,'core'=2] {'x_hi','z_hi'}, dimensions={0} | all-to-all | bytes 24576 | tf_op jit(solution)/shard_map/all_to_all | solution.py:213
  152.0 6.9 %all_to_all.67 = f32[4,20,128]{2,1,0:T(8,128)S(1)} all-to-all(f32[4,20,128]{2,1,0:T(8,128)S(1)} %broadcast_in_dim.9), channel_id=1, replica_groups=mesh['y'=4,'x_lo'=2,'x_hi'=2,'z_hi'=4,'z_lo'=4,'core'=2] {'z_lo'}, dimensions={0} | all-to-all | bytes 81920 | tf_op jit(solution)/shard_map/all_to_all | solution.py:213
  158.9 19.8 %all_to_all.68 = f32[16,80,128]{2,1,0:T(8,128)S(1)} all-to-all(f32[16,80,128]{2,1,0:T(8,128)S(1)} %broadcast_in_dim.22), channel_id=1, replica_groups=mesh['y'=4,'x_lo'=2,'x_hi'=2,'z_hi'=4,'z_lo'=4,'core'=2] {'y','x_lo','co..., dimensions={0} | all-to-all | bytes 1310720 | tf_op jit(solution)/shard_map/all_to_all | solution.py:213
  178.7 26.5 %shard_map.53 = bf16[512,1024]{1,0:T(8,128)(2,1)S(1)} custom-call(f32[1280,128]{1,0:T(8,128)S(1)} %bitcast.23, bf16[512,1024]{1,0:T(8,128)(2,1)S(1)} %bitcast.12), custom_call_target="tpu_custom_call" | custom-call | tf_op jit(solution)/shard_map/pallas_call | solution.py:197
  205.2 17.3 %all_to_all.69 = bf16[8,64,1024]{2,1,0:T(8,128)(2,1)S(1)} all-to-all(bf16[8,64,1024]{2,1,0:T(8,128)(2,1)S(1)} %bitcast.21), channel_id=1, replica_groups=mesh['y'=4,'x_lo'=2,'x_hi'=2,'z_hi'=4,'z_lo'=4,'core'=2] {'y','x_lo'}, dimensions={0} | all-to-all | bytes 2097152 | tf_op jit(solution)/shard_map/all_to_all | solution.py:240
  222.5 0.6 copy.10
  223.1 1.3 reshape.50
  (20 shorter events, 0.2 us)
Async XLA Ops:
  0.0 18.1 %copy-start = (bf16[128,384]{1,0:T(8,128)(2,1)S(1)}, bf16[128,384]{1,0:T(8,128)(2,1)}, u32[]{:S(2)}) copy-start(bf16[128,384]{1,0:T(8,128)(2,1)} %constant.10.clone.across_ref) | copy-start | bytes 294916
  0.0 18.1 %copy-start.2 = (bf16[128,128]{1,0:T(8,128)(2,1)S(1)}, bf16[128,128]{1,0:T(8,128)(2,1)}, u32[]{:S(2)}) copy-start(bf16[128,128]{1,0:T(8,128)(2,1)} %constant.11.clone.along_ref) | copy-start | bytes 98308
  0.0 18.1 %copy-start.1 = (f32[2,32,128]{2,1,0:T(8,128)S(1)}, f32[2,32,128]{2,1,0:T(8,128)}, u32[]{:S(2)}) copy-start(f32[2,32,128]{2,1,0:T(8,128)} %param.5) | copy-start | bytes 98308
  1.3 16.3 %collective-permute-start.7 = (bf16[2048,128]{1,0:T(8,128)(2,1)S(1)}, bf16[2048,128]{1,0:T(8,128)(2,1)S(1)}, u32[]{:S(2)}, u32[]{:S(2)}) collective-permute-start(bf16[2048,128]{1,0:T(8,128)(2,1)S(1)} %bitcast.17), channel_id=1, source_target_pairs={{1,0},{2,1},{3,2},{4,3},{5,4},{6,5},{7,6},{8,7},{9,8},{10,9},{11,1... | collective-permute-start | bytes 1572872 | tf_op jit(solution)/shard_map/ppermute | solution.py:70
  10.1 8.0 %collective-permute-start.6 = (bf16[2048,128]{1,0:T(8,128)(2,1)S(1)}, bf16[2048,128]{1,0:T(8,128)(2,1)S(1)}, u32[]{:S(2)}, u32[]{:S(2)}) collective-permute-start(bf16[2048,128]{1,0:T(8,128)(2,1)S(1)} %bitcast.18), channel_id=1, source_target_pairs={{0,1},{1,2},{2,3},{3,4},{4,5},{5,6},{6,7},{7,8},{8,9},{9,10},{10,1... | collective-permute-start | bytes 1572872 | tf_op jit(solution)/shard_map/ppermute | solution.py:69
  12.0 13.2 %collective-permute-start.1 = (bf16[2048,128]{1,0:T(8,128)(2,1)S(1)}, bf16[2048,128]{1,0:T(8,128)(2,1)S(1)}, u32[]{:S(2)}, u32[]{:S(2)}) collective-permute-start(bf16[2048,128]{1,0:T(8,128)(2,1)S(1)} %bitcast.13), channel_id=1, source_target_pairs={{1,0},{2,1},{3,2},{4,3},{5,4},{6,5},{7,6},{8,7},{9,8},{10,9},{11,1... | collective-permute-start | bytes 1572872 | tf_op jit(solution)/shard_map/ppermute | solution.py:70
  14.5 10.7 %collective-permute-start = (bf16[2048,128]{1,0:T(8,128)(2,1)S(1)}, bf16[2048,128]{1,0:T(8,128)(2,1)S(1)}, u32[]{:S(2)}, u32[]{:S(2)}) collective-permute-start(bf16[2048,128]{1,0:T(8,128)(2,1)S(1)} %bitcast.14), channel_id=1, source_target_pairs={{0,1},{1,2},{2,3},{3,4},{4,5},{5,6},{6,7},{7,8},{8,9},{9,10},{10,1... | collective-permute-start | bytes 1572872 | tf_op jit(solution)/shard_map/ppermute | solution.py:69
  18.9 12.6 %collective-permute-start.9 = (bf16[2048,128]{1,0:T(8,128)(2,1)S(1)}, bf16[2048,128]{1,0:T(8,128)(2,1)S(1)}, u32[]{:S(2)}, u32[]{:S(2)}) collective-permute-start(bf16[2048,128]{1,0:T(8,128)(2,1)S(1)} %shard_map.49.cells_ref.rest_0_), channel_id=1, source_target_pairs={{1,0},{2,1},{3,2},{4,3},{5,4},{6,5},{7,6},{8,7},{9,8},{10,9},{11,1... | collective-permute-start | bytes 1572872 | tf_op jit(solution)/shard_map/ppermute | solution.py:70
  20.8 10.7 %collective-permute-start.8 = (bf16[2048,128]{1,0:T(8,128)(2,1)S(1)}, bf16[2048,128]{1,0:T(8,128)(2,1)S(1)}, u32[]{:S(2)}, u32[]{:S(2)}) collective-permute-start(bf16[2048,128]{1,0:T(8,128)(2,1)S(1)} %shard_map.49.cells_ref.rest_0_), channel_id=1, source_target_pairs={{0,1},{1,2},{2,3},{3,4},{4,5},{5,6},{6,7},{7,8},{8,9},{9,10},{10,1... | collective-permute-start | bytes 1572872 | tf_op jit(solution)/shard_map/ppermute | solution.py:69
  25.9 12.4 %collective-permute-start.3 = (bf16[2048,128]{1,0:T(8,128)(2,1)S(1)}, bf16[2048,128]{1,0:T(8,128)(2,1)S(1)}, u32[]{:S(2)}, u32[]{:S(2)}) collective-permute-start(bf16[2048,128]{1,0:T(8,128)(2,1)S(1)} %shard_map.46.cells_ref.rest_0_), channel_id=1, source_target_pairs={{1,0},{2,1},{3,2},{4,3},{5,4},{6,5},{7,6},{8,7},{9,8},{10,9},{11,1... | collective-permute-start | bytes 1572872 | tf_op jit(solution)/shard_map/ppermute | solution.py:70
  27.8 10.5 %collective-permute-start.2 = (bf16[2048,128]{1,0:T(8,128)(2,1)S(1)}, bf16[2048,128]{1,0:T(8,128)(2,1)S(1)}, u32[]{:S(2)}, u32[]{:S(2)}) collective-permute-start(bf16[2048,128]{1,0:T(8,128)(2,1)S(1)} %shard_map.46.cells_ref.rest_0_), channel_id=1, source_target_pairs={{0,1},{1,2},{2,3},{3,4},{4,5},{5,6},{6,7},{7,8},{8,9},{9,10},{10,1... | collective-permute-start | bytes 1572872 | tf_op jit(solution)/shard_map/ppermute | solution.py:69
  32.2 12.4 %collective-permute-start.11 = (bf16[2048,128]{1,0:T(8,128)(2,1)S(1)}, bf16[2048,128]{1,0:T(8,128)(2,1)S(1)}, u32[]{:S(2)}, u32[]{:S(2)}) collective-permute-start(bf16[2048,128]{1,0:T(8,128)(2,1)S(1)} %shard_map.50.cells_ref), channel_id=1, source_target_pairs={{1,0},{2,1},{3,2},{4,3},{5,4},{6,5},{7,6},{8,7},{9,8},{10,9},{11,1... | collective-permute-start | bytes 1572872 | tf_op jit(solution)/shard_map/ppermute | solution.py:70
  34.1 10.5 %collective-permute-start.10 = (bf16[2048,128]{1,0:T(8,128)(2,1)S(1)}, bf16[2048,128]{1,0:T(8,128)(2,1)S(1)}, u32[]{:S(2)}, u32[]{:S(2)}) collective-permute-start(bf16[2048,128]{1,0:T(8,128)(2,1)S(1)} %shard_map.50.cells_ref), channel_id=1, source_target_pairs={{0,1},{1,2},{2,3},{3,4},{4,5},{5,6},{6,7},{7,8},{8,9},{9,10},{10,1... | collective-permute-start | bytes 1572872 | tf_op jit(solution)/shard_map/ppermute | solution.py:69
  39.0 10.5 %collective-permute-start.5 = (bf16[2048,128]{1,0:T(8,128)(2,1)S(1)}, bf16[2048,128]{1,0:T(8,128)(2,1)S(1)}, u32[]{:S(2)}, u32[]{:S(2)}) collective-permute-start(bf16[2048,128]{1,0:T(8,128)(2,1)S(1)} %shard_map.47.cells_ref), channel_id=1, source_target_pairs={{1,0},{2,1},{3,2},{4,3},{5,4},{6,5},{7,6},{8,7},{9,8},{10,9},{11,1... | collective-permute-start | bytes 1572872 | tf_op jit(solution)/shard_map/ppermute | solution.py:70
  41.0 9.8 %collective-permute-start.4 = (bf16[2048,128]{1,0:T(8,128)(2,1)S(1)}, bf16[2048,128]{1,0:T(8,128)(2,1)S(1)}, u32[]{:S(2)}, u32[]{:S(2)}) collective-permute-start(bf16[2048,128]{1,0:T(8,128)(2,1)S(1)} %shard_map.47.cells_ref), channel_id=1, source_target_pairs={{0,1},{1,2},{2,3},{3,4},{4,5},{5,6},{6,7},{7,8},{8,9},{9,10},{10,1... | collective-permute-start | bytes 1572872 | tf_op jit(solution)/shard_map/ppermute | solution.py:69
  51.4 1.0 copy-start.3

commit v4 on v2

--- a/solution.py
+++ b/solution.py
@@ -12,7 +12,7 @@
 BAND, DOM = ("y", "x_lo"), ("x_hi", "z", "core")
 NEAR, FAR = ("y", "x_lo", "core"), ("x_hi", "z")
 
-PARTS = 2
+BANDS, PARTS = 8, 2
 
 HIGHEST = lax.Precision.HIGHEST
 
@@ -93,11 +93,6 @@
     return lax.dot_general(a, b, (((1,), (1,)), ((), ())), precision=HIGHEST, preferred_element_type=jnp.float32)
 
 
-def reciprocal(value):
-    guess = pl.reciprocal(value, approx=True)
-    return guess * (2.0 - value * guess)
-
-
 def inverse_factor_of_block(rows):
     lane = lax.broadcasted_iota(jnp.int32, (8, 128), 1)
     sub = lax.broadcasted_iota(jnp.int32, (8, 128), 0)
@@ -112,14 +107,22 @@
         x = jnp.where(inside, (lane - k0 == sub).astype(jnp.float32), x)
         z = [jnp.broadcast_to(x[i : i + 1, :], (8, 128)) for i in range(8)]
         inv, m = [], [[None] * 8 for _ in range(8)]
+        ahead = []
+        if p < 15:
+            ahead = [jnp.broadcast_to(rows[p + 1][:, k0 + j : k0 + j + 1], (8, 128)) for j in range(8)]
+            following = jnp.where(inside, 0.0, rows[p + 1])
         for j in range(8):
-            inv.append(reciprocal(a[j][j]))
+            products = {(l, q): a[l][j] * a[q][j] for l in range(j + 1, 8) for q in range(j + 1, l + 1)}
+            inv.append(1.0 / a[j][j])
             for l in range(j + 1, 8):
                 m[l][j] = a[l][j] * inv[j]
-            for l in range(j + 1, 8):
                 for q in range(j + 1, l + 1):
-                    a[l][q] = a[l][q] - m[l][j] * a[q][j]
+                    a[l][q] = a[l][q] - products[l, q] * inv[j]
                 z[l] = z[l] - m[l][j] * z[j]
+                if ahead:
+                    ahead[l] = ahead[l] - m[l][j] * ahead[j]
+            if ahead:
+                following = following - (ahead[j] * inv[j]) * z[j]
         w = z[0] * lax.rsqrt(a[0][0])
         for i in range(1, 8):
             w = jnp.where(sub == i, z[i] * lax.rsqrt(a[i][i]), w)
@@ -130,7 +133,8 @@
         for l in range(7, 0, -1):
             for j in range(l):
                 y[j] = y[j] - m[l][j] * y[l]
-        for i in range(p + 1, 16):
+        rows[p + 1] = following
+        for i in range(p + 2, 16):
             c = [jnp.broadcast_to(rows[i][:, k0 + j : k0 + j + 1], (8, 128)) for j in range(8)]
             t = [c[j] * y[j] for j in range(8)]
             t = ((t[0] + t[1]) + (t[2] + t[3])) + ((t[4] + t[5]) + (t[6] + t[7]))
@@ -138,12 +142,17 @@
     return out
 
 
-def gram_kernel(field_ref, tiles_ref):
+def gram_kernel(*refs):
+    part_refs, field_ref, tiles_ref = refs[:-2], refs[-2], refs[-1]
+    rows = part_refs[0].shape[0] // BANDS
+    for band in range(BANDS):
+        for part, part_ref in enumerate(part_refs):
+            at = (band * len(part_refs) + part) * rows
+            field_ref[at : at + rows, :] = part_ref[band * rows : band * rows + rows, :]
     tile = 0
     for i in range(field_ref.shape[0] // 128):
-        rows = slice(128 * i, 128 * i + 128)
         terms = lax.dot_general(
-            field_ref[rows, :],
+            field_ref[128 * i : 128 * i + 128, :],
             field_ref[: 128 * i + 128, :],
             (((1,), (1,)), ((), ())),
             preferred_element_type=jnp.float32,
@@ -153,15 +162,19 @@
             tile += 1
 
 
-def gram_tiles(field):
-    count = field.shape[0] // 128
+def field_and_tiles(parts):
+    rows = sum(part.shape[0] for part in parts)
+    count = rows // 128
     return pl.pallas_call(
         gram_kernel,
-        out_shape=jax.ShapeDtypeStruct((64 * count * (count + 1), 128), jnp.float32),
-        in_specs=[pl.BlockSpec(memory_space=pltpu.VMEM)],
-        out_specs=pl.BlockSpec(memory_space=pltpu.VMEM),
+        out_shape=[
+            jax.ShapeDtypeStruct((rows, parts[0].shape[1]), jnp.bfloat16),
+            jax.ShapeDtypeStruct((64 * count * (count + 1), 128), jnp.float32),
+        ],
+        in_specs=[pl.BlockSpec(memory_space=pltpu.VMEM)] * len(parts),
+        out_specs=[pl.BlockSpec(memory_space=pltpu.VMEM)] * 2,
         compiler_params=pltpu.CompilerParams(vmem_limit_bytes=32 * 1024 * 1024),
-    )(field)
+    )(*parts)
 
 
 def rotation_kernel(tiles_ref, field_ref, out_ref, s_ref, a_ref, w_ref, r_ref):
@@ -230,9 +243,11 @@
     total_cells = cells_dev * lax.axis_size(DOM)
     slabs = orbitals.reshape(PARTS, -1, orbitals.shape[3])
     filtered = chebyshev([slabs[g] for g in range(PARTS)], potential.reshape(-1, potential.shape[2]))
-    flat = jnp.concatenate([part.reshape(-1, cells_dev) for part in filtered], axis=0)
-    everyone = lax.all_to_all(flat, BAND, 1, 0, tiled=True)
-    tiles = summed_everywhere(gram_tiles(everyone), 1.0 / total_cells)
+    shares = [
+        lax.all_to_all(part.reshape(-1, cells_dev), BAND, 1, 0, tiled=True) for part in filtered
+    ]
+    everyone, terms = field_and_tiles(shares)
+    tiles = summed_everywhere(terms, 1.0 / total_cells)
     turned = rotated_by(tiles, everyone)
     result = lax.all_to_all(turned, BAND, 0, 1, tiled=True)
     return result.reshape(orbitals.shape)

time: 212 us -> 203 us (0.958)
  blocking collectives: 129 us -> 109 us
  waiting for transfers between devices: 4.59 us -> 20.1 us
  Pallas kernels: 31.6 us -> 24.3 us
  starting transfers between devices: 39.8 us -> 43.3 us
    all_to_all x0 -> x1, waiting for transfers between devices: none -> 19 us  [local(): lax.all_to_all(part.reshape(-1, cells_dev), BAND, 1, 0, tiled=True)]
    all_to_all x1, blocking collectives: 29.5 us -> 14.2 us  [local(): lax.all_to_all(part.reshape(-1, cells_dev), BAND, 1, 0, tiled=True)]
    pallas_call x1, Pallas kernels: 26.5 us -> 19.2 us  [rotated_by(): pl.pallas_call(rotation_kernel, out_shape=jax.ShapeDtypeStruct(field.shap...]
    all_to_all x4, blocking collectives: 81.9 us -> 77.7 us  [exchange(): return lax.all_to_all(pieces, axis, 0, 0, tiled=True)]
    all_to_all x0 -> x1, starting transfers between devices: none -> 3.49 us  [local(): lax.all_to_all(part.reshape(-1, cells_dev), BAND, 1, 0, tiled=True)]
    ppermute x6, waiting for transfers between devices: 2.89 us -> 0.02 us  [halo(): right = lax.ppermute(cells, DOM, [(i + 1, i) for i in range(count - 1)])]
  transfers between devices with their start and end apart: 12 -> 13, of which waited for: 3 -> 3; matrix products, arithmetic and copies ran while one was open for 1% -> 1% of each run, Pallas kernels for 2% -> 2%
where the time goes in v4:
time: 203 us; the launch traced here: 202 us
  blocking collectives  109 us (54%)
  starting transfers between devices  43.3 us (21%)
  Pallas kernels  24.3 us (12%)
  waiting for transfers between devices  20.1 us (10%)
  local copies, waits for them, and re-layouts  5.11 us (3%)
    all_to_all x4, blocking collectives, exchange(): return lax.all_to_all(pieces, axis, 0, 0, tiled=True)  77.7 us
    ppermute x6, starting transfers between devices, halo(): left = lax.ppermute(cells, DOM, [(i, i + 1) for i in range(count - 1)])  20.9 us
    pallas_call x1, Pallas kernels, rotated_by(): pl.pallas_call(rotation_kernel, out_shape=jax.ShapeDtypeStruct(field.shap...  19.2 us
    all_to_all x1, waiting for transfers between devices, local(): lax.all_to_all(part.reshape(-1, cells_dev), BAND, 1, 0, tiled=True)  19 us
    ppermute x6, starting transfers between devices, halo(): right = lax.ppermute(cells, DOM, [(i + 1, i) for i in range(count - 1)])  18.9 us
    all_to_all x1, blocking collectives, local(): result = lax.all_to_all(turned, BAND, 0, 1, tiled=True)  17.3 us
    all_to_all x1, blocking collectives, local(): lax.all_to_all(part.reshape(-1, cells_dev), BAND, 1, 0, tiled=True)  14.2 us
    pallas_call x6, Pallas kernels, filtered_by_one(): pl.pallas_call(partial(stencil_kernel, degree), out_shape=jax.ShapeDtypeS...  4.22 us
  transfers between devices with their start and end apart: 13, of which 3 were waited for; matrix products, arithmetic and copies ran while one was open for 1% of the time, Pallas kernels for 2%

profile of v4, /device:TPU:1, one launch (start us, length us, event | category | flops | bytes accessed | tf_op | source)
XLA Modules:
  0.0 202.4 jit_solution(16217871170597334070)
XLA Ops:
  0.0 1.3 fusion
  1.3 8.8 %collective-permute-start.1 = (bf16[2048,128]{1,0:T(8,128)(2,1)S(1)}, bf16[2048,128]{1,0:T(8,128)(2,1)S(1)}, u32[]{:S(2)}, u32[]{:S(2)}) collective-permute-start(bf16[2048,128]{1,0:T(8,128)(2,1)S(1)} %bitcast.17), channel_id=1, source_target_pairs={{1,0},{2,1},{3,2},{4,3},{5,4},{6,5},{7,6},{8,7},{9,8},{10,9},{11,1... | collective-permute-start | bytes 1572872 | tf_op jit(solution)/shard_map/ppermute | solution.py:70
  10.1 1.9 collective-permute-start
  12.0 2.4 %collective-permute-start.7 = (bf16[2048,128]{1,0:T(8,128)(2,1)S(1)}, bf16[2048,128]{1,0:T(8,128)(2,1)S(1)}, u32[]{:S(2)}, u32[]{:S(2)}) collective-permute-start(bf16[2048,128]{1,0:T(8,128)(2,1)S(1)} %bitcast.13), channel_id=1, source_target_pairs={{1,0},{2,1},{3,2},{4,3},{5,4},{6,5},{7,6},{8,7},{9,8},{10,9},{11,1... | collective-permute-start | bytes 1572872 | tf_op jit(solution)/shard_map/ppermute | solution.py:70
  14.5 3.1 %collective-permute-start.6 = (bf16[2048,128]{1,0:T(8,128)(2,1)S(1)}, bf16[2048,128]{1,0:T(8,128)(2,1)S(1)}, u32[]{:S(2)}, u32[]{:S(2)}) collective-permute-start(bf16[2048,128]{1,0:T(8,128)(2,1)S(1)} %bitcast.14), channel_id=1, source_target_pairs={{0,1},{1,2},{2,3},{3,4},{4,5},{5,6},{6,7},{7,8},{8,9},{9,10},{10,1... | collective-permute-start | bytes 1572872 | tf_op jit(solution)/shard_map/ppermute | solution.py:69
  17.6 0.0 collective-permute-done.1.right_ref
  17.6 0.5 collective-permute-done.left_ref
  18.1 0.0 copy-done
  18.1 0.7 shard_map.46.cells_ref.rest_0_
  18.9 1.9 collective-permute-start.3
  20.8 4.4 %collective-permute-start.2 = (bf16[2048,128]{1,0:T(8,128)(2,1)S(1)}, bf16[2048,128]{1,0:T(8,128)(2,1)S(1)}, u32[]{:S(2)}, u32[]{:S(2)}) collective-permute-start(bf16[2048,128]{1,0:T(8,128)(2,1)S(1)} %shard_map.46.cells_ref.rest_0_), channel_id=1, source_target_pairs={{0,1},{1,2},{2,3},{3,4},{4,5},{5,6},{6,7},{7,8},{8,9},{9,10},{10,1... | collective-permute-start | bytes 1572872 | tf_op jit(solution)/shard_map/ppermute | solution.py:69
  25.2 0.0 collective-permute-done.7.right_ref
  25.2 0.0 collective-permute-done.6.left_ref
  25.2 0.7 shard_map.49.cells_ref.rest_0_
  25.9 1.9 collective-permute-start.9
  27.8 3.6 %collective-permute-start.8 = (bf16[2048,128]{1,0:T(8,128)(2,1)S(1)}, bf16[2048,128]{1,0:T(8,128)(2,1)S(1)}, u32[]{:S(2)}, u32[]{:S(2)}) collective-permute-start(bf16[2048,128]{1,0:T(8,128)(2,1)S(1)} %shard_map.49.cells_ref.rest_0_), channel_id=1, source_target_pairs={{0,1},{1,2},{2,3},{3,4},{4,5},{5,6},{6,7},{7,8},{8,9},{9,10},{10,1... | collective-permute-start | bytes 1572872 | tf_op jit(solution)/shard_map/ppermute | solution.py:69
  31.5 0.0 collective-permute-done.3.right_ref
  31.5 0.0 collective-permute-done.2.left_ref
  31.5 0.7 shard_map.47.cells_ref
  32.2 1.9 collective-permute-start.5
  34.1 4.2 %collective-permute-start.4 = (bf16[2048,128]{1,0:T(8,128)(2,1)S(1)}, bf16[2048,128]{1,0:T(8,128)(2,1)S(1)}, u32[]{:S(2)}, u32[]{:S(2)}) collective-permute-start(bf16[2048,128]{1,0:T(8,128)(2,1)S(1)} %shard_map.47.cells_ref), channel_id=1, source_target_pairs={{0,1},{1,2},{2,3},{3,4},{4,5},{5,6},{6,7},{7,8},{8,9},{9,10},{10,1... | collective-permute-start | bytes 1572872 | tf_op jit(solution)/shard_map/ppermute | solution.py:69
  38.3 0.0 collective-permute-done.9.right_ref
  38.3 0.0 collective-permute-done.8.left_ref
  38.3 0.7 shard_map.50.cells_ref
  39.0 1.9 collective-permute-start.11
  41.0 3.6 %collective-permute-start.10 = (bf16[2048,128]{1,0:T(8,128)(2,1)S(1)}, bf16[2048,128]{1,0:T(8,128)(2,1)S(1)}, u32[]{:S(2)}, u32[]{:S(2)}) collective-permute-start(bf16[2048,128]{1,0:T(8,128)(2,1)S(1)} %shard_map.50.cells_ref), channel_id=1, source_target_pairs={{0,1},{1,2},{2,3},{3,4},{4,5},{5,6},{6,7},{7,8},{8,9},{9,10},{10,1... | collective-permute-start | bytes 1572872 | tf_op jit(solution)/shard_map/ppermute | solution.py:69
  44.6 0.0 collective-permute-done.5.right_ref
  44.6 0.0 collective-permute-done.4.left_ref
  44.6 0.7 shard_map.48
  45.4 0.2 all_to_all.52
  45.6 1.1 copy.8
  46.7 3.5 %all-to-all-start = ((bf16[32,8,1024]{2,0,1:T(8,128)(2,1)}), bf16[32,8,1024]{2,0,1:T(8,128)(2,1)S(1)}, u32[]{:S(2)}, u32[]{:S(2)}) async-start(bf16[32,8,1024]{2,0,1:T(8,128)(2,1)} %copy.8), calls=%async_computation | async-start | bytes 1048576 | tf_op jit(solution)/shard_map/all_to_all | solution.py:247
  50.2 0.0 collective-permute-done.11.right_ref
  50.2 0.5 collective-permute-done.10.left_ref
  50.7 0.7 shard_map.51
  51.4 0.2 all_to_all.56
  51.7 0.3 copy.9
  52.0 19.0 %all-to-all-done = bf16[32,8,1024]{2,0,1:T(8,128)(2,1)S(1)} async-done(((bf16[32,8,1024]{2,0,1:T(8,128)(2,1)}), bf16[32,8,1024]{2,0,1:T(8,128)(2,1)S(1)}, u32[]{:S(2)}, u32[]{:S(2)}) %all-to-all-start) | async-done | bytes 524320 | tf_op jit(solution)/shard_map/all_to_all | solution.py:247
  71.0 14.2 %all_to_all.74 = bf16[32,8,1024]{2,0,1:T(8,128)(2,1)S(1)} all-to-all(bf16[32,8,1024]{2,0,1:T(8,128)(2,1)S(1)} %copy.9), channel_id=1, replica_groups=mesh['y'=4,'x_lo'=2,'x_hi'=2,'z'=16,'core'=2] {'y','x_lo'}, dimensions={1} | all-to-all | bytes 1048576 | tf_op jit(solution)/shard_map/all_to_all | solution.py:247
  85.2 0.9 shard_map.52
  86.1 14.7 %all_to_all.75 = f32[16,80,128]{2,1,0:T(8,128)S(1)} all-to-all(f32[16,80,128]{2,1,0:T(8,128)S(1)} %bitcast.31), channel_id=1, replica_groups=mesh['y'=4,'x_lo'=2,'x_hi'=2,'z'=16,'core'=2] {'y','x_lo','core'}, dimensions={0} | all-to-all | bytes 1310720 | tf_op jit(solution)/shard_map/all_to_all | solution.py:226
  100.9 28.0 %all_to_all.76 = f32[32,3,128]{2,1,0:T(4,128)S(1)} all-to-all(f32[32,3,128]{2,1,0:T(4,128)S(1)} %reshape.44), channel_id=1, replica_groups=mesh['y'=4,'x_lo'=2,'x_hi'=2,'z'=16,'core'=2] {'x_hi','z'}, dimensions={0} | all-to-all | bytes 98304 | tf_op jit(solution)/shard_map/all_to_all | solution.py:226
  129.0 17.7 %all_to_all.77 = f32[32,3,128]{2,1,0:T(4,128)S(1)} all-to-all(f32[32,3,128]{2,1,0:T(4,128)S(1)} %broadcast_in_dim.4), channel_id=1, replica_groups=mesh['y'=4,'x_lo'=2,'x_hi'=2,'z'=16,'core'=2] {'x_hi','z'}, dimensions={0} | all-to-all | bytes 98304 | tf_op jit(solution)/shard_map/all_to_all | solution.py:226
  146.8 17.3 %all_to_all.78 = f32[16,80,128]{2,1,0:T(8,128)S(1)} all-to-all(f32[16,80,128]{2,1,0:T(8,128)S(1)} %broadcast_in_dim.5), channel_id=1, replica_groups=mesh['y'=4,'x_lo'=2,'x_hi'=2,'z'=16,'core'=2] {'y','x_lo','core'}, dimensions={0} | all-to-all | bytes 1310720 | tf_op jit(solution)/shard_map/all_to_all | solution.py:226
  164.1 19.2 %shard_map.53 = bf16[512,1024]{1,0:T(8,128)(2,1)S(1)} custom-call(f32[1280,128]{1,0:T(8,128)S(1)} %bitcast.22, bf16[512,1024]{1,0:T(8,128)(2,1)S(1)} %get-tuple-element.8.field_ref), custom_call_target="tpu_custom_call" | custom-call | tf_op jit(solution)/shard_map/pallas_call | solution.py:210
  183.3 17.3 %all_to_all.79 = bf16[8,64,1024]{2,1,0:T(8,128)(2,1)S(1)} all-to-all(bf16[8,64,1024]{2,1,0:T(8,128)(2,1)S(1)} %bitcast.21), channel_id=1, replica_groups=mesh['y'=4,'x_lo'=2,'x_hi'=2,'z'=16,'core'=2] {'y','x_lo'}, dimensions={0} | all-to-all | bytes 2097152 | tf_op jit(solution)/shard_map/all_to_all | solution.py:252
  200.6 0.6 copy.10
  201.2 1.3 reshape.47
  (14 shorter events, 0.2 us)
Async XLA Ops:
  0.0 18.1 %copy-start = (bf16[128,384]{1,0:T(8,128)(2,1)S(1)}, bf16[128,384]{1,0:T(8,128)(2,1)}, u32[]{:S(2)}) copy-start(bf16[128,384]{1,0:T(8,128)(2,1)} %constant.10.clone.across_ref) | copy-start | bytes 294916
  0.0 18.1 %copy-start.2 = (bf16[128,128]{1,0:T(8,128)(2,1)S(1)}, bf16[128,128]{1,0:T(8,128)(2,1)}, u32[]{:S(2)}) copy-start(bf16[128,128]{1,0:T(8,128)(2,1)} %constant.11.clone.along_ref) | copy-start | bytes 98308
  0.0 18.1 %copy-start.1 = (f32[2,32,128]{2,1,0:T(8,128)S(1)}, f32[2,32,128]{2,1,0:T(8,128)}, u32[]{:S(2)}) copy-start(f32[2,32,128]{2,1,0:T(8,128)} %param.5) | copy-start | bytes 98308
  1.3 16.3 %collective-permute-start.1 = (bf16[2048,128]{1,0:T(8,128)(2,1)S(1)}, bf16[2048,128]{1,0:T(8,128)(2,1)S(1)}, u32[]{:S(2)}, u32[]{:S(2)}) collective-permute-start(bf16[2048,128]{1,0:T(8,128)(2,1)S(1)} %bitcast.17), channel_id=1, source_target_pairs={{1,0},{2,1},{3,2},{4,3},{5,4},{6,5},{7,6},{8,7},{9,8},{10,9},{11,1... | collective-permute-start | bytes 1572872 | tf_op jit(solution)/shard_map/ppermute | solution.py:70
  10.1 8.0 %collective-permute-start = (bf16[2048,128]{1,0:T(8,128)(2,1)S(1)}, bf16[2048,128]{1,0:T(8,128)(2,1)S(1)}, u32[]{:S(2)}, u32[]{:S(2)}) collective-permute-start(bf16[2048,128]{1,0:T(8,128)(2,1)S(1)} %bitcast.18), channel_id=1, source_target_pairs={{0,1},{1,2},{2,3},{3,4},{4,5},{5,6},{6,7},{7,8},{8,9},{9,10},{10,1... | collective-permute-start | bytes 1572872 | tf_op jit(solution)/shard_map/ppermute | solution.py:69
  12.0 13.2 %collective-permute-start.7 = (bf16[2048,128]{1,0:T(8,128)(2,1)S(1)}, bf16[2048,128]{1,0:T(8,128)(2,1)S(1)}, u32[]{:S(2)}, u32[]{:S(2)}) collective-permute-start(bf16[2048,128]{1,0:T(8,128)(2,1)S(1)} %bitcast.13), channel_id=1, source_target_pairs={{1,0},{2,1},{3,2},{4,3},{5,4},{6,5},{7,6},{8,7},{9,8},{10,9},{11,1... | collective-permute-start | bytes 1572872 | tf_op jit(solution)/shard_map/ppermute | solution.py:70
  14.5 10.7 %collective-permute-start.6 = (bf16[2048,128]{1,0:T(8,128)(2,1)S(1)}, bf16[2048,128]{1,0:T(8,128)(2,1)S(1)}, u32[]{:S(2)}, u32[]{:S(2)}) collective-permute-start(bf16[2048,128]{1,0:T(8,128)(2,1)S(1)} %bitcast.14), channel_id=1, source_target_pairs={{0,1},{1,2},{2,3},{3,4},{4,5},{5,6},{6,7},{7,8},{8,9},{9,10},{10,1... | collective-permute-start | bytes 1572872 | tf_op jit(solution)/shard_map/ppermute | solution.py:69
  18.9 12.6 %collective-permute-start.3 = (bf16[2048,128]{1,0:T(8,128)(2,1)S(1)}, bf16[2048,128]{1,0:T(8,128)(2,1)S(1)}, u32[]{:S(2)}, u32[]{:S(2)}) collective-permute-start(bf16[2048,128]{1,0:T(8,128)(2,1)S(1)} %shard_map.46.cells_ref.rest_0_), channel_id=1, source_target_pairs={{1,0},{2,1},{3,2},{4,3},{5,4},{6,5},{7,6},{8,7},{9,8},{10,9},{11,1... | collective-permute-start | bytes 1572872 | tf_op jit(solution)/shard_map/ppermute | solution.py:70
  20.8 10.7 %collective-permute-start.2 = (bf16[2048,128]{1,0:T(8,128)(2,1)S(1)}, bf16[2048,128]{1,0:T(8,128)(2,1)S(1)}, u32[]{:S(2)}, u32[]{:S(2)}) collective-permute-start(bf16[2048,128]{1,0:T(8,128)(2,1)S(1)} %shard_map.46.cells_ref.rest_0_), channel_id=1, source_target_pairs={{0,1},{1,2},{2,3},{3,4},{4,5},{5,6},{6,7},{7,8},{8,9},{9,10},{10,1... | collective-permute-start | bytes 1572872 | tf_op jit(solution)/shard_map/ppermute | solution.py:69
  25.9 12.4 %collective-permute-start.9 = (bf16[2048,128]{1,0:T(8,128)(2,1)S(1)}, bf16[2048,128]{1,0:T(8,128)(2,1)S(1)}, u32[]{:S(2)}, u32[]{:S(2)}) collective-permute-start(bf16[2048,128]{1,0:T(8,128)(2,1)S(1)} %shard_map.49.cells_ref.rest_0_), channel_id=1, source_target_pairs={{1,0},{2,1},{3,2},{4,3},{5,4},{6,5},{7,6},{8,7},{9,8},{10,9},{11,1... | collective-permute-start | bytes 1572872 | tf_op jit(solution)/shard_map/ppermute | solution.py:70
  27.8 10.5 %collective-permute-start.8 = (bf16[2048,128]{1,0:T(8,128)(2,1)S(1)}, bf16[2048,128]{1,0:T(8,128)(2,1)S(1)}, u32[]{:S(2)}, u32[]{:S(2)}) collective-permute-start(bf16[2048,128]{1,0:T(8,128)(2,1)S(1)} %shard_map.49.cells_ref.rest_0_), channel_id=1, source_target_pairs={{0,1},{1,2},{2,3},{3,4},{4,5},{5,6},{6,7},{7,8},{8,9},{9,10},{10,1... | collective-permute-start | bytes 1572872 | tf_op jit(solution)/shard_map/ppermute | solution.py:69
  32.2 12.4 %collective-permute-start.5 = (bf16[2048,128]{1,0:T(8,128)(2,1)S(1)}, bf16[2048,128]{1,0:T(8,128)(2,1)S(1)}, u32[]{:S(2)}, u32[]{:S(2)}) collective-permute-start(bf16[2048,128]{1,0:T(8,128)(2,1)S(1)} %shard_map.47.cells_ref), channel_id=1, source_target_pairs={{1,0},{2,1},{3,2},{4,3},{5,4},{6,5},{7,6},{8,7},{9,8},{10,9},{11,1... | collective-permute-start | bytes 1572872 | tf_op jit(solution)/shard_map/ppermute | solution.py:70
  34.1 10.5 %collective-permute-start.4 = (bf16[2048,128]{1,0:T(8,128)(2,1)S(1)}, bf16[2048,128]{1,0:T(8,128)(2,1)S(1)}, u32[]{:S(2)}, u32[]{:S(2)}) collective-permute-start(bf16[2048,128]{1,0:T(8,128)(2,1)S(1)} %shard_map.47.cells_ref), channel_id=1, source_target_pairs={{0,1},{1,2},{2,3},{3,4},{4,5},{5,6},{6,7},{7,8},{8,9},{9,10},{10,1... | collective-permute-start | bytes 1572872 | tf_op jit(solution)/shard_map/ppermute | solution.py:69
  39.0 11.1 %collective-permute-start.11 = (bf16[2048,128]{1,0:T(8,128)(2,1)S(1)}, bf16[2048,128]{1,0:T(8,128)(2,1)S(1)}, u32[]{:S(2)}, u32[]{:S(2)}) collective-permute-start(bf16[2048,128]{1,0:T(8,128)(2,1)S(1)} %shard_map.50.cells_ref), channel_id=1, source_target_pairs={{1,0},{2,1},{3,2},{4,3},{5,4},{6,5},{7,6},{8,7},{9,8},{10,9},{11,1... | collective-permute-start | bytes 1572872 | tf_op jit(solution)/shard_map/ppermute | solution.py:70
  41.0 9.8 %collective-permute-start.10 = (bf16[2048,128]{1,0:T(8,128)(2,1)S(1)}, bf16[2048,128]{1,0:T(8,128)(2,1)S(1)}, u32[]{:S(2)}, u32[]{:S(2)}) collective-permute-start(bf16[2048,128]{1,0:T(8,128)(2,1)S(1)} %shard_map.50.cells_ref), channel_id=1, source_target_pairs={{0,1},{1,2},{2,3},{3,4},{4,5},{5,6},{6,7},{7,8},{8,9},{9,10},{10,1... | collective-permute-start | bytes 1572872 | tf_op jit(solution)/shard_map/ppermute | solution.py:69
  46.7 24.3 %all-to-all-start = ((bf16[32,8,1024]{2,0,1:T(8,128)(2,1)}), bf16[32,8,1024]{2,0,1:T(8,128)(2,1)S(1)}, u32[]{:S(2)}, u32[]{:S(2)}) async-start(bf16[32,8,1024]{2,0,1:T(8,128)(2,1)} %copy.8), calls=%async_computation | async-start | bytes 1048576 | tf_op jit(solution)/shard_map/all_to_all | solution.py:247

commit v5 on v4

--- a/solution.py
+++ b/solution.py
@@ -10,7 +10,7 @@
 from jax.sharding import PartitionSpec as P
 
 BAND, DOM = ("y", "x_lo"), ("x_hi", "z", "core")
-NEAR, FAR = ("y", "x_lo", "core"), ("x_hi", "z")
+NEAR = ("y", "x_lo", "core")
 
 BANDS, PARTS = 8, 2
 
@@ -227,15 +227,13 @@
 
 
 def summed_everywhere(terms, scale):
-    first, second = lax.axis_size(NEAR), lax.axis_size(FAR)
-    rows = terms.shape[0] // first
-    share = -(-rows // second)
-    part = jnp.sum(exchange(terms.reshape(first, rows, 128), NEAR), axis=0)
-    part = jnp.pad(part, ((0, share * second - rows), (0, 0))).reshape(second, share, 128)
-    own = jnp.sum(exchange(part, FAR), axis=0, keepdims=True) * scale
-    part = exchange(jnp.broadcast_to(own, (second, share, 128)), FAR)
-    part = part.reshape(share * second, 128)[:rows]
-    return exchange(jnp.broadcast_to(part[None], (first, rows, 128)), NEAR).reshape(terms.shape)
+    near, far = lax.axis_size(NEAR), lax.axis_size("z")
+    rows = terms.shape[0] // near
+    part = jnp.sum(exchange(terms.reshape(near, rows, 128), NEAR), axis=0)
+    part = jnp.sum(exchange(part.reshape(far, rows // far, 128), "z"), axis=0)
+    part = (part + lax.ppermute(part, "x_hi", [(0, 1), (1, 0)])) * scale
+    part = exchange(jnp.broadcast_to(part[None], (far,) + part.shape), "z").reshape(rows, 128)
+    return exchange(jnp.broadcast_to(part[None], (near, rows, 128)), NEAR).reshape(terms.shape)
 
 
 def local(orbitals, potential):

time: 203 us -> 203 us (level)
  blocking collectives: 109 us -> 100 us
  starting transfers between devices: 43.3 us -> 50 us
    all_to_all x4, blocking collectives: 77.7 us -> 68.7 us  [exchange(): return lax.all_to_all(pieces, axis, 0, 0, tiled=True)]
    ppermute x0 -> x1, starting transfers between devices: none -> 6.75 us  [summed_everywhere(): part = (part + lax.ppermute(part, 'x_hi', [(0, 1), (1, 0)])) * scale]
  transfers between devices with their start and end apart: 13 -> 14, of which waited for: 3 -> 4; matrix products, arithmetic and copies ran while one was open for 1% -> 1% of each run, Pallas kernels for 2% -> 2%
where the time goes in v5:
time: 203 us; the launch traced here: 201 us
  blocking collectives  100 us (49%)
  starting transfers between devices  50 us (25%)
  Pallas kernels  24.3 us (12%)
  waiting for transfers between devices  21.1 us (10%)
  local copies, waits for them, and re-layouts  5.06 us (2%)
    all_to_all x4, blocking collectives, exchange(): return lax.all_to_all(pieces, axis, 0, 0, tiled=True)  68.7 us
    ppermute x6, starting transfers between devices, halo(): left = lax.ppermute(cells, DOM, [(i, i + 1) for i in range(count - 1)])  20.9 us
    pallas_call x1, Pallas kernels, rotated_by(): pl.pallas_call(rotation_kernel, out_shape=jax.ShapeDtypeStruct(field.shap...  19.2 us
    all_to_all x1, waiting for transfers between devices, local(): lax.all_to_all(part.reshape(-1, cells_dev), BAND, 1, 0, tiled=True)  19 us
    ppermute x6, starting transfers between devices, halo(): right = lax.ppermute(cells, DOM, [(i + 1, i) for i in range(count - 1)])  18.9 us
    all_to_all x1, blocking collectives, local(): result = lax.all_to_all(turned, BAND, 0, 1, tiled=True)  17.3 us
    all_to_all x1, blocking collectives, local(): lax.all_to_all(part.reshape(-1, cells_dev), BAND, 1, 0, tiled=True)  14.2 us
    ppermute x1, starting transfers between devices, summed_everywhere(): part = (part + lax.ppermute(part, 'x_hi', [(0, 1), (1, 0)])) * scale  6.75 us
  transfers between devices with their start and end apart: 14, of which 4 were waited for; matrix products, arithmetic and copies ran while one was open for 1% of the time, Pallas kernels for 2%

profile of v5, /device:TPU:1, one launch (start us, length us, event | category | flops | bytes accessed | tf_op | source)
XLA Modules:
  0.0 201.1 jit_solution(4258304575301490615)
XLA Ops:
  0.0 1.3 fusion
  1.3 8.8 %collective-permute-start.1 = (bf16[2048,128]{1,0:T(8,128)(2,1)S(1)}, bf16[2048,128]{1,0:T(8,128)(2,1)S(1)}, u32[]{:S(2)}, u32[]{:S(2)}) collective-permute-start(bf16[2048,128]{1,0:T(8,128)(2,1)S(1)} %bitcast.17), channel_id=1, source_target_pairs={{1,0},{2,1},{3,2},{4,3},{5,4},{6,5},{7,6},{8,7},{9,8},{10,9},{11,1... | collective-permute-start | bytes 1572872 | tf_op jit(solution)/shard_map/ppermute | solution.py:70
  10.1 1.9 collective-permute-start
  12.0 2.4 %collective-permute-start.7 = (bf16[2048,128]{1,0:T(8,128)(2,1)S(1)}, bf16[2048,128]{1,0:T(8,128)(2,1)S(1)}, u32[]{:S(2)}, u32[]{:S(2)}) collective-permute-start(bf16[2048,128]{1,0:T(8,128)(2,1)S(1)} %bitcast.13), channel_id=1, source_target_pairs={{1,0},{2,1},{3,2},{4,3},{5,4},{6,5},{7,6},{8,7},{9,8},{10,9},{11,1... | collective-permute-start | bytes 1572872 | tf_op jit(solution)/shard_map/ppermute | solution.py:70
  14.5 3.1 %collective-permute-start.6 = (bf16[2048,128]{1,0:T(8,128)(2,1)S(1)}, bf16[2048,128]{1,0:T(8,128)(2,1)S(1)}, u32[]{:S(2)}, u32[]{:S(2)}) collective-permute-start(bf16[2048,128]{1,0:T(8,128)(2,1)S(1)} %bitcast.14), channel_id=1, source_target_pairs={{0,1},{1,2},{2,3},{3,4},{4,5},{5,6},{6,7},{7,8},{8,9},{9,10},{10,1... | collective-permute-start | bytes 1572872 | tf_op jit(solution)/shard_map/ppermute | solution.py:69
  17.6 0.0 collective-permute-done.1.right_ref
  17.6 0.5 collective-permute-done.left_ref
  18.1 0.7 shard_map.46.cells_ref.rest_0_
  18.9 1.9 collective-permute-start.3
  20.8 4.4 %collective-permute-start.2 = (bf16[2048,128]{1,0:T(8,128)(2,1)S(1)}, bf16[2048,128]{1,0:T(8,128)(2,1)S(1)}, u32[]{:S(2)}, u32[]{:S(2)}) collective-permute-start(bf16[2048,128]{1,0:T(8,128)(2,1)S(1)} %shard_map.46.cells_ref.rest_0_), channel_id=1, source_target_pairs={{0,1},{1,2},{2,3},{3,4},{4,5},{5,6},{6,7},{7,8},{8,9},{9,10},{10,1... | collective-permute-start | bytes 1572872 | tf_op jit(solution)/shard_map/ppermute | solution.py:69
  25.2 0.0 collective-permute-done.7.right_ref
  25.2 0.0 collective-permute-done.6.left_ref
  25.2 0.7 shard_map.49.cells_ref.rest_0_
  25.9 1.9 collective-permute-start.9
  27.8 3.6 %collective-permute-start.8 = (bf16[2048,128]{1,0:T(8,128)(2,1)S(1)}, bf16[2048,128]{1,0:T(8,128)(2,1)S(1)}, u32[]{:S(2)}, u32[]{:S(2)}) collective-permute-start(bf16[2048,128]{1,0:T(8,128)(2,1)S(1)} %shard_map.49.cells_ref.rest_0_), channel_id=1, source_target_pairs={{0,1},{1,2},{2,3},{3,4},{4,5},{5,6},{6,7},{7,8},{8,9},{9,10},{10,1... | collective-permute-start | bytes 1572872 | tf_op jit(solution)/shard_map/ppermute | solution.py:69
  31.5 0.0 collective-permute-done.3.right_ref
  31.5 0.0 collective-permute-done.2.left_ref
  31.5 0.7 shard_map.47.cells_ref
  32.2 1.9 collective-permute-start.5
  34.1 4.2 %collective-permute-start.4 = (bf16[2048,128]{1,0:T(8,128)(2,1)S(1)}, bf16[2048,128]{1,0:T(8,128)(2,1)S(1)}, u32[]{:S(2)}, u32[]{:S(2)}) collective-permute-start(bf16[2048,128]{1,0:T(8,128)(2,1)S(1)} %shard_map.47.cells_ref), channel_id=1, source_target_pairs={{0,1},{1,2},{2,3},{3,4},{4,5},{5,6},{6,7},{7,8},{8,9},{9,10},{10,1... | collective-permute-start | bytes 1572872 | tf_op jit(solution)/shard_map/ppermute | solution.py:69
  38.3 0.0 collective-permute-done.9.right_ref
  38.3 0.0 collective-permute-done.8.left_ref
  38.3 0.7 shard_map.50.cells_ref
  39.0 1.9 collective-permute-start.11
  41.0 3.6 %collective-permute-start.10 = (bf16[2048,128]{1,0:T(8,128)(2,1)S(1)}, bf16[2048,128]{1,0:T(8,128)(2,1)S(1)}, u32[]{:S(2)}, u32[]{:S(2)}) collective-permute-start(bf16[2048,128]{1,0:T(8,128)(2,1)S(1)} %shard_map.50.cells_ref), channel_id=1, source_target_pairs={{0,1},{1,2},{2,3},{3,4},{4,5},{5,6},{6,7},{7,8},{8,9},{9,10},{10,1... | collective-permute-start | bytes 1572872 | tf_op jit(solution)/shard_map/ppermute | solution.py:69
  44.6 0.0 collective-permute-done.5.right_ref
  44.6 0.0 collective-permute-done.4.left_ref
  44.6 0.7 shard_map.48
  45.4 0.2 all_to_all.52
  45.6 1.1 copy.8
  46.7 3.5 %all-to-all-start = ((bf16[32,8,1024]{2,0,1:T(8,128)(2,1)}), bf16[32,8,1024]{2,0,1:T(8,128)(2,1)S(1)}, u32[]{:S(2)}, u32[]{:S(2)}) async-start(bf16[32,8,1024]{2,0,1:T(8,128)(2,1)} %copy.8), calls=%async_computation | async-start | bytes 1048576 | tf_op jit(solution)/shard_map/all_to_all | solution.py:245
  50.2 0.5 collective-permute-done.10.left_ref
  50.7 0.7 shard_map.51
  51.4 0.2 all_to_all.56
  51.7 0.3 copy.9
  52.0 19.0 %all-to-all-done = bf16[32,8,1024]{2,0,1:T(8,128)(2,1)S(1)} async-done(((bf16[32,8,1024]{2,0,1:T(8,128)(2,1)}), bf16[32,8,1024]{2,0,1:T(8,128)(2,1)S(1)}, u32[]{:S(2)}, u32[]{:S(2)}) %all-to-all-start) | async-done | bytes 524320 | tf_op jit(solution)/shard_map/all_to_all | solution.py:245
  71.0 14.2 %all_to_all.74 = bf16[32,8,1024]{2,0,1:T(8,128)(2,1)S(1)} all-to-all(bf16[32,8,1024]{2,0,1:T(8,128)(2,1)S(1)} %copy.9), channel_id=1, replica_groups=mesh['y'=4,'x_lo'=2,'x_hi'=2,'z'=16,'core'=2] {'y','x_lo'}, dimensions={1} | all-to-all | bytes 1048576 | tf_op jit(solution)/shard_map/all_to_all | solution.py:245
  85.2 0.9 shard_map.52
  86.1 14.7 %all_to_all.75 = f32[16,80,128]{2,1,0:T(8,128)S(1)} all-to-all(f32[16,80,128]{2,1,0:T(8,128)S(1)} %bitcast.31), channel_id=1, replica_groups=mesh['y'=4,'x_lo'=2,'x_hi'=2,'z'=16,'core'=2] {'y','x_lo','core'}, dimensions={0} | all-to-all | bytes 1310720 | tf_op jit(solution)/shard_map/all_to_all | solution.py:226
  100.9 21.3 %all_to_all.76 = f32[16,5,128]{2,1,0:T(8,128)S(1)} all-to-all(f32[16,5,128]{2,1,0:T(8,128)S(1)} %reshape.38), channel_id=1, replica_groups=mesh['y'=4,'x_lo'=2,'x_hi'=2,'z'=16,'core'=2] {'z'}, dimensions={0} | all-to-all | bytes 81920 | tf_op jit(solution)/shard_map/all_to_all | solution.py:226
  122.3 6.8 %collective-permute-start.12 = (f32[5,128]{1,0:T(8,128)S(1)}, f32[5,128]{1,0:T(8,128)S(1)}, u32[]{:S(2)}, u32[]{:S(2)}) collective-permute-start(f32[5,128]{1,0:T(8,128)S(1)} %reduce_sum.19), channel_id=1, source_target_pairs={{0,32},{32,0},{1,33},{33,1},{2,34},{34,2},{3,35},{35,3},{4,36},{36... | collective-permute-start | bytes 7688 | tf_op jit(solution)/shard_map/ppermute | solution.py:234
  129.0 1.0 collective-permute-done.12
  130.0 15.2 %all_to_all.77 = f32[16,5,128]{2,1,0:T(8,128)S(1)} all-to-all(f32[16,5,128]{2,1,0:T(8,128)S(1)} %broadcast_in_dim.6), channel_id=1, replica_groups=mesh['y'=4,'x_lo'=2,'x_hi'=2,'z'=16,'core'=2] {'z'}, dimensions={0} | all-to-all | bytes 81920 | tf_op jit(solution)/shard_map/all_to_all | solution.py:226
  145.2 17.5 %all_to_all.78 = f32[16,80,128]{2,1,0:T(8,128)S(1)} all-to-all(f32[16,80,128]{2,1,0:T(8,128)S(1)} %broadcast_in_dim.15), channel_id=1, replica_groups=mesh['y'=4,'x_lo'=2,'x_hi'=2,'z'=16,'core'=2] {'y','x_lo','core'}, dimensions={0} | all-to-all | bytes 1310720 | tf_op jit(solution)/shard_map/all_to_all | solution.py:226
  162.7 19.2 %shard_map.53 = bf16[512,1024]{1,0:T(8,128)(2,1)S(1)} custom-call(f32[1280,128]{1,0:T(8,128)S(1)} %bitcast.22, bf16[512,1024]{1,0:T(8,128)(2,1)S(1)} %get-tuple-element.8.field_ref), custom_call_target="tpu_custom_call" | custom-call | tf_op jit(solution)/shard_map/pallas_call | solution.py:210
  181.9 17.3 %all_to_all.79 = bf16[8,64,1024]{2,1,0:T(8,128)(2,1)S(1)} all-to-all(bf16[8,64,1024]{2,1,0:T(8,128)(2,1)S(1)} %bitcast.21), channel_id=1, replica_groups=mesh['y'=4,'x_lo'=2,'x_hi'=2,'z'=16,'core'=2] {'y','x_lo'}, dimensions={0} | all-to-all | bytes 2097152 | tf_op jit(solution)/shard_map/all_to_all | solution.py:250
  199.2 0.6 copy.10
  199.8 1.3 reshape.40
  (14 shorter events, 0.1 us)
Async XLA Ops:
  0.0 18.1 %copy-start = (bf16[128,384]{1,0:T(8,128)(2,1)S(1)}, bf16[128,384]{1,0:T(8,128)(2,1)}, u32[]{:S(2)}) copy-start(bf16[128,384]{1,0:T(8,128)(2,1)} %constant.8.clone.across_ref) | copy-start | bytes 294916
  0.0 18.1 %copy-start.2 = (bf16[128,128]{1,0:T(8,128)(2,1)S(1)}, bf16[128,128]{1,0:T(8,128)(2,1)}, u32[]{:S(2)}) copy-start(bf16[128,128]{1,0:T(8,128)(2,1)} %constant.9.clone.along_ref) | copy-start | bytes 98308
  0.0 18.1 %copy-start.1 = (f32[2,32,128]{2,1,0:T(8,128)S(1)}, f32[2,32,128]{2,1,0:T(8,128)}, u32[]{:S(2)}) copy-start(f32[2,32,128]{2,1,0:T(8,128)} %param.5) | copy-start | bytes 98308
  1.3 16.3 %collective-permute-start.1 = (bf16[2048,128]{1,0:T(8,128)(2,1)S(1)}, bf16[2048,128]{1,0:T(8,128)(2,1)S(1)}, u32[]{:S(2)}, u32[]{:S(2)}) collective-permute-start(bf16[2048,128]{1,0:T(8,128)(2,1)S(1)} %bitcast.17), channel_id=1, source_target_pairs={{1,0},{2,1},{3,2},{4,3},{5,4},{6,5},{7,6},{8,7},{9,8},{10,9},{11,1... | collective-permute-start | bytes 1572872 | tf_op jit(solution)/shard_map/ppermute | solution.py:70
  10.1 8.0 %collective-permute-start = (bf16[2048,128]{1,0:T(8,128)(2,1)S(1)}, bf16[2048,128]{1,0:T(8,128)(2,1)S(1)}, u32[]{:S(2)}, u32[]{:S(2)}) collective-permute-start(bf16[2048,128]{1,0:T(8,128)(2,1)S(1)} %bitcast.18), channel_id=1, source_target_pairs={{0,1},{1,2},{2,3},{3,4},{4,5},{5,6},{6,7},{7,8},{8,9},{9,10},{10,1... | collective-permute-start | bytes 1572872 | tf_op jit(solution)/shard_map/ppermute | solution.py:69
  12.0 13.2 %collective-permute-start.7 = (bf16[2048,128]{1,0:T(8,128)(2,1)S(1)}, bf16[2048,128]{1,0:T(8,128)(2,1)S(1)}, u32[]{:S(2)}, u32[]{:S(2)}) collective-permute-start(bf16[2048,128]{1,0:T(8,128)(2,1)S(1)} %bitcast.13), channel_id=1, source_target_pairs={{1,0},{2,1},{3,2},{4,3},{5,4},{6,5},{7,6},{8,7},{9,8},{10,9},{11,1... | collective-permute-start | bytes 1572872 | tf_op jit(solution)/shard_map/ppermute | solution.py:70
  14.5 10.7 %collective-permute-start.6 = (bf16[2048,128]{1,0:T(8,128)(2,1)S(1)}, bf16[2048,128]{1,0:T(8,128)(2,1)S(1)}, u32[]{:S(2)}, u32[]{:S(2)}) collective-permute-start(bf16[2048,128]{1,0:T(8,128)(2,1)S(1)} %bitcast.14), channel_id=1, source_target_pairs={{0,1},{1,2},{2,3},{3,4},{4,5},{5,6},{6,7},{7,8},{8,9},{9,10},{10,1... | collective-permute-start | bytes 1572872 | tf_op jit(solution)/shard_map/ppermute | solution.py:69
  18.9 12.6 %collective-permute-start.3 = (bf16[2048,128]{1,0:T(8,128)(2,1)S(1)}, bf16[2048,128]{1,0:T(8,128)(2,1)S(1)}, u32[]{:S(2)}, u32[]{:S(2)}) collective-permute-start(bf16[2048,128]{1,0:T(8,128)(2,1)S(1)} %shard_map.46.cells_ref.rest_0_), channel_id=1, source_target_pairs={{1,0},{2,1},{3,2},{4,3},{5,4},{6,5},{7,6},{8,7},{9,8},{10,9},{11,1... | collective-permute-start | bytes 1572872 | tf_op jit(solution)/shard_map/ppermute | solution.py:70
  20.8 10.7 %collective-permute-start.2 = (bf16[2048,128]{1,0:T(8,128)(2,1)S(1)}, bf16[2048,128]{1,0:T(8,128)(2,1)S(1)}, u32[]{:S(2)}, u32[]{:S(2)}) collective-permute-start(bf16[2048,128]{1,0:T(8,128)(2,1)S(1)} %shard_map.46.cells_ref.rest_0_), channel_id=1, source_target_pairs={{0,1},{1,2},{2,3},{3,4},{4,5},{5,6},{6,7},{7,8},{8,9},{9,10},{10,1... | collective-permute-start | bytes 1572872 | tf_op jit(solution)/shard_map/ppermute | solution.py:69
  25.9 12.4 %collective-permute-start.9 = (bf16[2048,128]{1,0:T(8,128)(2,1)S(1)}, bf16[2048,128]{1,0:T(8,128)(2,1)S(1)}, u32[]{:S(2)}, u32[]{:S(2)}) collective-permute-start(bf16[2048,128]{1,0:T(8,128)(2,1)S(1)} %shard_map.49.cells_ref.rest_0_), channel_id=1, source_target_pairs={{1,0},{2,1},{3,2},{4,3},{5,4},{6,5},{7,6},{8,7},{9,8},{10,9},{11,1... | collective-permute-start | bytes 1572872 | tf_op jit(solution)/shard_map/ppermute | solution.py:70
  27.8 10.5 %collective-permute-start.8 = (bf16[2048,128]{1,0:T(8,128)(2,1)S(1)}, bf16[2048,128]{1,0:T(8,128)(2,1)S(1)}, u32[]{:S(2)}, u32[]{:S(2)}) collective-permute-start(bf16[2048,128]{1,0:T(8,128)(2,1)S(1)} %shard_map.49.cells_ref.rest_0_), channel_id=1, source_target_pairs={{0,1},{1,2},{2,3},{3,4},{4,5},{5,6},{6,7},{7,8},{8,9},{9,10},{10,1... | collective-permute-start | bytes 1572872 | tf_op jit(solution)/shard_map/ppermute | solution.py:69
  32.2 12.4 %collective-permute-start.5 = (bf16[2048,128]{1,0:T(8,128)(2,1)S(1)}, bf16[2048,128]{1,0:T(8,128)(2,1)S(1)}, u32[]{:S(2)}, u32[]{:S(2)}) collective-permute-start(bf16[2048,128]{1,0:T(8,128)(2,1)S(1)} %shard_map.47.cells_ref), channel_id=1, source_target_pairs={{1,0},{2,1},{3,2},{4,3},{5,4},{6,5},{7,6},{8,7},{9,8},{10,9},{11,1... | collective-permute-start | bytes 1572872 | tf_op jit(solution)/shard_map/ppermute | solution.py:70
  34.1 10.5 %collective-permute-start.4 = (bf16[2048,128]{1,0:T(8,128)(2,1)S(1)}, bf16[2048,128]{1,0:T(8,128)(2,1)S(1)}, u32[]{:S(2)}, u32[]{:S(2)}) collective-permute-start(bf16[2048,128]{1,0:T(8,128)(2,1)S(1)} %shard_map.47.cells_ref), channel_id=1, source_target_pairs={{0,1},{1,2},{2,3},{3,4},{4,5},{5,6},{6,7},{7,8},{8,9},{9,10},{10,1... | collective-permute-start | bytes 1572872 | tf_op jit(solution)/shard_map/ppermute | solution.py:69
  39.0 11.1 %collective-permute-start.11 = (bf16[2048,128]{1,0:T(8,128)(2,1)S(1)}, bf16[2048,128]{1,0:T(8,128)(2,1)S(1)}, u32[]{:S(2)}, u32[]{:S(2)}) collective-permute-start(bf16[2048,128]{1,0:T(8,128)(2,1)S(1)} %shard_map.50.cells_ref), channel_id=1, source_target_pairs={{1,0},{2,1},{3,2},{4,3},{5,4},{6,5},{7,6},{8,7},{9,8},{10,9},{11,1... | collective-permute-start | bytes 1572872 | tf_op jit(solution)/shard_map/ppermute | solution.py:70
  41.0 9.8 %collective-permute-start.10 = (bf16[2048,128]{1,0:T(8,128)(2,1)S(1)}, bf16[2048,128]{1,0:T(8,128)(2,1)S(1)}, u32[]{:S(2)}, u32[]{:S(2)}) collective-permute-start(bf16[2048,128]{1,0:T(8,128)(2,1)S(1)} %shard_map.50.cells_ref), channel_id=1, source_target_pairs={{0,1},{1,2},{2,3},{3,4},{4,5},{5,6},{6,7},{7,8},{8,9},{9,10},{10,1... | collective-permute-start | bytes 1572872 | tf_op jit(solution)/shard_map/ppermute | solution.py:69
  46.7 24.3 %all-to-all-start = ((bf16[32,8,1024]{2,0,1:T(8,128)(2,1)}), bf16[32,8,1024]{2,0,1:T(8,128)(2,1)S(1)}, u32[]{:S(2)}, u32[]{:S(2)}) async-start(bf16[32,8,1024]{2,0,1:T(8,128)(2,1)} %copy.8), calls=%async_computation | async-start | bytes 1048576 | tf_op jit(solution)/shard_map/all_to_all | solution.py:245
  122.3 7.7 %collective-permute-start.12 = (f32[5,128]{1,0:T(8,128)S(1)}, f32[5,128]{1,0:T(8,128)S(1)}, u32[]{:S(2)}, u32[]{:S(2)}) collective-permute-start(f32[5,128]{1,0:T(8,128)S(1)} %reduce_sum.19), channel_id=1, source_target_pairs={{0,32},{32,0},{1,33},{33,1},{2,34},{34,2},{3,35},{35,3},{4,36},{36... | collective-permute-start | bytes 7688 | tf_op jit(solution)/shard_map/ppermute | solution.py:234

commit v6 on v5

--- a/solution.py
+++ b/solution.py
@@ -9,8 +9,7 @@
 from jax.sharding import Mesh
 from jax.sharding import PartitionSpec as P
 
-BAND, DOM = ("y", "x_lo"), ("x_hi", "z", "core")
-NEAR = ("y", "x_lo", "core")
+BAND, DOM = ("y", "x_lo"), ("x_hi", "z_hi", "z_lo", "core")
 
 BANDS, PARTS = 8, 2
 
@@ -226,14 +225,26 @@
     return lax.all_to_all(pieces, axis, 0, 0, tiled=True)
 
 
+def scattered_sum(part, axis):
+    count = lax.axis_size(axis)
+    return jnp.sum(exchange(part.reshape(count, part.shape[0] // count, 128), axis), axis=0)
+
+
+def spread(part, axis):
+    count, rows = lax.axis_size(axis), part.shape[0]
+    return exchange(jnp.broadcast_to(part[None], (count, rows, 128)), axis).reshape(count * rows, 128)
+
+
+def shifted(part, axis, by):
+    count = lax.axis_size(axis)
+    return lax.ppermute(part, axis, [(i, (i + by) % count) for i in range(count)])
+
+
 def summed_everywhere(terms, scale):
-    near, far = lax.axis_size(NEAR), lax.axis_size("z")
-    rows = terms.shape[0] // near
-    part = jnp.sum(exchange(terms.reshape(near, rows, 128), NEAR), axis=0)
-    part = jnp.sum(exchange(part.reshape(far, rows // far, 128), "z"), axis=0)
-    part = (part + lax.ppermute(part, "x_hi", [(0, 1), (1, 0)])) * scale
-    part = exchange(jnp.broadcast_to(part[None], (far,) + part.shape), "z").reshape(rows, 128)
-    return exchange(jnp.broadcast_to(part[None], (near, rows, 128)), NEAR).reshape(terms.shape)
+    part = scattered_sum(scattered_sum(scattered_sum(terms, "core"), BAND), "z_lo")
+    part = (part + shifted(part, "z_hi", 2)) + (shifted(part, "z_hi", 1) + shifted(part, "z_hi", 3))
+    part = (part + shifted(part, "x_hi", 1)) * scale
+    return lax.all_gather(spread(spread(part, "z_lo"), BAND), "core", axis=0, tiled=True)
 
 
 def local(orbitals, potential):
@@ -252,7 +263,7 @@
 
 
 def solution(mesh):
-    named = Mesh(mesh.devices.reshape(4, 2, 2, 16, 2), ("y", "x_lo", "x_hi", "z", "core"))
+    named = Mesh(mesh.devices.reshape(4, 2, 2, 4, 4, 2), BAND + DOM)
     placed = (P(BAND, DOM, None, None), P(DOM, None, None))
     return jax.shard_map(
         local, mesh=named, in_specs=placed, out_specs=P(BAND, DOM, None, None), check_vma=False

time: 203 us -> 210 us (1.034)
  starting transfers between devices: 50 us -> 73.2 us
  blocking collectives: 100 us -> 78.7 us
  waiting for transfers between devices: 21.1 us -> 27.3 us
    all_to_all x4 -> x5, blocking collectives: 68.7 us -> 37.1 us  [exchange(): return lax.all_to_all(pieces, axis, 0, 0, tiled=True)]
    ppermute x1 -> x4, starting transfers between devices: 6.75 us -> 29.9 us  [shifted(): lax.ppermute(part, axis, [(i, (i + by) % count) for i in range(count)])]
    all_gather x0 -> x1, blocking collectives: none -> 9.58 us  [summed_everywhere(): lax.all_gather(spread(spread(part, 'z_lo'), BAND), 'core', axis=0, tiled=...]
    ppermute x1 -> x4, waiting for transfers between devices: 0.98 us -> 7.2 us  [shifted(): lax.ppermute(part, axis, [(i, (i + by) % count) for i in range(count)])]
  transfers between devices with their start and end apart: 14 -> 17, of which waited for: 4 -> 5; matrix products, arithmetic and copies ran while one was open for 1% -> 1% of each run, Pallas kernels for 2% -> 2%
where the time goes in v6:
time: 210 us; the launch traced here: 209 us
  blocking collectives  78.7 us (37%)
  starting transfers between devices  73.2 us (35%)
  waiting for transfers between devices  27.3 us (13%)
  Pallas kernels  24.3 us (12%)
  local copies, waits for them, and re-layouts  5.04 us (2%)
    all_to_all x5, blocking collectives, exchange(): return lax.all_to_all(pieces, axis, 0, 0, tiled=True)  37.1 us
    ppermute x4, starting transfers between devices, shifted(): lax.ppermute(part, axis, [(i, (i + by) % count) for i in range(count)])  29.9 us
    ppermute x6, starting transfers between devices, halo(): left = lax.ppermute(cells, DOM, [(i, i + 1) for i in range(count - 1)])  20.9 us
    pallas_call x1, Pallas kernels, rotated_by(): pl.pallas_call(rotation_kernel, out_shape=jax.ShapeDtypeStruct(field.shap...  19.2 us
    all_to_all x1, waiting for transfers between devices, local(): lax.all_to_all(part.reshape(-1, cells_dev), BAND, 1, 0, tiled=True)  19 us
    ppermute x6, starting transfers between devices, halo(): right = lax.ppermute(cells, DOM, [(i + 1, i) for i in range(count - 1)])  18.9 us
    all_to_all x1, blocking collectives, local(): result = lax.all_to_all(turned, BAND, 0, 1, tiled=True)  17.9 us
    all_to_all x1, blocking collectives, local(): lax.all_to_all(part.reshape(-1, cells_dev), BAND, 1, 0, tiled=True)  14.2 us
  transfers between devices with their start and end apart: 17, of which 5 were waited for; matrix products, arithmetic and copies ran while one was open for 1% of the time, Pallas kernels for 2%

profile of v6, /device:TPU:1, one launch (start us, length us, event | category | flops | bytes accessed | tf_op | source)
XLA Modules:
  0.0 209.0 jit_solution(4243062504894453393)
XLA Ops:
  0.0 1.3 fusion
  1.3 8.8 %collective-permute-start.1 = (bf16[2048,128]{1,0:T(8,128)(2,1)S(1)}, bf16[2048,128]{1,0:T(8,128)(2,1)S(1)}, u32[]{:S(2)}, u32[]{:S(2)}) collective-permute-start(bf16[2048,128]{1,0:T(8,128)(2,1)S(1)} %bitcast.18), channel_id=1, source_target_pairs={{1,0},{2,1},{3,2},{4,3},{5,4},{6,5},{7,6},{8,7},{9,8},{10,9},{11,1... | collective-permute-start | bytes 1572872 | tf_op jit(solution)/shard_map/ppermute | solution.py:69
  10.1 1.9 collective-permute-start
  12.0 2.4 %collective-permute-start.7 = (bf16[2048,128]{1,0:T(8,128)(2,1)S(1)}, bf16[2048,128]{1,0:T(8,128)(2,1)S(1)}, u32[]{:S(2)}, u32[]{:S(2)}) collective-permute-start(bf16[2048,128]{1,0:T(8,128)(2,1)S(1)} %bitcast.14), channel_id=1, source_target_pairs={{1,0},{2,1},{3,2},{4,3},{5,4},{6,5},{7,6},{8,7},{9,8},{10,9},{11,1... | collective-permute-start | bytes 1572872 | tf_op jit(solution)/shard_map/ppermute | solution.py:69
  14.5 3.1 %collective-permute-start.6 = (bf16[2048,128]{1,0:T(8,128)(2,1)S(1)}, bf16[2048,128]{1,0:T(8,128)(2,1)S(1)}, u32[]{:S(2)}, u32[]{:S(2)}) collective-permute-start(bf16[2048,128]{1,0:T(8,128)(2,1)S(1)} %bitcast.15), channel_id=1, source_target_pairs={{0,1},{1,2},{2,3},{3,4},{4,5},{5,6},{6,7},{7,8},{8,9},{9,10},{10,1... | collective-permute-start | bytes 1572872 | tf_op jit(solution)/shard_map/ppermute | solution.py:68
  17.6 0.0 collective-permute-done.1.right_ref
  17.6 0.5 collective-permute-done.left_ref
  18.1 0.7 shard_map.46.cells_ref.rest_0_
  18.9 1.9 collective-permute-start.3
  20.8 4.4 %collective-permute-start.2 = (bf16[2048,128]{1,0:T(8,128)(2,1)S(1)}, bf16[2048,128]{1,0:T(8,128)(2,1)S(1)}, u32[]{:S(2)}, u32[]{:S(2)}) collective-permute-start(bf16[2048,128]{1,0:T(8,128)(2,1)S(1)} %shard_map.46.cells_ref.rest_0_), channel_id=1, source_target_pairs={{0,1},{1,2},{2,3},{3,4},{4,5},{5,6},{6,7},{7,8},{8,9},{9,10},{10,1... | collective-permute-start | bytes 1572872 | tf_op jit(solution)/shard_map/ppermute | solution.py:68
  25.2 0.0 collective-permute-done.7.right_ref
  25.2 0.7 shard_map.49.cells_ref.rest_0_
  25.9 1.9 collective-permute-start.9
  27.8 3.6 %collective-permute-start.8 = (bf16[2048,128]{1,0:T(8,128)(2,1)S(1)}, bf16[2048,128]{1,0:T(8,128)(2,1)S(1)}, u32[]{:S(2)}, u32[]{:S(2)}) collective-permute-start(bf16[2048,128]{1,0:T(8,128)(2,1)S(1)} %shard_map.49.cells_ref.rest_0_), channel_id=1, source_target_pairs={{0,1},{1,2},{2,3},{3,4},{4,5},{5,6},{6,7},{7,8},{8,9},{9,10},{10,1... | collective-permute-start | bytes 1572872 | tf_op jit(solution)/shard_map/ppermute | solution.py:68
  31.5 0.0 collective-permute-done.3.right_ref
  31.5 0.7 shard_map.47.cells_ref
  32.2 1.9 collective-permute-start.5
  34.1 4.2 %collective-permute-start.4 = (bf16[2048,128]{1,0:T(8,128)(2,1)S(1)}, bf16[2048,128]{1,0:T(8,128)(2,1)S(1)}, u32[]{:S(2)}, u32[]{:S(2)}) collective-permute-start(bf16[2048,128]{1,0:T(8,128)(2,1)S(1)} %shard_map.47.cells_ref), channel_id=1, source_target_pairs={{0,1},{1,2},{2,3},{3,4},{4,5},{5,6},{6,7},{7,8},{8,9},{9,10},{10,1... | collective-permute-start | bytes 1572872 | tf_op jit(solution)/shard_map/ppermute | solution.py:68
  38.3 0.7 shard_map.50.cells_ref
  39.0 1.9 collective-permute-start.11
  41.0 3.6 %collective-permute-start.10 = (bf16[2048,128]{1,0:T(8,128)(2,1)S(1)}, bf16[2048,128]{1,0:T(8,128)(2,1)S(1)}, u32[]{:S(2)}, u32[]{:S(2)}) collective-permute-start(bf16[2048,128]{1,0:T(8,128)(2,1)S(1)} %shard_map.50.cells_ref), channel_id=1, source_target_pairs={{0,1},{1,2},{2,3},{3,4},{4,5},{5,6},{6,7},{7,8},{8,9},{9,10},{10,1... | collective-permute-start | bytes 1572872 | tf_op jit(solution)/shard_map/ppermute | solution.py:68
  44.6 0.7 shard_map.48
  45.4 0.2 all_to_all.55
  45.6 1.1 copy.11
  46.7 3.5 %all-to-all-start = ((bf16[32,8,1024]{2,0,1:T(8,128)(2,1)}), bf16[32,8,1024]{2,0,1:T(8,128)(2,1)S(1)}, u32[]{:S(2)}, u32[]{:S(2)}) async-start(bf16[32,8,1024]{2,0,1:T(8,128)(2,1)} %copy.11), calls=%async_computation | async-start | bytes 1048576 | tf_op jit(solution)/shard_map/all_to_all | solution.py:256
  50.2 0.5 collective-permute-done.10.left_ref
  50.7 0.7 shard_map.51
  51.4 0.2 all_to_all.59
  51.7 0.3 copy.12
  52.0 19.0 %all-to-all-done = bf16[32,8,1024]{2,0,1:T(8,128)(2,1)S(1)} async-done(((bf16[32,8,1024]{2,0,1:T(8,128)(2,1)}), bf16[32,8,1024]{2,0,1:T(8,128)(2,1)S(1)}, u32[]{:S(2)}, u32[]{:S(2)}) %all-to-all-start) | async-done | bytes 524320 | tf_op jit(solution)/shard_map/all_to_all | solution.py:256
  71.0 14.2 %all_to_all.79 = bf16[32,8,1024]{2,0,1:T(8,128)(2,1)S(1)} all-to-all(bf16[32,8,1024]{2,0,1:T(8,128)(2,1)S(1)} %copy.12), channel_id=1, replica_groups=mesh['y'=4,'x_lo'=2,'x_hi'=2,'z_hi'=4,'z_lo'=4,'core'=2] {'y','x_lo'}, dimensions={1} | all-to-all | bytes 1048576 | tf_op jit(solution)/shard_map/all_to_all | solution.py:256
  85.2 0.9 shard_map.52
  86.1 4.4 %all_to_all.80 = f32[2,640,128]{2,1,0:T(8,128)S(1)} all-to-all(f32[2,640,128]{2,1,0:T(8,128)S(1)} %bitcast.31), channel_id=1, replica_groups=mesh['y'=4,'x_lo'=2,'x_hi'=2,'z_hi'=4,'z_lo'=4,'core'=2] {'core'}, dimensions={0} | all-to-all | bytes 1310720 | tf_op jit(solution)/shard_map/all_to_all | solution.py:225
  90.5 9.9 %all_to_all.81 = f32[8,80,128]{2,1,0:T(8,128)S(1)} all-to-all(f32[8,80,128]{2,1,0:T(8,128)S(1)} %bitcast.33), channel_id=1, replica_groups=mesh['y'=4,'x_lo'=2,'x_hi'=2,'z_hi'=4,'z_lo'=4,'core'=2] {'y','x_lo'}, dimensions={0} | all-to-all | bytes 655360 | tf_op jit(solution)/shard_map/all_to_all | solution.py:225
  100.5 6.9 %all_to_all.82 = f32[4,20,128]{2,1,0:T(8,128)S(1)} all-to-all(f32[4,20,128]{2,1,0:T(8,128)S(1)} %reshape.42), channel_id=1, replica_groups=mesh['y'=4,'x_lo'=2,'x_hi'=2,'z_hi'=4,'z_lo'=4,'core'=2] {'z_lo'}, dimensions={0} | all-to-all | bytes 81920 | tf_op jit(solution)/shard_map/all_to_all | solution.py:225
  107.4 12.1 %collective-permute-start.14 = (f32[20,128]{1,0:T(8,128)S(1)}, f32[20,128]{1,0:T(8,128)S(1)}, u32[]{:S(2)}, u32[]{:S(2)}) collective-permute-start(f32[20,128]{1,0:T(8,128)S(1)} %reduce_sum.29), channel_id=1, source_target_pairs={{0,24},{8,0},{16,8},{24,16},{1,25},{9,1},{17,9},{25,17},{2,26},{10... | collective-permute-start | bytes 30728 | tf_op jit(solution)/shard_map/ppermute | solution.py:240
  119.5 1.9 collective-permute-start.13
  121.4 7.0 %collective-permute-start.12 = (f32[20,128]{1,0:T(8,128)S(1)}, f32[20,128]{1,0:T(8,128)S(1)}, u32[]{:S(2)}, u32[]{:S(2)}) collective-permute-start(f32[20,128]{1,0:T(8,128)S(1)} %reduce_sum.29), channel_id=1, source_target_pairs={{0,16},{8,24},{16,0},{24,8},{1,17},{9,25},{17,1},{25,9},{2,18},{10... | collective-permute-start | bytes 30728 | tf_op jit(solution)/shard_map/ppermute | solution.py:240
  128.4 6.1 %collective-permute-done.12 = f32[20,128]{1,0:T(8,128)S(1)} collective-permute-done((f32[20,128]{1,0:T(8,128)S(1)}, f32[20,128]{1,0:T(8,128)S(1)}, u32[]{:S(2)}, u32[]{:S(2)}) %collective-permute-start.12) | collective-permute-done | bytes 10272 | tf_op jit(solution)/shard_map/ppermute | solution.py:240
  134.6 8.9 %collective-permute-start.15 = (f32[20,128]{1,0:T(8,128)S(1)}, f32[20,128]{1,0:T(8,128)S(1)}, u32[]{:S(2)}, u32[]{:S(2)}) collective-permute-start(f32[20,128]{1,0:T(8,128)S(1)} %add_add_fusion), channel_id=1, source_target_pairs={{0,32},{32,0},{1,33},{33,1},{2,34},{34,2},{3,35},{35,3},{4,36},{36... | collective-permute-start | bytes 30728 | tf_op jit(solution)/shard_map/ppermute | solution.py:240
  143.5 1.1 collective-permute-done.15
  144.6 6.9 %all_to_all.83 = f32[4,20,128]{2,1,0:T(8,128)S(1)} all-to-all(f32[4,20,128]{2,1,0:T(8,128)S(1)} %broadcast_in_dim.6), channel_id=1, replica_groups=mesh['y'=4,'x_lo'=2,'x_hi'=2,'z_hi'=4,'z_lo'=4,'core'=2] {'z_lo'}, dimensions={0} | all-to-all | bytes 81920 | tf_op jit(solution)/shard_map/all_to_all | solution.py:225
  151.5 9.0 %all_to_all.84 = f32[8,80,128]{2,1,0:T(8,128)S(1)} all-to-all(f32[8,80,128]{2,1,0:T(8,128)S(1)} %broadcast_in_dim.15), channel_id=1, replica_groups=mesh['y'=4,'x_lo'=2,'x_hi'=2,'z_hi'=4,'z_lo'=4,'core'=2] {'y','x_lo'}, dimensions={0} | all-to-all | bytes 655360 | tf_op jit(solution)/shard_map/all_to_all | solution.py:225
  160.5 9.6 %all_gather.3.tiles_ref = f32[1280,128]{1,0:T(8,128)S(1)} all-gather(f32[640,128]{1,0:T(8,128)S(1)} %bitcast.34), channel_id=1, replica_groups=mesh['y'=4,'x_lo'=2,'x_hi'=2,'z_hi'=4,'z_lo'=4,'core'=2] {'core'}, dimensions={0}, use_global_device_ids=true | all-gather | bytes 983040 | tf_op jit(solution)/shard_map/all_gather | solution.py:247
  170.1 19.2 %shard_map.53 = bf16[512,1024]{1,0:T(8,128)(2,1)S(1)} custom-call(f32[1280,128]{1,0:T(8,128)S(1)} %all_gather.3.tiles_ref, bf16[512,1024]{1,0:T(8,128)(2,1)S(1)} %get-tuple-element.8.field_ref), custom_call_target="tpu_custom_call" | custom-call | tf_op jit(solution)/shard_map/pallas_call | solution.py:209
  189.3 17.9 %all_to_all.85 = bf16[8,64,1024]{2,1,0:T(8,128)(2,1)S(1)} all-to-all(bf16[8,64,1024]{2,1,0:T(8,128)(2,1)S(1)} %bitcast.22), channel_id=1, replica_groups=mesh['y'=4,'x_lo'=2,'x_hi'=2,'z_hi'=4,'z_lo'=4,'core'=2] {'y','x_lo'}, dimensions={0} | all-to-all | bytes 2097152 | tf_op jit(solution)/shard_map/all_to_all | solution.py:261
  207.2 0.6 copy.13
  207.7 1.3 reshape.44
  (24 shorter events, 0.2 us)
Async XLA Ops:
  0.0 18.1 %copy-start = (bf16[128,384]{1,0:T(8,128)(2,1)S(1)}, bf16[128,384]{1,0:T(8,128)(2,1)}, u32[]{:S(2)}) copy-start(bf16[128,384]{1,0:T(8,128)(2,1)} %constant.8.clone.across_ref) | copy-start | bytes 294916
  0.0 18.1 %copy-start.2 = (bf16[128,128]{1,0:T(8,128)(2,1)S(1)}, bf16[128,128]{1,0:T(8,128)(2,1)}, u32[]{:S(2)}) copy-start(bf16[128,128]{1,0:T(8,128)(2,1)} %constant.9.clone.along_ref) | copy-start | bytes 98308
  0.0 18.1 %copy-start.1 = (f32[2,32,128]{2,1,0:T(8,128)S(1)}, f32[2,32,128]{2,1,0:T(8,128)}, u32[]{:S(2)}) copy-start(f32[2,32,128]{2,1,0:T(8,128)} %param.5) | copy-start | bytes 98308
  1.3 16.3 %collective-permute-start.1 = (bf16[2048,128]{1,0:T(8,128)(2,1)S(1)}, bf16[2048,128]{1,0:T(8,128)(2,1)S(1)}, u32[]{:S(2)}, u32[]{:S(2)}) collective-permute-start(bf16[2048,128]{1,0:T(8,128)(2,1)S(1)} %bitcast.18), channel_id=1, source_target_pairs={{1,0},{2,1},{3,2},{4,3},{5,4},{6,5},{7,6},{8,7},{9,8},{10,9},{11,1... | collective-permute-start | bytes 1572872 | tf_op jit(solution)/shard_map/ppermute | solution.py:69
  10.1 8.0 %collective-permute-start = (bf16[2048,128]{1,0:T(8,128)(2,1)S(1)}, bf16[2048,128]{1,0:T(8,128)(2,1)S(1)}, u32[]{:S(2)}, u32[]{:S(2)}) collective-permute-start(bf16[2048,128]{1,0:T(8,128)(2,1)S(1)} %bitcast.19), channel_id=1, source_target_pairs={{0,1},{1,2},{2,3},{3,4},{4,5},{5,6},{6,7},{7,8},{8,9},{9,10},{10,1... | collective-permute-start | bytes 1572872 | tf_op jit(solution)/shard_map/ppermute | solution.py:68
  12.0 13.2 %collective-permute-start.7 = (bf16[2048,128]{1,0:T(8,128)(2,1)S(1)}, bf16[2048,128]{1,0:T(8,128)(2,1)S(1)}, u32[]{:S(2)}, u32[]{:S(2)}) collective-permute-start(bf16[2048,128]{1,0:T(8,128)(2,1)S(1)} %bitcast.14), channel_id=1, source_target_pairs={{1,0},{2,1},{3,2},{4,3},{5,4},{6,5},{7,6},{8,7},{9,8},{10,9},{11,1... | collective-permute-start | bytes 1572872 | tf_op jit(solution)/shard_map/ppermute | solution.py:69
  14.5 10.7 %collective-permute-start.6 = (bf16[2048,128]{1,0:T(8,128)(2,1)S(1)}, bf16[2048,128]{1,0:T(8,128)(2,1)S(1)}, u32[]{:S(2)}, u32[]{:S(2)}) collective-permute-start(bf16[2048,128]{1,0:T(8,128)(2,1)S(1)} %bitcast.15), channel_id=1, source_target_pairs={{0,1},{1,2},{2,3},{3,4},{4,5},{5,6},{6,7},{7,8},{8,9},{9,10},{10,1... | collective-permute-start | bytes 1572872 | tf_op jit(solution)/shard_map/ppermute | solution.py:68
  18.9 12.6 %collective-permute-start.3 = (bf16[2048,128]{1,0:T(8,128)(2,1)S(1)}, bf16[2048,128]{1,0:T(8,128)(2,1)S(1)}, u32[]{:S(2)}, u32[]{:S(2)}) collective-permute-start(bf16[2048,128]{1,0:T(8,128)(2,1)S(1)} %shard_map.46.cells_ref.rest_0_), channel_id=1, source_target_pairs={{1,0},{2,1},{3,2},{4,3},{5,4},{6,5},{7,6},{8,7},{9,8},{10,9},{11,1... | collective-permute-start | bytes 1572872 | tf_op jit(solution)/shard_map/ppermute | solution.py:69
  20.8 10.7 %collective-permute-start.2 = (bf16[2048,128]{1,0:T(8,128)(2,1)S(1)}, bf16[2048,128]{1,0:T(8,128)(2,1)S(1)}, u32[]{:S(2)}, u32[]{:S(2)}) collective-permute-start(bf16[2048,128]{1,0:T(8,128)(2,1)S(1)} %shard_map.46.cells_ref.rest_0_), channel_id=1, source_target_pairs={{0,1},{1,2},{2,3},{3,4},{4,5},{5,6},{6,7},{7,8},{8,9},{9,10},{10,1... | collective-permute-start | bytes 1572872 | tf_op jit(solution)/shard_map/ppermute | solution.py:68
  25.9 12.4 %collective-permute-start.9 = (bf16[2048,128]{1,0:T(8,128)(2,1)S(1)}, bf16[2048,128]{1,0:T(8,128)(2,1)S(1)}, u32[]{:S(2)}, u32[]{:S(2)}) collective-permute-start(bf16[2048,128]{1,0:T(8,128)(2,1)S(1)} %shard_map.49.cells_ref.rest_0_), channel_id=1, source_target_pairs={{1,0},{2,1},{3,2},{4,3},{5,4},{6,5},{7,6},{8,7},{9,8},{10,9},{11,1... | collective-permute-start | bytes 1572872 | tf_op jit(solution)/shard_map/ppermute | solution.py:69
  27.8 10.5 %collective-permute-start.8 = (bf16[2048,128]{1,0:T(8,128)(2,1)S(1)}, bf16[2048,128]{1,0:T(8,128)(2,1)S(1)}, u32[]{:S(2)}, u32[]{:S(2)}) collective-permute-start(bf16[2048,128]{1,0:T(8,128)(2,1)S(1)} %shard_map.49.cells_ref.rest_0_), channel_id=1, source_target_pairs={{0,1},{1,2},{2,3},{3,4},{4,5},{5,6},{6,7},{7,8},{8,9},{9,10},{10,1... | collective-permute-start | bytes 1572872 | tf_op jit(solution)/shard_map/ppermute | solution.py:68
  32.2 12.4 %collective-permute-start.5 = (bf16[2048,128]{1,0:T(8,128)(2,1)S(1)}, bf16[2048,128]{1,0:T(8,128)(2,1)S(1)}, u32[]{:S(2)}, u32[]{:S(2)}) collective-permute-start(bf16[2048,128]{1,0:T(8,128)(2,1)S(1)} %shard_map.47.cells_ref), channel_id=1, source_target_pairs={{1,0},{2,1},{3,2},{4,3},{5,4},{6,5},{7,6},{8,7},{9,8},{10,9},{11,1... | collective-permute-start | bytes 1572872 | tf_op jit(solution)/shard_map/ppermute | solution.py:69
  34.1 10.5 %collective-permute-start.4 = (bf16[2048,128]{1,0:T(8,128)(2,1)S(1)}, bf16[2048,128]{1,0:T(8,128)(2,1)S(1)}, u32[]{:S(2)}, u32[]{:S(2)}) collective-permute-start(bf16[2048,128]{1,0:T(8,128)(2,1)S(1)} %shard_map.47.cells_ref), channel_id=1, source_target_pairs={{0,1},{1,2},{2,3},{3,4},{4,5},{5,6},{6,7},{7,8},{8,9},{9,10},{10,1... | collective-permute-start | bytes 1572872 | tf_op jit(solution)/shard_map/ppermute | solution.py:68
  39.0 11.1 %collective-permute-start.11 = (bf16[2048,128]{1,0:T(8,128)(2,1)S(1)}, bf16[2048,128]{1,0:T(8,128)(2,1)S(1)}, u32[]{:S(2)}, u32[]{:S(2)}) collective-permute-start(bf16[2048,128]{1,0:T(8,128)(2,1)S(1)} %shard_map.50.cells_ref), channel_id=1, source_target_pairs={{1,0},{2,1},{3,2},{4,3},{5,4},{6,5},{7,6},{8,7},{9,8},{10,9},{11,1... | collective-permute-start | bytes 1572872 | tf_op jit(solution)/shard_map/ppermute | solution.py:69
  41.0 9.8 %collective-permute-start.10 = (bf16[2048,128]{1,0:T(8,128)(2,1)S(1)}, bf16[2048,128]{1,0:T(8,128)(2,1)S(1)}, u32[]{:S(2)}, u32[]{:S(2)}) collective-permute-start(bf16[2048,128]{1,0:T(8,128)(2,1)S(1)} %shard_map.50.cells_ref), channel_id=1, source_target_pairs={{0,1},{1,2},{2,3},{3,4},{4,5},{5,6},{6,7},{7,8},{8,9},{9,10},{10,1... | collective-permute-start | bytes 1572872 | tf_op jit(solution)/shard_map/ppermute | solution.py:68
  46.7 24.3 %all-to-all-start = ((bf16[32,8,1024]{2,0,1:T(8,128)(2,1)}), bf16[32,8,1024]{2,0,1:T(8,128)(2,1)S(1)}, u32[]{:S(2)}, u32[]{:S(2)}) async-start(bf16[32,8,1024]{2,0,1:T(8,128)(2,1)} %copy.11), calls=%async_computation | async-start | bytes 1048576 | tf_op jit(solution)/shard_map/all_to_all | solution.py:256
  107.4 21.0 %collective-permute-start.14 = (f32[20,128]{1,0:T(8,128)S(1)}, f32[20,128]{1,0:T(8,128)S(1)}, u32[]{:S(2)}, u32[]{:S(2)}) collective-permute-start(f32[20,128]{1,0:T(8,128)S(1)} %reduce_sum.29), channel_id=1, source_target_pairs={{0,24},{8,0},{16,8},{24,16},{1,25},{9,1},{17,9},{25,17},{2,26},{10... | collective-permute-start | bytes 30728 | tf_op jit(solution)/shard_map/ppermute | solution.py:240
  119.5 8.9 %collective-permute-start.13 = (f32[20,128]{1,0:T(8,128)S(1)}, f32[20,128]{1,0:T(8,128)S(1)}, u32[]{:S(2)}, u32[]{:S(2)}) collective-permute-start(f32[20,128]{1,0:T(8,128)S(1)} %reduce_sum.29), channel_id=1, source_target_pairs={{0,8},{8,16},{16,24},{24,0},{1,9},{9,17},{17,25},{25,1},{2,10},{10... | collective-permute-start | bytes 30728 | tf_op jit(solution)/shard_map/ppermute | solution.py:240
  121.4 13.2 %collective-permute-start.12 = (f32[20,128]{1,0:T(8,128)S(1)}, f32[20,128]{1,0:T(8,128)S(1)}, u32[]{:S(2)}, u32[]{:S(2)}) collective-permute-start(f32[20,128]{1,0:T(8,128)S(1)} %reduce_sum.29), channel_id=1, source_target_pairs={{0,16},{8,24},{16,0},{24,8},{1,17},{9,25},{17,1},{25,9},{2,18},{10... | collective-permute-start | bytes 30728 | tf_op jit(solution)/shard_map/ppermute | solution.py:240
  134.6 10.0 %collective-permute-start.15 = (f32[20,128]{1,0:T(8,128)S(1)}, f32[20,128]{1,0:T(8,128)S(1)}, u32[]{:S(2)}, u32[]{:S(2)}) collective-permute-start(f32[20,128]{1,0:T(8,128)S(1)} %add_add_fusion), channel_id=1, source_target_pairs={{0,32},{32,0},{1,33},{33,1},{2,34},{34,2},{3,35},{35,3},{4,36},{36... | collective-permute-start | bytes 30728 | tf_op jit(solution)/shard_map/ppermute | solution.py:240

commit v7 on v5

--- a/solution.py
+++ b/solution.py
@@ -10,7 +10,7 @@
 from jax.sharding import PartitionSpec as P
 
 BAND, DOM = ("y", "x_lo"), ("x_hi", "z", "core")
-NEAR = ("y", "x_lo", "core")
+NEAR = ("core", "y", "x_lo")
 
 BANDS, PARTS = 8, 2
 
@@ -233,7 +233,9 @@
     part = jnp.sum(exchange(part.reshape(far, rows // far, 128), "z"), axis=0)
     part = (part + lax.ppermute(part, "x_hi", [(0, 1), (1, 0)])) * scale
     part = exchange(jnp.broadcast_to(part[None], (far,) + part.shape), "z").reshape(rows, 128)
-    return exchange(jnp.broadcast_to(part[None], (near, rows, 128)), NEAR).reshape(terms.shape)
+    bands = lax.axis_size(BAND)
+    part = exchange(jnp.broadcast_to(part[None], (bands, rows, 128)), BAND).reshape(-1, 128)
+    return lax.all_gather(part, "core", axis=0, tiled=True)
 
 
 def local(orbitals, potential):

time: 203 us -> 200 us (0.985)
    all_to_all x4, blocking collectives: 68.7 us -> 60 us  [exchange(): return lax.all_to_all(pieces, axis, 0, 0, tiled=True)]
    all_gather x0 -> x1, blocking collectives: none -> 6.68 us  [summed_everywhere(): return lax.all_gather(part, 'core', axis=0, tiled=True)]
where the time goes in v7:
time: 200 us; the launch traced here: 199 us
  blocking collectives  98.7 us (49%)
  starting transfers between devices  49.9 us (25%)
  Pallas kernels  24.3 us (12%)
  waiting for transfers between devices  21.1 us (11%)
  local copies, waits for them, and re-layouts  5.04 us (3%)
    all_to_all x4, blocking collectives, exchange(): return lax.all_to_all(pieces, axis, 0, 0, tiled=True)  60 us
    ppermute x6, starting transfers between devices, halo(): left = lax.ppermute(cells, DOM, [(i, i + 1) for i in range(count - 1)])  20.9 us
    pallas_call x1, Pallas kernels, rotated_by(): pl.pallas_call(rotation_kernel, out_shape=jax.ShapeDtypeStruct(field.shap...  19.2 us
    all_to_all x1, waiting for transfers between devices, local(): lax.all_to_all(part.reshape(-1, cells_dev), BAND, 1, 0, tiled=True)  19 us
    ppermute x6, starting transfers between devices, halo(): right = lax.ppermute(cells, DOM, [(i + 1, i) for i in range(count - 1)])  18.9 us
    all_to_all x1, blocking collectives, local(): result = lax.all_to_all(turned, BAND, 0, 1, tiled=True)  17.9 us
    all_to_all x1, blocking collectives, local(): lax.all_to_all(part.reshape(-1, cells_dev), BAND, 1, 0, tiled=True)  14.2 us
    all_gather x1, blocking collectives, summed_everywhere(): return lax.all_gather(part, 'core', axis=0, tiled=True)  6.68 us
  transfers between devices with their start and end apart: 14, of which 4 were waited for; matrix products, arithmetic and copies ran while one was open for 1% of the time, Pallas kernels for 2%

profile of v7, /device:TPU:1, one launch (start us, length us, event | category | flops | bytes accessed | tf_op | source)
XLA Modules:
  0.0 199.5 jit_solution(1399737068073646606)
XLA Ops:
  0.0 1.3 fusion
  1.3 8.8 %collective-permute-start.1 = (bf16[2048,128]{1,0:T(8,128)(2,1)S(1)}, bf16[2048,128]{1,0:T(8,128)(2,1)S(1)}, u32[]{:S(2)}, u32[]{:S(2)}) collective-permute-start(bf16[2048,128]{1,0:T(8,128)(2,1)S(1)} %bitcast.17), channel_id=1, source_target_pairs={{1,0},{2,1},{3,2},{4,3},{5,4},{6,5},{7,6},{8,7},{9,8},{10,9},{11,1... | collective-permute-start | bytes 1572872 | tf_op jit(solution)/shard_map/ppermute | solution.py:70
  10.1 1.9 collective-permute-start
  12.0 2.4 %collective-permute-start.7 = (bf16[2048,128]{1,0:T(8,128)(2,1)S(1)}, bf16[2048,128]{1,0:T(8,128)(2,1)S(1)}, u32[]{:S(2)}, u32[]{:S(2)}) collective-permute-start(bf16[2048,128]{1,0:T(8,128)(2,1)S(1)} %bitcast.13), channel_id=1, source_target_pairs={{1,0},{2,1},{3,2},{4,3},{5,4},{6,5},{7,6},{8,7},{9,8},{10,9},{11,1... | collective-permute-start | bytes 1572872 | tf_op jit(solution)/shard_map/ppermute | solution.py:70
  14.5 3.1 %collective-permute-start.6 = (bf16[2048,128]{1,0:T(8,128)(2,1)S(1)}, bf16[2048,128]{1,0:T(8,128)(2,1)S(1)}, u32[]{:S(2)}, u32[]{:S(2)}) collective-permute-start(bf16[2048,128]{1,0:T(8,128)(2,1)S(1)} %bitcast.14), channel_id=1, source_target_pairs={{0,1},{1,2},{2,3},{3,4},{4,5},{5,6},{6,7},{7,8},{8,9},{9,10},{10,1... | collective-permute-start | bytes 1572872 | tf_op jit(solution)/shard_map/ppermute | solution.py:69
  17.6 0.0 collective-permute-done.1.right_ref
  17.6 0.5 collective-permute-done.left_ref
  18.1 0.7 shard_map.46.cells_ref.rest_0_
  18.9 1.9 collective-permute-start.3
  20.8 4.4 %collective-permute-start.2 = (bf16[2048,128]{1,0:T(8,128)(2,1)S(1)}, bf16[2048,128]{1,0:T(8,128)(2,1)S(1)}, u32[]{:S(2)}, u32[]{:S(2)}) collective-permute-start(bf16[2048,128]{1,0:T(8,128)(2,1)S(1)} %shard_map.46.cells_ref.rest_0_), channel_id=1, source_target_pairs={{0,1},{1,2},{2,3},{3,4},{4,5},{5,6},{6,7},{7,8},{8,9},{9,10},{10,1... | collective-permute-start | bytes 1572872 | tf_op jit(solution)/shard_map/ppermute | solution.py:69
  25.2 0.0 collective-permute-done.7.right_ref
  25.2 0.0 collective-permute-done.6.left_ref
  25.2 0.7 shard_map.49.cells_ref.rest_0_
  25.9 1.9 collective-permute-start.9
  27.8 3.6 %collective-permute-start.8 = (bf16[2048,128]{1,0:T(8,128)(2,1)S(1)}, bf16[2048,128]{1,0:T(8,128)(2,1)S(1)}, u32[]{:S(2)}, u32[]{:S(2)}) collective-permute-start(bf16[2048,128]{1,0:T(8,128)(2,1)S(1)} %shard_map.49.cells_ref.rest_0_), channel_id=1, source_target_pairs={{0,1},{1,2},{2,3},{3,4},{4,5},{5,6},{6,7},{7,8},{8,9},{9,10},{10,1... | collective-permute-start | bytes 1572872 | tf_op jit(solution)/shard_map/ppermute | solution.py:69
  31.5 0.0 collective-permute-done.3.right_ref
  31.5 0.0 collective-permute-done.2.left_ref
  31.5 0.7 shard_map.47.cells_ref
  32.2 1.9 collective-permute-start.5
  34.1 4.2 %collective-permute-start.4 = (bf16[2048,128]{1,0:T(8,128)(2,1)S(1)}, bf16[2048,128]{1,0:T(8,128)(2,1)S(1)}, u32[]{:S(2)}, u32[]{:S(2)}) collective-permute-start(bf16[2048,128]{1,0:T(8,128)(2,1)S(1)} %shard_map.47.cells_ref), channel_id=1, source_target_pairs={{0,1},{1,2},{2,3},{3,4},{4,5},{5,6},{6,7},{7,8},{8,9},{9,10},{10,1... | collective-permute-start | bytes 1572872 | tf_op jit(solution)/shard_map/ppermute | solution.py:69
  38.3 0.0 collective-permute-done.9.right_ref
  38.3 0.7 shard_map.50.cells_ref
  39.0 1.9 collective-permute-start.11
  41.0 3.6 %collective-permute-start.10 = (bf16[2048,128]{1,0:T(8,128)(2,1)S(1)}, bf16[2048,128]{1,0:T(8,128)(2,1)S(1)}, u32[]{:S(2)}, u32[]{:S(2)}) collective-permute-start(bf16[2048,128]{1,0:T(8,128)(2,1)S(1)} %shard_map.50.cells_ref), channel_id=1, source_target_pairs={{0,1},{1,2},{2,3},{3,4},{4,5},{5,6},{6,7},{7,8},{8,9},{9,10},{10,1... | collective-permute-start | bytes 1572872 | tf_op jit(solution)/shard_map/ppermute | solution.py:69
  44.6 0.0 collective-permute-done.5.right_ref
  44.6 0.7 shard_map.48
  45.4 0.2 all_to_all.52
  45.6 1.1 copy.8
  46.7 3.5 %all-to-all-start = ((bf16[32,8,1024]{2,0,1:T(8,128)(2,1)}), bf16[32,8,1024]{2,0,1:T(8,128)(2,1)S(1)}, u32[]{:S(2)}, u32[]{:S(2)}) async-start(bf16[32,8,1024]{2,0,1:T(8,128)(2,1)} %copy.8), calls=%async_computation | async-start | bytes 1048576 | tf_op jit(solution)/shard_map/all_to_all | solution.py:247
  50.2 0.0 collective-permute-done.11.right_ref
  50.2 0.5 collective-permute-done.10.left_ref
  50.7 0.7 shard_map.51
  51.4 0.2 all_to_all.56
  51.7 0.3 copy.9
  52.0 19.0 %all-to-all-done = bf16[32,8,1024]{2,0,1:T(8,128)(2,1)S(1)} async-done(((bf16[32,8,1024]{2,0,1:T(8,128)(2,1)}), bf16[32,8,1024]{2,0,1:T(8,128)(2,1)S(1)}, u32[]{:S(2)}, u32[]{:S(2)}) %all-to-all-start) | async-done | bytes 524320 | tf_op jit(solution)/shard_map/all_to_all | solution.py:247
  71.0 14.2 %all_to_all.74 = bf16[32,8,1024]{2,0,1:T(8,128)(2,1)S(1)} all-to-all(bf16[32,8,1024]{2,0,1:T(8,128)(2,1)S(1)} %copy.9), channel_id=1, replica_groups=mesh['y'=4,'x_lo'=2,'x_hi'=2,'z'=16,'core'=2] {'y','x_lo'}, dimensions={1} | all-to-all | bytes 1048576 | tf_op jit(solution)/shard_map/all_to_all | solution.py:247
  85.2 0.9 shard_map.52
  86.1 14.4 %all_to_all.75 = f32[16,80,128]{2,1,0:T(8,128)S(1)} all-to-all(f32[16,80,128]{2,1,0:T(8,128)S(1)} %bitcast.30), channel_id=1, replica_groups=mesh['y'=4,'x_lo'=2,'x_hi'=2,'z'=16,'core'=2] {'core','y','x_lo'}, dimensions={0} | all-to-all | bytes 1310720 | tf_op jit(solution)/shard_map/all_to_all | solution.py:226
  100.5 21.4 %all_to_all.76 = f32[16,5,128]{2,1,0:T(8,128)S(1)} all-to-all(f32[16,5,128]{2,1,0:T(8,128)S(1)} %reshape.38), channel_id=1, replica_groups=mesh['y'=4,'x_lo'=2,'x_hi'=2,'z'=16,'core'=2] {'z'}, dimensions={0} | all-to-all | bytes 81920 | tf_op jit(solution)/shard_map/all_to_all | solution.py:226
  122.0 6.6 %collective-permute-start.12 = (f32[5,128]{1,0:T(8,128)S(1)}, f32[5,128]{1,0:T(8,128)S(1)}, u32[]{:S(2)}, u32[]{:S(2)}) collective-permute-start(f32[5,128]{1,0:T(8,128)S(1)} %reduce_sum.19), channel_id=1, source_target_pairs={{0,32},{32,0},{1,33},{33,1},{2,34},{34,2},{3,35},{35,3},{4,36},{36... | collective-permute-start | bytes 7688 | tf_op jit(solution)/shard_map/ppermute | solution.py:234
  128.6 1.0 collective-permute-done.12
  129.6 14.3 %all_to_all.77 = f32[16,5,128]{2,1,0:T(8,128)S(1)} all-to-all(f32[16,5,128]{2,1,0:T(8,128)S(1)} %broadcast_in_dim.6), channel_id=1, replica_groups=mesh['y'=4,'x_lo'=2,'x_hi'=2,'z'=16,'core'=2] {'z'}, dimensions={0} | all-to-all | bytes 81920 | tf_op jit(solution)/shard_map/all_to_all | solution.py:226
  143.9 9.9 %all_to_all.78 = f32[8,80,128]{2,1,0:T(8,128)S(1)} all-to-all(f32[8,80,128]{2,1,0:T(8,128)S(1)} %broadcast_in_dim.15), channel_id=1, replica_groups=mesh['y'=4,'x_lo'=2,'x_hi'=2,'z'=16,'core'=2] {'y','x_lo'}, dimensions={0} | all-to-all | bytes 655360 | tf_op jit(solution)/shard_map/all_to_all | solution.py:226
  153.9 6.7 %all_gather.3.tiles_ref = f32[1280,128]{1,0:T(8,128)S(1)} all-gather(f32[640,128]{1,0:T(8,128)S(1)} %bitcast.32), channel_id=1, replica_groups=mesh['y'=4,'x_lo'=2,'x_hi'=2,'z'=16,'core'=2] {'core'}, dimensions={0}, use_global_device_ids=true | all-gather | bytes 983040 | tf_op jit(solution)/shard_map/all_gather | solution.py:238
  160.5 19.2 %shard_map.53 = bf16[512,1024]{1,0:T(8,128)(2,1)S(1)} custom-call(f32[1280,128]{1,0:T(8,128)S(1)} %all_gather.3.tiles_ref, bf16[512,1024]{1,0:T(8,128)(2,1)S(1)} %get-tuple-element.8.field_ref), custom_call_target="tpu_custom_call" | custom-call | tf_op jit(solution)/shard_map/pallas_call | solution.py:210
  179.7 17.9 %all_to_all.79 = bf16[8,64,1024]{2,1,0:T(8,128)(2,1)S(1)} all-to-all(bf16[8,64,1024]{2,1,0:T(8,128)(2,1)S(1)} %bitcast.21), channel_id=1, replica_groups=mesh['y'=4,'x_lo'=2,'x_hi'=2,'z'=16,'core'=2] {'y','x_lo'}, dimensions={0} | all-to-all | bytes 2097152 | tf_op jit(solution)/shard_map/all_to_all | solution.py:252
  197.6 0.6 copy.10
  198.2 1.3 reshape.40
  (15 shorter events, 0.1 us)
Async XLA Ops:
  0.0 18.1 %copy-start = (bf16[128,384]{1,0:T(8,128)(2,1)S(1)}, bf16[128,384]{1,0:T(8,128)(2,1)}, u32[]{:S(2)}) copy-start(bf16[128,384]{1,0:T(8,128)(2,1)} %constant.8.clone.across_ref) | copy-start | bytes 294916
  0.0 18.1 %copy-start.2 = (bf16[128,128]{1,0:T(8,128)(2,1)S(1)}, bf16[128,128]{1,0:T(8,128)(2,1)}, u32[]{:S(2)}) copy-start(bf16[128,128]{1,0:T(8,128)(2,1)} %constant.9.clone.along_ref) | copy-start | bytes 98308
  0.0 18.1 %copy-start.1 = (f32[2,32,128]{2,1,0:T(8,128)S(1)}, f32[2,32,128]{2,1,0:T(8,128)}, u32[]{:S(2)}) copy-start(f32[2,32,128]{2,1,0:T(8,128)} %param.5) | copy-start | bytes 98308
  1.3 16.3 %collective-permute-start.1 = (bf16[2048,128]{1,0:T(8,128)(2,1)S(1)}, bf16[2048,128]{1,0:T(8,128)(2,1)S(1)}, u32[]{:S(2)}, u32[]{:S(2)}) collective-permute-start(bf16[2048,128]{1,0:T(8,128)(2,1)S(1)} %bitcast.17), channel_id=1, source_target_pairs={{1,0},{2,1},{3,2},{4,3},{5,4},{6,5},{7,6},{8,7},{9,8},{10,9},{11,1... | collective-permute-start | bytes 1572872 | tf_op jit(solution)/shard_map/ppermute | solution.py:70
  10.1 8.0 %collective-permute-start = (bf16[2048,128]{1,0:T(8,128)(2,1)S(1)}, bf16[2048,128]{1,0:T(8,128)(2,1)S(1)}, u32[]{:S(2)}, u32[]{:S(2)}) collective-permute-start(bf16[2048,128]{1,0:T(8,128)(2,1)S(1)} %bitcast.18), channel_id=1, source_target_pairs={{0,1},{1,2},{2,3},{3,4},{4,5},{5,6},{6,7},{7,8},{8,9},{9,10},{10,1... | collective-permute-start | bytes 1572872 | tf_op jit(solution)/shard_map/ppermute | solution.py:69
  12.0 13.2 %collective-permute-start.7 = (bf16[2048,128]{1,0:T(8,128)(2,1)S(1)}, bf16[2048,128]{1,0:T(8,128)(2,1)S(1)}, u32[]{:S(2)}, u32[]{:S(2)}) collective-permute-start(bf16[2048,128]{1,0:T(8,128)(2,1)S(1)} %bitcast.13), channel_id=1, source_target_pairs={{1,0},{2,1},{3,2},{4,3},{5,4},{6,5},{7,6},{8,7},{9,8},{10,9},{11,1... | collective-permute-start | bytes 1572872 | tf_op jit(solution)/shard_map/ppermute | solution.py:70
  14.5 10.7 %collective-permute-start.6 = (bf16[2048,128]{1,0:T(8,128)(2,1)S(1)}, bf16[2048,128]{1,0:T(8,128)(2,1)S(1)}, u32[]{:S(2)}, u32[]{:S(2)}) collective-permute-start(bf16[2048,128]{1,0:T(8,128)(2,1)S(1)} %bitcast.14), channel_id=1, source_target_pairs={{0,1},{1,2},{2,3},{3,4},{4,5},{5,6},{6,7},{7,8},{8,9},{9,10},{10,1... | collective-permute-start | bytes 1572872 | tf_op jit(solution)/shard_map/ppermute | solution.py:69
  18.9 12.6 %collective-permute-start.3 = (bf16[2048,128]{1,0:T(8,128)(2,1)S(1)}, bf16[2048,128]{1,0:T(8,128)(2,1)S(1)}, u32[]{:S(2)}, u32[]{:S(2)}) collective-permute-start(bf16[2048,128]{1,0:T(8,128)(2,1)S(1)} %shard_map.46.cells_ref.rest_0_), channel_id=1, source_target_pairs={{1,0},{2,1},{3,2},{4,3},{5,4},{6,5},{7,6},{8,7},{9,8},{10,9},{11,1... | collective-permute-start | bytes 1572872 | tf_op jit(solution)/shard_map/ppermute | solution.py:70
  20.8 10.7 %collective-permute-start.2 = (bf16[2048,128]{1,0:T(8,128)(2,1)S(1)}, bf16[2048,128]{1,0:T(8,128)(2,1)S(1)}, u32[]{:S(2)}, u32[]{:S(2)}) collective-permute-start(bf16[2048,128]{1,0:T(8,128)(2,1)S(1)} %shard_map.46.cells_ref.rest_0_), channel_id=1, source_target_pairs={{0,1},{1,2},{2,3},{3,4},{4,5},{5,6},{6,7},{7,8},{8,9},{9,10},{10,1... | collective-permute-start | bytes 1572872 | tf_op jit(solution)/shard_map/ppermute | solution.py:69
  25.9 12.4 %collective-permute-start.9 = (bf16[2048,128]{1,0:T(8,128)(2,1)S(1)}, bf16[2048,128]{1,0:T(8,128)(2,1)S(1)}, u32[]{:S(2)}, u32[]{:S(2)}) collective-permute-start(bf16[2048,128]{1,0:T(8,128)(2,1)S(1)} %shard_map.49.cells_ref.rest_0_), channel_id=1, source_target_pairs={{1,0},{2,1},{3,2},{4,3},{5,4},{6,5},{7,6},{8,7},{9,8},{10,9},{11,1... | collective-permute-start | bytes 1572872 | tf_op jit(solution)/shard_map/ppermute | solution.py:70
  27.8 10.5 %collective-permute-start.8 = (bf16[2048,128]{1,0:T(8,128)(2,1)S(1)}, bf16[2048,128]{1,0:T(8,128)(2,1)S(1)}, u32[]{:S(2)}, u32[]{:S(2)}) collective-permute-start(bf16[2048,128]{1,0:T(8,128)(2,1)S(1)} %shard_map.49.cells_ref.rest_0_), channel_id=1, source_target_pairs={{0,1},{1,2},{2,3},{3,4},{4,5},{5,6},{6,7},{7,8},{8,9},{9,10},{10,1... | collective-permute-start | bytes 1572872 | tf_op jit(solution)/shard_map/ppermute | solution.py:69
  32.2 12.4 %collective-permute-start.5 = (bf16[2048,128]{1,0:T(8,128)(2,1)S(1)}, bf16[2048,128]{1,0:T(8,128)(2,1)S(1)}, u32[]{:S(2)}, u32[]{:S(2)}) collective-permute-start(bf16[2048,128]{1,0:T(8,128)(2,1)S(1)} %shard_map.47.cells_ref), channel_id=1, source_target_pairs={{1,0},{2,1},{3,2},{4,3},{5,4},{6,5},{7,6},{8,7},{9,8},{10,9},{11,1... | collective-permute-start | bytes 1572872 | tf_op jit(solution)/shard_map/ppermute | solution.py:70
  34.1 10.5 %collective-permute-start.4 = (bf16[2048,128]{1,0:T(8,128)(2,1)S(1)}, bf16[2048,128]{1,0:T(8,128)(2,1)S(1)}, u32[]{:S(2)}, u32[]{:S(2)}) collective-permute-start(bf16[2048,128]{1,0:T(8,128)(2,1)S(1)} %shard_map.47.cells_ref), channel_id=1, source_target_pairs={{0,1},{1,2},{2,3},{3,4},{4,5},{5,6},{6,7},{7,8},{8,9},{9,10},{10,1... | collective-permute-start | bytes 1572872 | tf_op jit(solution)/shard_map/ppermute | solution.py:69
  39.0 11.1 %collective-permute-start.11 = (bf16[2048,128]{1,0:T(8,128)(2,1)S(1)}, bf16[2048,128]{1,0:T(8,128)(2,1)S(1)}, u32[]{:S(2)}, u32[]{:S(2)}) collective-permute-start(bf16[2048,128]{1,0:T(8,128)(2,1)S(1)} %shard_map.50.cells_ref), channel_id=1, source_target_pairs={{1,0},{2,1},{3,2},{4,3},{5,4},{6,5},{7,6},{8,7},{9,8},{10,9},{11,1... | collective-permute-start | bytes 1572872 | tf_op jit(solution)/shard_map/ppermute | solution.py:70
  41.0 9.8 %collective-permute-start.10 = (bf16[2048,128]{1,0:T(8,128)(2,1)S(1)}, bf16[2048,128]{1,0:T(8,128)(2,1)S(1)}, u32[]{:S(2)}, u32[]{:S(2)}) collective-permute-start(bf16[2048,128]{1,0:T(8,128)(2,1)S(1)} %shard_map.50.cells_ref), channel_id=1, source_target_pairs={{0,1},{1,2},{2,3},{3,4},{4,5},{5,6},{6,7},{7,8},{8,9},{9,10},{10,1... | collective-permute-start | bytes 1572872 | tf_op jit(solution)/shard_map/ppermute | solution.py:69
  46.7 24.3 %all-to-all-start = ((bf16[32,8,1024]{2,0,1:T(8,128)(2,1)}), bf16[32,8,1024]{2,0,1:T(8,128)(2,1)S(1)}, u32[]{:S(2)}, u32[]{:S(2)}) async-start(bf16[32,8,1024]{2,0,1:T(8,128)(2,1)} %copy.8), calls=%async_computation | async-start | bytes 1048576 | tf_op jit(solution)/shard_map/all_to_all | solution.py:247
  122.0 7.6 %collective-permute-start.12 = (f32[5,128]{1,0:T(8,128)S(1)}, f32[5,128]{1,0:T(8,128)S(1)}, u32[]{:S(2)}, u32[]{:S(2)}) collective-permute-start(f32[5,128]{1,0:T(8,128)S(1)} %reduce_sum.19), channel_id=1, source_target_pairs={{0,32},{32,0},{1,33},{33,1},{2,34},{34,2},{3,35},{35,3},{4,36},{36... | collective-permute-start | bytes 7688 | tf_op jit(solution)/shard_map/ppermute | solution.py:234

commit v8 on v7

--- a/solution.py
+++ b/solution.py
@@ -242,7 +242,11 @@
     cells_dev = orbitals.shape[1] * orbitals.shape[2] * orbitals.shape[3]
     total_cells = cells_dev * lax.axis_size(DOM)
     slabs = orbitals.reshape(PARTS, -1, orbitals.shape[3])
-    filtered = chebyshev([slabs[g] for g in range(PARTS)], potential.reshape(-1, potential.shape[2]))
+    parts = [slabs[0]]
+    for g in range(1, PARTS):
+        slabs, parts[-1] = lax.optimization_barrier((slabs, parts[-1]))
+        parts.append(slabs[g])
+    filtered = chebyshev(parts, potential.reshape(-1, potential.shape[2]))
     shares = [
         lax.all_to_all(part.reshape(-1, cells_dev), BAND, 1, 0, tiled=True) for part in filtered
     ]

time: 200 us -> 201 us (level)
  no operation moved by 1% of the time
where the time goes in v8:
time: 201 us; the launch traced here: 200 us
  blocking collectives  98.7 us (49%)
  starting transfers between devices  50 us (25%)
  Pallas kernels  24.3 us (12%)
  waiting for transfers between devices  21.1 us (10%)
  local copies, waits for them, and re-layouts  5.15 us (3%)
    all_to_all x4, blocking collectives, exchange(): return lax.all_to_all(pieces, axis, 0, 0, tiled=True)  60 us
    ppermute x6, starting transfers between devices, halo(): left = lax.ppermute(cells, DOM, [(i, i + 1) for i in range(count - 1)])  20.9 us
    pallas_call x1, Pallas kernels, rotated_by(): pl.pallas_call(rotation_kernel, out_shape=jax.ShapeDtypeStruct(field.shap...  19.2 us
    ppermute x6, starting transfers between devices, halo(): right = lax.ppermute(cells, DOM, [(i + 1, i) for i in range(count - 1)])  19 us
    all_to_all x1, waiting for transfers between devices, local(): lax.all_to_all(part.reshape(-1, cells_dev), BAND, 1, 0, tiled=True)  19 us
    all_to_all x1, blocking collectives, local(): result = lax.all_to_all(turned, BAND, 0, 1, tiled=True)  17.9 us
    all_to_all x1, blocking collectives, local(): lax.all_to_all(part.reshape(-1, cells_dev), BAND, 1, 0, tiled=True)  14.2 us
    all_gather x1, blocking collectives, summed_everywhere(): return lax.all_gather(part, 'core', axis=0, tiled=True)  6.68 us
  transfers between devices with their start and end apart: 14, of which 4 were waited for; matrix products, arithmetic and copies ran while one was open for 1% of the time, Pallas kernels for 2%

profile of v8, /device:TPU:1, one launch (start us, length us, event | category | flops | bytes accessed | tf_op | source)
XLA Modules:
  0.0 199.7 jit_solution(9689630887480598264)
XLA Ops:
  0.0 1.2 slice.7
  1.2 0.2 copy-done.3
  1.4 8.9 %collective-permute-start.7 = (bf16[2048,128]{1,0:T(8,128)(2,1)S(1)}, bf16[2048,128]{1,0:T(8,128)(2,1)S(1)}, u32[]{:S(2)}, u32[]{:S(2)}) collective-permute-start(bf16[2048,128]{1,0:T(8,128)(2,1)S(1)} %slice_bitcast_fusion.cells_ref.rest_0_), channel_id=1, source_target_pairs={{1,0},{2,1},{3,2},{4,3},{5,4},{6,5},{7,6},{8,7},{9,8},{10,9},{11,1... | collective-permute-start | bytes 1572872 | tf_op jit(solution)/shard_map/ppermute | solution.py:70
  10.4 1.9 collective-permute-start.6
  12.3 2.4 %collective-permute-start.1 = (bf16[2048,128]{1,0:T(8,128)(2,1)S(1)}, bf16[2048,128]{1,0:T(8,128)(2,1)S(1)}, u32[]{:S(2)}, u32[]{:S(2)}) collective-permute-start(bf16[2048,128]{1,0:T(8,128)(2,1)S(1)} %bitcast.15), channel_id=1, source_target_pairs={{1,0},{2,1},{3,2},{4,3},{5,4},{6,5},{7,6},{8,7},{9,8},{10,9},{11,1... | collective-permute-start | bytes 1572872 | tf_op jit(solution)/shard_map/ppermute | solution.py:70
  14.7 3.1 %collective-permute-start = (bf16[2048,128]{1,0:T(8,128)(2,1)S(1)}, bf16[2048,128]{1,0:T(8,128)(2,1)S(1)}, u32[]{:S(2)}, u32[]{:S(2)}) collective-permute-start(bf16[2048,128]{1,0:T(8,128)(2,1)S(1)} %bitcast.16), channel_id=1, source_target_pairs={{0,1},{1,2},{2,3},{3,4},{4,5},{5,6},{6,7},{7,8},{8,9},{9,10},{10,1... | collective-permute-start | bytes 1572872 | tf_op jit(solution)/shard_map/ppermute | solution.py:69
  17.9 0.0 collective-permute-done.7.right_ref
  17.9 0.5 collective-permute-done.6.left_ref
  18.4 0.7 shard_map.49.cells_ref.rest_0_
  19.1 1.9 collective-permute-start.9
  21.0 4.4 %collective-permute-start.8 = (bf16[2048,128]{1,0:T(8,128)(2,1)S(1)}, bf16[2048,128]{1,0:T(8,128)(2,1)S(1)}, u32[]{:S(2)}, u32[]{:S(2)}) collective-permute-start(bf16[2048,128]{1,0:T(8,128)(2,1)S(1)} %shard_map.49.cells_ref.rest_0_), channel_id=1, source_target_pairs={{0,1},{1,2},{2,3},{3,4},{4,5},{5,6},{6,7},{7,8},{8,9},{9,10},{10,1... | collective-permute-start | bytes 1572872 | tf_op jit(solution)/shard_map/ppermute | solution.py:69
  25.4 0.0 collective-permute-done.1.right_ref
  25.4 0.0 collective-permute-done.left_ref
  25.4 0.7 shard_map.46.cells_ref.rest_0_
  26.2 1.9 collective-permute-start.3
  28.1 3.6 %collective-permute-start.2 = (bf16[2048,128]{1,0:T(8,128)(2,1)S(1)}, bf16[2048,128]{1,0:T(8,128)(2,1)S(1)}, u32[]{:S(2)}, u32[]{:S(2)}) collective-permute-start(bf16[2048,128]{1,0:T(8,128)(2,1)S(1)} %shard_map.46.cells_ref.rest_0_), channel_id=1, source_target_pairs={{0,1},{1,2},{2,3},{3,4},{4,5},{5,6},{6,7},{7,8},{8,9},{9,10},{10,1... | collective-permute-start | bytes 1572872 | tf_op jit(solution)/shard_map/ppermute | solution.py:69
  31.7 0.0 collective-permute-done.8.left_ref
  31.8 0.7 shard_map.50.cells_ref
  32.5 1.9 collective-permute-start.11
  34.4 4.2 %collective-permute-start.10 = (bf16[2048,128]{1,0:T(8,128)(2,1)S(1)}, bf16[2048,128]{1,0:T(8,128)(2,1)S(1)}, u32[]{:S(2)}, u32[]{:S(2)}) collective-permute-start(bf16[2048,128]{1,0:T(8,128)(2,1)S(1)} %shard_map.50.cells_ref), channel_id=1, source_target_pairs={{0,1},{1,2},{2,3},{3,4},{4,5},{5,6},{6,7},{7,8},{8,9},{9,10},{10,1... | collective-permute-start | bytes 1572872 | tf_op jit(solution)/shard_map/ppermute | solution.py:69
  38.6 0.0 collective-permute-done.3.right_ref
  38.6 0.0 collective-permute-done.2.left_ref
  38.6 0.7 shard_map.47.cells_ref
  39.3 1.9 collective-permute-start.5
  41.2 3.6 %collective-permute-start.4 = (bf16[2048,128]{1,0:T(8,128)(2,1)S(1)}, bf16[2048,128]{1,0:T(8,128)(2,1)S(1)}, u32[]{:S(2)}, u32[]{:S(2)}) collective-permute-start(bf16[2048,128]{1,0:T(8,128)(2,1)S(1)} %shard_map.47.cells_ref), channel_id=1, source_target_pairs={{0,1},{1,2},{2,3},{3,4},{4,5},{5,6},{6,7},{7,8},{8,9},{9,10},{10,1... | collective-permute-start | bytes 1572872 | tf_op jit(solution)/shard_map/ppermute | solution.py:69
  44.9 0.0 collective-permute-done.11.right_ref
  44.9 0.7 shard_map.51
  45.6 0.2 all_to_all.56
  45.8 1.1 copy.9
  46.9 3.5 %all-to-all-start.1 = ((bf16[32,8,1024]{2,0,1:T(8,128)(2,1)}), bf16[32,8,1024]{2,0,1:T(8,128)(2,1)S(1)}, u32[]{:S(2)}, u32[]{:S(2)}) async-start(bf16[32,8,1024]{2,0,1:T(8,128)(2,1)} %copy.9), calls=%async_computation.1 | async-start | bytes 1048576 | tf_op jit(solution)/shard_map/all_to_all | solution.py:251
  50.4 0.5 collective-permute-done.4.left_ref
  51.0 0.7 shard_map.48
  51.7 0.2 all_to_all.52
  51.9 0.3 copy.8
  52.2 19.0 %all-to-all-done.1 = bf16[32,8,1024]{2,0,1:T(8,128)(2,1)S(1)} async-done(((bf16[32,8,1024]{2,0,1:T(8,128)(2,1)}), bf16[32,8,1024]{2,0,1:T(8,128)(2,1)S(1)}, u32[]{:S(2)}, u32[]{:S(2)}) %all-to-all-start.1) | async-done | bytes 524320 | tf_op jit(solution)/shard_map/all_to_all | solution.py:251
  71.2 14.2 %all_to_all.74 = bf16[32,8,1024]{2,0,1:T(8,128)(2,1)S(1)} all-to-all(bf16[32,8,1024]{2,0,1:T(8,128)(2,1)S(1)} %copy.8), channel_id=1, replica_groups=mesh['y'=4,'x_lo'=2,'x_hi'=2,'z'=16,'core'=2] {'y','x_lo'}, dimensions={1} | all-to-all | bytes 1048576 | tf_op jit(solution)/shard_map/all_to_all | solution.py:251
  85.5 0.9 shard_map.52
  86.4 14.3 %all_to_all.75 = f32[16,80,128]{2,1,0:T(8,128)S(1)} all-to-all(f32[16,80,128]{2,1,0:T(8,128)S(1)} %bitcast.28), channel_id=1, replica_groups=mesh['y'=4,'x_lo'=2,'x_hi'=2,'z'=16,'core'=2] {'core','y','x_lo'}, dimensions={0} | all-to-all | bytes 1310720 | tf_op jit(solution)/shard_map/all_to_all | solution.py:226
  100.8 21.4 %all_to_all.76 = f32[16,5,128]{2,1,0:T(8,128)S(1)} all-to-all(f32[16,5,128]{2,1,0:T(8,128)S(1)} %reshape.39), channel_id=1, replica_groups=mesh['y'=4,'x_lo'=2,'x_hi'=2,'z'=16,'core'=2] {'z'}, dimensions={0} | all-to-all | bytes 81920 | tf_op jit(solution)/shard_map/all_to_all | solution.py:226
  122.2 6.6 %collective-permute-start.12 = (f32[5,128]{1,0:T(8,128)S(1)}, f32[5,128]{1,0:T(8,128)S(1)}, u32[]{:S(2)}, u32[]{:S(2)}) collective-permute-start(f32[5,128]{1,0:T(8,128)S(1)} %reduce_sum.19), channel_id=1, source_target_pairs={{0,32},{32,0},{1,33},{33,1},{2,34},{34,2},{3,35},{35,3},{4,36},{36... | collective-permute-start | bytes 7688 | tf_op jit(solution)/shard_map/ppermute | solution.py:234
  128.8 1.0 collective-permute-done.12
  129.8 14.3 %all_to_all.77 = f32[16,5,128]{2,1,0:T(8,128)S(1)} all-to-all(f32[16,5,128]{2,1,0:T(8,128)S(1)} %broadcast_in_dim.6), channel_id=1, replica_groups=mesh['y'=4,'x_lo'=2,'x_hi'=2,'z'=16,'core'=2] {'z'}, dimensions={0} | all-to-all | bytes 81920 | tf_op jit(solution)/shard_map/all_to_all | solution.py:226
  144.2 9.9 %all_to_all.78 = f32[8,80,128]{2,1,0:T(8,128)S(1)} all-to-all(f32[8,80,128]{2,1,0:T(8,128)S(1)} %broadcast_in_dim.15), channel_id=1, replica_groups=mesh['y'=4,'x_lo'=2,'x_hi'=2,'z'=16,'core'=2] {'y','x_lo'}, dimensions={0} | all-to-all | bytes 655360 | tf_op jit(solution)/shard_map/all_to_all | solution.py:226
  154.1 6.7 %all_gather.3.tiles_ref = f32[1280,128]{1,0:T(8,128)S(1)} all-gather(f32[640,128]{1,0:T(8,128)S(1)} %bitcast.30), channel_id=1, replica_groups=mesh['y'=4,'x_lo'=2,'x_hi'=2,'z'=16,'core'=2] {'core'}, dimensions={0}, use_global_device_ids=true | all-gather | bytes 983040 | tf_op jit(solution)/shard_map/all_gather | solution.py:238
  160.8 19.2 %shard_map.53 = bf16[512,1024]{1,0:T(8,128)(2,1)S(1)} custom-call(f32[1280,128]{1,0:T(8,128)S(1)} %all_gather.3.tiles_ref, bf16[512,1024]{1,0:T(8,128)(2,1)S(1)} %get-tuple-element.12.field_ref), custom_call_target="tpu_custom_call" | custom-call | tf_op jit(solution)/shard_map/pallas_call | solution.py:210
  180.0 17.9 %all_to_all.79 = bf16[8,64,1024]{2,1,0:T(8,128)(2,1)S(1)} all-to-all(bf16[8,64,1024]{2,1,0:T(8,128)(2,1)S(1)} %bitcast.19), channel_id=1, replica_groups=mesh['y'=4,'x_lo'=2,'x_hi'=2,'z'=16,'core'=2] {'y','x_lo'}, dimensions={0} | all-to-all | bytes 2097152 | tf_op jit(solution)/shard_map/all_to_all | solution.py:256
  197.9 0.6 copy.10
  198.4 1.3 reshape.41
  (18 shorter events, 0.2 us)
Async XLA Ops:
  0.0 1.4 copy-start.3
  1.4 17.0 %copy-start = (bf16[128,384]{1,0:T(8,128)(2,1)S(1)}, bf16[128,384]{1,0:T(8,128)(2,1)}, u32[]{:S(2)}) copy-start(bf16[128,384]{1,0:T(8,128)(2,1)} %constant.8.clone.across_ref) | copy-start | bytes 294916
  1.4 17.0 %copy-start.1 = (f32[2,32,128]{2,1,0:T(8,128)S(1)}, f32[2,32,128]{2,1,0:T(8,128)}, u32[]{:S(2)}) copy-start(f32[2,32,128]{2,1,0:T(8,128)} %param.5) | copy-start | bytes 98308
  1.4 17.0 %copy-start.2 = (bf16[128,128]{1,0:T(8,128)(2,1)S(1)}, bf16[128,128]{1,0:T(8,128)(2,1)}, u32[]{:S(2)}) copy-start(bf16[128,128]{1,0:T(8,128)(2,1)} %constant.9.clone.along_ref) | copy-start | bytes 98308
  1.4 16.4 %collective-permute-start.7 = (bf16[2048,128]{1,0:T(8,128)(2,1)S(1)}, bf16[2048,128]{1,0:T(8,128)(2,1)S(1)}, u32[]{:S(2)}, u32[]{:S(2)}) collective-permute-start(bf16[2048,128]{1,0:T(8,128)(2,1)S(1)} %slice_bitcast_fusion.cells_ref.rest_0_), channel_id=1, source_target_pairs={{1,0},{2,1},{3,2},{4,3},{5,4},{6,5},{7,6},{8,7},{9,8},{10,9},{11,1... | collective-permute-start | bytes 1572872 | tf_op jit(solution)/shard_map/ppermute | solution.py:70
  10.4 8.0 %collective-permute-start.6 = (bf16[2048,128]{1,0:T(8,128)(2,1)S(1)}, bf16[2048,128]{1,0:T(8,128)(2,1)S(1)}, u32[]{:S(2)}, u32[]{:S(2)}) collective-permute-start(bf16[2048,128]{1,0:T(8,128)(2,1)S(1)} %slice_bitcast_fusion.cells_ref.rest_0_), channel_id=1, source_target_pairs={{0,1},{1,2},{2,3},{3,4},{4,5},{5,6},{6,7},{7,8},{8,9},{9,10},{10,1... | collective-permute-start | bytes 1572872 | tf_op jit(solution)/shard_map/ppermute | solution.py:69
  12.3 13.1 %collective-permute-start.1 = (bf16[2048,128]{1,0:T(8,128)(2,1)S(1)}, bf16[2048,128]{1,0:T(8,128)(2,1)S(1)}, u32[]{:S(2)}, u32[]{:S(2)}) collective-permute-start(bf16[2048,128]{1,0:T(8,128)(2,1)S(1)} %bitcast.15), channel_id=1, source_target_pairs={{1,0},{2,1},{3,2},{4,3},{5,4},{6,5},{7,6},{8,7},{9,8},{10,9},{11,1... | collective-permute-start | bytes 1572872 | tf_op jit(solution)/shard_map/ppermute | solution.py:70
  14.7 10.7 %collective-permute-start = (bf16[2048,128]{1,0:T(8,128)(2,1)S(1)}, bf16[2048,128]{1,0:T(8,128)(2,1)S(1)}, u32[]{:S(2)}, u32[]{:S(2)}) collective-permute-start(bf16[2048,128]{1,0:T(8,128)(2,1)S(1)} %bitcast.16), channel_id=1, source_target_pairs={{0,1},{1,2},{2,3},{3,4},{4,5},{5,6},{6,7},{7,8},{8,9},{9,10},{10,1... | collective-permute-start | bytes 1572872 | tf_op jit(solution)/shard_map/ppermute | solution.py:69
  19.1 12.6 %collective-permute-start.9 = (bf16[2048,128]{1,0:T(8,128)(2,1)S(1)}, bf16[2048,128]{1,0:T(8,128)(2,1)S(1)}, u32[]{:S(2)}, u32[]{:S(2)}) collective-permute-start(bf16[2048,128]{1,0:T(8,128)(2,1)S(1)} %shard_map.49.cells_ref.rest_0_), channel_id=1, source_target_pairs={{1,0},{2,1},{3,2},{4,3},{5,4},{6,5},{7,6},{8,7},{9,8},{10,9},{11,1... | collective-permute-start | bytes 1572872 | tf_op jit(solution)/shard_map/ppermute | solution.py:70
  21.0 10.7 %collective-permute-start.8 = (bf16[2048,128]{1,0:T(8,128)(2,1)S(1)}, bf16[2048,128]{1,0:T(8,128)(2,1)S(1)}, u32[]{:S(2)}, u32[]{:S(2)}) collective-permute-start(bf16[2048,128]{1,0:T(8,128)(2,1)S(1)} %shard_map.49.cells_ref.rest_0_), channel_id=1, source_target_pairs={{0,1},{1,2},{2,3},{3,4},{4,5},{5,6},{6,7},{7,8},{8,9},{9,10},{10,1... | collective-permute-start | bytes 1572872 | tf_op jit(solution)/shard_map/ppermute | solution.py:69
  26.2 12.4 %collective-permute-start.3 = (bf16[2048,128]{1,0:T(8,128)(2,1)S(1)}, bf16[2048,128]{1,0:T(8,128)(2,1)S(1)}, u32[]{:S(2)}, u32[]{:S(2)}) collective-permute-start(bf16[2048,128]{1,0:T(8,128)(2,1)S(1)} %shard_map.46.cells_ref.rest_0_), channel_id=1, source_target_pairs={{1,0},{2,1},{3,2},{4,3},{5,4},{6,5},{7,6},{8,7},{9,8},{10,9},{11,1... | collective-permute-start | bytes 1572872 | tf_op jit(solution)/shard_map/ppermute | solution.py:70
  28.1 10.5 %collective-permute-start.2 = (bf16[2048,128]{1,0:T(8,128)(2,1)S(1)}, bf16[2048,128]{1,0:T(8,128)(2,1)S(1)}, u32[]{:S(2)}, u32[]{:S(2)}) collective-permute-start(bf16[2048,128]{1,0:T(8,128)(2,1)S(1)} %shard_map.46.cells_ref.rest_0_), channel_id=1, source_target_pairs={{0,1},{1,2},{2,3},{3,4},{4,5},{5,6},{6,7},{7,8},{8,9},{9,10},{10,1... | collective-permute-start | bytes 1572872 | tf_op jit(solution)/shard_map/ppermute | solution.py:69
  32.5 12.4 %collective-permute-start.11 = (bf16[2048,128]{1,0:T(8,128)(2,1)S(1)}, bf16[2048,128]{1,0:T(8,128)(2,1)S(1)}, u32[]{:S(2)}, u32[]{:S(2)}) collective-permute-start(bf16[2048,128]{1,0:T(8,128)(2,1)S(1)} %shard_map.50.cells_ref), channel_id=1, source_target_pairs={{1,0},{2,1},{3,2},{4,3},{5,4},{6,5},{7,6},{8,7},{9,8},{10,9},{11,1... | collective-permute-start | bytes 1572872 | tf_op jit(solution)/shard_map/ppermute | solution.py:70
  34.4 10.5 %collective-permute-start.10 = (bf16[2048,128]{1,0:T(8,128)(2,1)S(1)}, bf16[2048,128]{1,0:T(8,128)(2,1)S(1)}, u32[]{:S(2)}, u32[]{:S(2)}) collective-permute-start(bf16[2048,128]{1,0:T(8,128)(2,1)S(1)} %shard_map.50.cells_ref), channel_id=1, source_target_pairs={{0,1},{1,2},{2,3},{3,4},{4,5},{5,6},{6,7},{7,8},{8,9},{9,10},{10,1... | collective-permute-start | bytes 1572872 | tf_op jit(solution)/shard_map/ppermute | solution.py:69
  39.3 11.1 %collective-permute-start.5 = (bf16[2048,128]{1,0:T(8,128)(2,1)S(1)}, bf16[2048,128]{1,0:T(8,128)(2,1)S(1)}, u32[]{:S(2)}, u32[]{:S(2)}) collective-permute-start(bf16[2048,128]{1,0:T(8,128)(2,1)S(1)} %shard_map.47.cells_ref), channel_id=1, source_target_pairs={{1,0},{2,1},{3,2},{4,3},{5,4},{6,5},{7,6},{8,7},{9,8},{10,9},{11,1... | collective-permute-start | bytes 1572872 | tf_op jit(solution)/shard_map/ppermute | solution.py:70
  41.2 9.8 %collective-permute-start.4 = (bf16[2048,128]{1,0:T(8,128)(2,1)S(1)}, bf16[2048,128]{1,0:T(8,128)(2,1)S(1)}, u32[]{:S(2)}, u32[]{:S(2)}) collective-permute-start(bf16[2048,128]{1,0:T(8,128)(2,1)S(1)} %shard_map.47.cells_ref), channel_id=1, source_target_pairs={{0,1},{1,2},{2,3},{3,4},{4,5},{5,6},{6,7},{7,8},{8,9},{9,10},{10,1... | collective-permute-start | bytes 1572872 | tf_op jit(solution)/shard_map/ppermute | solution.py:69
  46.9 24.3 %all-to-all-start.1 = ((bf16[32,8,1024]{2,0,1:T(8,128)(2,1)}), bf16[32,8,1024]{2,0,1:T(8,128)(2,1)S(1)}, u32[]{:S(2)}, u32[]{:S(2)}) async-start(bf16[32,8,1024]{2,0,1:T(8,128)(2,1)} %copy.9), calls=%async_computation.1 | async-start | bytes 1048576 | tf_op jit(solution)/shard_map/all_to_all | solution.py:251
  122.2 7.6 %collective-permute-start.12 = (f32[5,128]{1,0:T(8,128)S(1)}, f32[5,128]{1,0:T(8,128)S(1)}, u32[]{:S(2)}, u32[]{:S(2)}) collective-permute-start(f32[5,128]{1,0:T(8,128)S(1)} %reduce_sum.19), channel_id=1, source_target_pairs={{0,32},{32,0},{1,33},{33,1},{2,34},{34,2},{3,35},{35,3},{4,36},{36... | collective-permute-start | bytes 7688 | tf_op jit(solution)/shard_map/ppermute | solution.py:234
